TPU v7x, 128 devices: a whole 4x4x4 slice. The times are simulated.
128 devices in a mesh: blk: 16 (over x, y_lo, core), head: 8 (over y_hi, z).
Axes of the slice: x: 4, y: 4 (y_hi: 2, y_lo: 2; y = y_hi * 2 + y_lo), z: 4, core: 2. Of those that a mesh axis runs over, the one named last changes fastest.
Arguments:
- queries: bfloat16 [16384, 8192], P(('blk', 'head')), may hold values from -6 to 6
- keys: bfloat16 [16384, 1024], P(('blk', 'head')), may hold values from -6 to 6
- values: bfloat16 [16384, 1024], P(('blk', 'head')), may hold values from -6 to 6
- live_keys: int32 [16, 16, 16], replicated, may hold values from 0 to 63, as said below
- live_count: int32 [16, 16], replicated, may hold values from 1 to 16, as said below
Outputs:
- attended: bfloat16 [16384, 8192], P(('blk', 'head'))
Inputs may be any that keep to these rules, and one draw needn't show every extreme that they name: live_keys[i, j, c] = a * 8 + b names the pair (query block i * 8 + a, key block j * 8 + b); the codes of one (i, j) are distinct, and a == b never occurs for i == j. Only slots c < live_count[i, j] are live. `live_count`: for every query shard i, some key shard j has all 16 slots live.
All inputs are finite; a program needn't handle non-finite values.
Results may differ from a plain program's by a relative error of at most 0.0065.
Values may be sent and summed in bfloat16 or wider, within the bound.
No kernel may reach another device: no remote copies, remote signals or barrier semaphores. Data moves between devices by JAX's collectives and lax.ppermute only.
A program may use at most 128 MiB of HBM per device.

v0:
```python
import functools

import jax
import jax.numpy as jnp
from jax import lax
from jax.experimental import pallas as pl
from jax.experimental.pallas import tpu as pltpu
from jax.sharding import Mesh
from jax.sharding import PartitionSpec as P

HEADS = 64
KV_HEADS = 8
HEAD_DIM = 128
BLOCK = 128
LOG2E = 1.4426950408889634
CHUNK = 4
GROUP_HEADS = 2
PIECE = 512


def plan_kernel(place_ref, codes_ref, counts_ref, key_ref, value_ref, chunks_ref, fill_ref, *, blocks, sizes, zero):
    x_size, y_size, core_size = sizes
    x, y, core = place_ref[0], place_ref[1], place_ref[2]
    shard = (x * y_size + y) * core_size + core
    for a in range(blocks):
        key_ref[a, 0] = a
        value_ref[a, 0] = a
        fill_ref[a] = 1

    def visit_shard(slot, _):
        from_x = lax.rem(x + lax.rem(slot, x_size), x_size)
        from_y = lax.rem(y + lax.rem(lax.div(slot, x_size), y_size), y_size)
        from_core = lax.rem(core + lax.div(slot, x_size * y_size), core_size)
        j = (from_x * y_size + from_y) * core_size + from_core

        def visit_entry(c, _):
            code = codes_ref[shard, j, c]
            a = lax.div(code, blocks)
            block = slot * blocks + lax.rem(code, blocks)
            at = fill_ref[a]
            key_ref[a, at] = block
            value_ref[a, at] = block
            fill_ref[a] = at + 1
            return 0

        return lax.fori_loop(0, counts_ref[shard, j], visit_entry, 0)

    lax.fori_loop(0, x_size * y_size * core_size, visit_shard, 0)
    for a in range(blocks):
        filled = fill_ref[a]
        chunks = lax.div(filled + CHUNK - 1, CHUNK)
        chunks_ref[a] = chunks

        def pad(at, _):
            key_ref[a, at] = a
            value_ref[a, at] = zero
            return 0

        lax.fori_loop(filled, chunks * CHUNK, pad, 0)


def plan(place, live_keys, live_count, blocks, sizes, zero):
    shards = live_keys.shape[0]
    width = -(-(shards * blocks + 1) // CHUNK) * CHUNK
    smem = pl.BlockSpec(memory_space=pltpu.SMEM)
    return pl.pallas_call(
        functools.partial(plan_kernel, blocks=blocks, sizes=sizes, zero=zero),
        in_specs=[smem] * 3,
        out_specs=[smem] * 3,
        out_shape=[
            jax.ShapeDtypeStruct((blocks, width), jnp.int32),
            jax.ShapeDtypeStruct((blocks, width), jnp.int32),
            jax.ShapeDtypeStruct((blocks,), jnp.int32),
        ],
        scratch_shapes=[pltpu.SMEM((blocks,), jnp.int32)],
        cost_estimate=pl.CostEstimate(flops=0, bytes_accessed=20_000_000, transcendentals=0),
    )(place, live_keys, live_count)


def attend_kernel(key_at, value_at, chunks, queries, *refs, heads, shards):
    pieces, (out, pairs, ones, total, peak, scaled, *rest) = refs[:shards], refs[shards:]
    groups = heads // GROUP_HEADS
    raw, soft, (level, fade, late_fade, ready, sem) = rest[:groups], rest[groups : groups + 2], rest[groups + 2 :]
    b = pl.program_id(0)
    count = pairs.shape[0] - 1
    span = count // shards
    width = GROUP_HEADS * BLOCK
    scale = HEAD_DIM**-0.5 * LOG2E

    def arrival(j):
        return pltpu.make_async_copy(pieces[j], pairs.at[pl.ds(j * span, span)], sem.at[j])

    @pl.when(b == 0)
    def _():
        for j in range(shards):
            arrival(j).start()
        ready[0] = 0
        ones[0] = jnp.ones(ones.shape[1:], jnp.bfloat16)
        ones[1] = jnp.zeros(ones.shape[1:], jnp.bfloat16)
        pairs[count] = jnp.zeros(pairs.shape[1:], jnp.bfloat16)

    def arrive(i):
        @pl.when(b == 0)
        def _():
            last = lax.div(key_at[b, i * CHUNK + CHUNK - 1], span) + 1
            needed = jnp.where(i >= chunks[b] - 1, shards, last)
            for j in range(shards):

                @pl.when((j >= ready[0]) & (j < needed))
                def _():
                    arrival(j).wait()

            ready[0] = jnp.maximum(ready[0], needed)

    def keys_of(i):
        return jnp.concatenate(
            [pairs[key_at[b, i * CHUNK + c], :, :HEAD_DIM] for c in range(CHUNK)], axis=0
        )

    def values_of(i):
        slots = [value_at[b, i * CHUNK + c] for c in range(CHUNK)]
        return jnp.concatenate(
            [
                jnp.concatenate([pairs[s, :, HEAD_DIM:] for s in slots], axis=1),
                jnp.concatenate([ones[(s == count).astype(jnp.int32)] for s in slots], axis=1),
            ],
            axis=0,
        )

    cuts = [slice(j * PIECE, (j + 1) * PIECE) for j in range(CHUNK * BLOCK // PIECE)]

    def columns(g):
        return slice(g * width, (g + 1) * width)

    def score(keys, g):
        return lax.dot_general(
            jnp.concatenate([keys, keys], axis=1),
            scaled[columns(g), :],
            (((1,), (1,)), ((), ())),
            preferred_element_type=jnp.float32,
        )

    def partial_max(piece):
        return jnp.max(piece.reshape(-1, 8, width), axis=0)

    for h in range(heads):
        at = slice(h * BLOCK, (h + 1) * BLOCK)
        exact = queries[:, h * HEAD_DIM : (h + 1) * HEAD_DIM].astype(jnp.float32) * scale
        high = exact.astype(jnp.bfloat16)
        scaled[at, :HEAD_DIM] = high
        scaled[at, HEAD_DIM:] = (exact - high.astype(jnp.float32)).astype(jnp.bfloat16)
    total[...] = jnp.zeros(total.shape, jnp.float32)
    peak[...] = jnp.full(peak.shape, -jnp.inf, jnp.float32)
    soft[1][...] = jnp.zeros(soft[1].shape, jnp.bfloat16)
    late_fade[...] = jnp.ones(late_fade.shape, jnp.float32)
    arrive(0)
    keys = keys_of(0)
    for g in range(2):
        raw[g][...] = score(keys, g)
    level[...] = jnp.max(partial_max(raw[0][...]), axis=0, keepdims=True)
    peak[:, columns(0)] = level[...]
    fade[...] = jnp.zeros(fade.shape, jnp.float32)
    end = chunks[b]

    def visit(i, _):
        following = jnp.minimum(i + 1, end - 1)
        arrive(following)
        keys = keys_of(i)
        next_keys = keys_of(following)
        values = values_of(i)
        before = values_of(jnp.maximum(i - 1, 0))
        new, factor, late = level[...], fade[...], late_fade[...]
        for g in range(groups):
            ahead, upcoming, done = (g + 2) % groups, (g + 1) % groups, (g - 1) % groups
            source = keys if g + 2 < groups else next_keys
            multiplier = values if g else before
            into = columns(done)
            total[:, into] = total[:, into] * late
            tops = None
            for cut in cuts:
                raw[ahead][cut, :] = score(source[cut, :], ahead)
                soft[g % 2][cut, :] = jnp.exp2(raw[g][cut, :] - new).astype(jnp.bfloat16)
                total[:, into] += jnp.dot(
                    multiplier[:, cut], soft[(g + 1) % 2][cut, :], preferred_element_type=jnp.float32
                )
                most = partial_max(raw[upcoming][cut, :])
                tops = most if tops is None else jnp.maximum(tops, most)
            at = columns(upcoming)
            old = peak[:, at]
            new = jnp.maximum(old, jnp.max(tops, axis=0, keepdims=True))
            peak[:, at] = new
            factor, late = jnp.exp2(old - new), factor
        level[...] = new
        fade[...] = factor
        late_fade[...] = late
        return 0

    lax.fori_loop(0, end, visit, 0)
    at = columns(groups - 1)
    total[:, at] = total[:, at] * late_fade[...] + jnp.dot(
        values_of(end - 1), soft[1][...], preferred_element_type=jnp.float32
    )
    square = (BLOCK, BLOCK)
    unit = (
        lax.broadcasted_iota(jnp.int32, square, 0) == lax.broadcasted_iota(jnp.int32, square, 1)
    ).astype(jnp.bfloat16)
    for h in range(heads):
        at = slice(h * BLOCK, (h + 1) * BLOCK)
        normed = (total[:HEAD_DIM, at] / total[HEAD_DIM : HEAD_DIM + 1, at]).astype(jnp.bfloat16)
        turned = lax.dot_general(
            unit, normed, (((1,), (1,)), ((), ())), preferred_element_type=jnp.float32
        )
        out[:, h * HEAD_DIM : (h + 1) * HEAD_DIM] = turned.astype(jnp.bfloat16)


def attend(queries, pieces, lists):
    rows, width = queries.shape
    heads = width // HEAD_DIM
    shards = len(pieces)
    span = pieces[0].shape[0] // BLOCK
    count = shards * span
    pieces = [piece.reshape(span, BLOCK, -1) for piece in pieces]
    pair_estimate = 180 * 2 * 2 * heads * BLOCK * BLOCK * HEAD_DIM
    return pl.pallas_call(
        functools.partial(attend_kernel, heads=heads, shards=shards),
        grid_spec=pltpu.PrefetchScalarGridSpec(
            num_scalar_prefetch=3,
            grid=(rows // BLOCK,),
            in_specs=[pl.BlockSpec((BLOCK, width), lambda b, *_: (b, 0))]
            + [pl.BlockSpec(memory_space=pl.ANY)] * shards,
            out_specs=pl.BlockSpec((BLOCK, width), lambda b, *_: (b, 0)),
            scratch_shapes=[
                pltpu.VMEM((count + 1, BLOCK, 2 * HEAD_DIM), jnp.bfloat16),
                pltpu.VMEM((2, 16, BLOCK), jnp.bfloat16),
                pltpu.VMEM((HEAD_DIM + 16, heads * BLOCK), jnp.float32),
                pltpu.VMEM((1, heads * BLOCK), jnp.float32),
                pltpu.VMEM((heads * BLOCK, 2 * HEAD_DIM), jnp.bfloat16),
            ]
            + [pltpu.VMEM((CHUNK * BLOCK, GROUP_HEADS * BLOCK), jnp.float32)] * (heads // GROUP_HEADS)
            + [pltpu.VMEM((CHUNK * BLOCK, GROUP_HEADS * BLOCK), jnp.bfloat16)] * 2
            + [pltpu.VMEM((1, GROUP_HEADS * BLOCK), jnp.float32)] * 3
            + [
                pltpu.SMEM((1,), jnp.int32),
                pltpu.SemaphoreType.DMA((shards,)),
            ],
        ),
        out_shape=jax.ShapeDtypeStruct((rows, width), jnp.bfloat16),
        compiler_params=pltpu.CompilerParams(vmem_limit_bytes=48 * 1024 * 1024),
        cost_estimate=pl.CostEstimate(flops=pair_estimate * 3, bytes_accessed=12_000_000, transcendentals=0),
    )(*lists, queries, *pieces)


def shift(array, axis, step):
    size = lax.axis_size(axis)
    return lax.ppermute(array, axis, [(i, (i + step) % size) for i in range(size)])


def gather_shards(own, meanwhile):
    here = [own, shift(own, "x", -1), None, shift(own, "x", 1)]
    across = shift(own, "y_lo", 1)
    here[3], across, result = lax.optimization_barrier((here[3], across, meanwhile()))
    here[2] = shift(here[3], "x", 1)
    there = [across, shift(across, "x", -1), None, shift(across, "x", 1)]
    there[2] = shift(there[1], "x", -1)
    near = here + there
    return near + [shift(piece, "core", 1) for piece in near], result


def local(queries, keys, values, live_keys, live_count):
    head_axes, blk_axes = ("y_hi", "z"), ("x", "y_lo", "core")
    parts = lax.axis_size(head_axes)
    tokens = queries.shape[0]
    sizes = tuple(lax.axis_size(axis) for axis in blk_axes)
    blocks = parts * tokens // BLOCK

    def exchange(cut):
        moved = lax.all_to_all(cut, head_axes, split_axis=0, concat_axis=0, tiled=True)
        return moved.reshape(parts * tokens, -1)

    def cut(array):
        return array.reshape(tokens, parts, -1)

    own = exchange(
        jnp.concatenate([cut(keys).transpose(1, 0, 2), cut(values).transpose(1, 2, 0)], axis=2)
    )
    place = jnp.stack([lax.axis_index(axis) for axis in blk_axes]).astype(jnp.int32)
    own, place = lax.optimization_barrier((own, place))
    zero = live_keys.shape[0] * blocks
    pieces, lists = gather_shards(own, lambda: plan(place, live_keys, live_count, blocks, sizes, zero))
    query_local = exchange(cut(queries).transpose(1, 0, 2))
    attended = attend(query_local, pieces, lists)
    back = lax.all_to_all(
        attended.reshape(parts, tokens, -1), head_axes, split_axis=0, concat_axis=0, tiled=True
    )
    return back.transpose(1, 0, 2).reshape(tokens, -1)


def solution(mesh):
    fine = Mesh(mesh.devices.reshape(4, 2, 2, 2, 4), ("x", "y_lo", "core", "y_hi", "z"))
    rows = P(("x", "y_lo", "core", "y_hi", "z"), None)
    return jax.shard_map(
        local,
        mesh=fine,
        in_specs=(rows, rows, rows, P(), P()),
        out_specs=rows,
        check_vma=False,
    )
```

profile of v0, /device:TPU:8, one launch (start us, length us, event | category | flops | bytes accessed | tf_op | source)
XLA Modules:
  0.0 158.2 jit_solution(4907481072293185112)
XLA Ops:
  0.0 1.1 copy.19
  1.3 1.1 copy.18
  2.4 0.8 pad_maximum_fusion
  3.3 7.0 %all-to-all-start = ((bf16[8,128,256]{1,2,0:T(8,128)(2,1)}), bf16[8,128,256]{1,2,0:T(8,128)(2,1)S(1)}, u32[]{:S(2)}, u32[]{:S(2)}) async-start(bf16[8,128,256]{1,2,0:T(8,128)(2,1)} %pad_maximum_fusion), calls=%async_computation | async-start | bytes 1048576 | tf_op jit(solution)/shard_map/all_to_all | solution.py:277
  10.9 10.5 %all-to-all-done = bf16[8,128,256]{1,2,0:T(8,128)(2,1)S(1)} async-done(((bf16[8,128,256]{1,2,0:T(8,128)(2,1)}), bf16[8,128,256]{1,2,0:T(8,128)(2,1)S(1)}, u32[]{:S(2)}, u32[]{:S(2)}) %all-to-all-start) | async-done | bytes 524320 | tf_op jit(solution)/shard_map/all_to_all | solution.py:277
  21.6 1.6 collective-permute-start
  23.2 1.3 collective-permute-start.1
  24.5 3.1 %copy.27 = bf16[16,8,8,1024]{3,2,0,1:T(8,128)(2,1)} copy(bf16[16,8,8,1024]{3,2,1,0:T(8,128)(2,1)} %bitcast.49) | data formatting | bytes 4194304 | tf_op jit(solution)/shard_map/reshape | solution.py:281
  27.7 4.3 %all-to-all-start.1 = ((bf16[8,128,1024]{2,1,0:T(8,128)(2,1)}), bf16[8,128,1024]{2,1,0:T(8,128)(2,1)}, u32[]{:S(2)}, u32[]{:S(2)}) async-start(bf16[8,128,1024]{2,1,0:T(8,128)(2,1)} %bitcast.47), calls=%async_computation.1 | async-start | bytes 4194304 | tf_op jit(solution)/shard_map/all_to_all | solution.py:277
  32.0 1.8 %collective-permute-start.2 = (bf16[1024,256]{1,0:T(8,128)(2,1)S(1)}, bf16[1024,256]{1,0:T(8,128)(2,1)S(1)}, u32[]{:S(2)}, u32[]{:S(2)}) collective-permute-start(bf16[1024,256]{1,0:T(8,128)(2,1)S(1)} %bitcast.39), channel_id=1, source_target_pairs={{0,96},{32,0},{64,32},{96,64},{1,97},{33,1},{65,33},{97,65},{2,98}... | collective-permute-start | bytes 1572872 | tf_op jit(solution)/shard_map/ppermute | solution.py:255
  33.8 7.0 %shard_map.55 = (s32[8,132]{1,0:T(8,128)}, s32[8,132]{1,0:T(8,128)}, s32[8]{0:T(128)}) custom-call(s32[3]{0:T(128)} %pad_add_fusion.place_ref, s32[16,16,16]{2,1,0:T(8,128)} %codes_ref.1, s32[16,16]{1,0:T(8,128)} %counts_ref.1), custom_call_target="tpu_custom_call" | custom-call | bytes 20000000 | tf_op jit(solution)/shard_map/pallas_call | solution.py:66
  40.9 1.9 %collective-permute-start.4 = (bf16[1024,256]{1,0:T(8,128)(2,1)S(1)}, bf16[1024,256]{1,0:T(8,128)(2,1)S(1)}, u32[]{:S(2)}, u32[]{:S(2)}) collective-permute-start(bf16[1024,256]{1,0:T(8,128)(2,1)S(1)} %collective-permute-done.1), channel_id=1, source_target_pairs={{0,96},{32,0},{64,32},{96,64},{1,97},{33,1},{65,33},{97,65},{2,98}... | collective-permute-start | bytes 1572872 | tf_op jit(solution)/shard_map/ppermute | solution.py:255
  43.8 11.3 %collective-permute-done.4 = bf16[1024,256]{1,0:T(8,128)(2,1)S(1)} collective-permute-done((bf16[1024,256]{1,0:T(8,128)(2,1)S(1)}, bf16[1024,256]{1,0:T(8,128)(2,1)S(1)}, u32[]{:S(2)}, u32[]{:S(2)}) %collective-permute-start.4) | collective-permute-done | bytes 524320 | tf_op jit(solution)/shard_map/ppermute | solution.py:255
  55.1 2.4 %collective-permute-start.5 = (bf16[1024,256]{1,0:T(8,128)(2,1)S(1)}, bf16[1024,256]{1,0:T(8,128)(2,1)}, u32[]{:S(2)}, u32[]{:S(2)}) collective-permute-start(bf16[1024,256]{1,0:T(8,128)(2,1)S(1)} %collective-permute-done.4), channel_id=1, source_target_pairs={{0,96},{32,0},{64,32},{96,64},{1,97},{33,1},{65,33},{97,65},{2,98}... | collective-permute-start | bytes 1572872 | tf_op jit(solution)/shard_map/ppermute | solution.py:255
  57.5 1.4 collective-permute-done.3
  58.9 9.6 %collective-permute-done.6 = bf16[1024,256]{1,0:T(8,128)(2,1)} collective-permute-done((bf16[1024,256]{1,0:T(8,128)(2,1)S(1)}, bf16[1024,256]{1,0:T(8,128)(2,1)}, u32[]{:S(2)}, u32[]{:S(2)}) %collective-permute-start.6) | collective-permute-done | bytes 524320 | tf_op jit(solution)/shard_map/ppermute | solution.py:255
  68.6 0.8 copy-done
  70.7 1.1 collective-permute-done.9
  71.8 0.7 collective-permute-done.14
  72.5 0.7 collective-permute-done.13
  73.3 1.0 copy-done.1
  76.4 46.1 %shard_map.56 = bf16[1024,1024]{1,0:T(8,128)(2,1)} custom-call(s32[8,132]{1,0:T(8,128)S(1)} %copy-done.2, s32[8,132]{1,0:T(8,128)S(1)} %copy-done.3, s32[8]{0:T(128)S(1)} %copy-done.4, bf16[1024,1024]{1,0:T(8,128)(2,1)} %bitcast.9.queries, bf16[8,128,256]{2,1,0:T(8,128)(2,1)S(1)} %copy.21, bf16[8,128,256]{2,1,0:T(8,128)(2,1)S(1)} %bitcast.43, ...), custom_call_target="tpu_custom_call" | custom-call | flops 36238786560 | bytes 12000000 | tf_op jit(solution)/shard_map/pallas_call | solution.py:224
  122.6 34.2 %all_to_all.15 = bf16[8,128,1024]{2,1,0:T(8,128)(2,1)S(1)} all-to-all(bf16[8,128,1024]{2,1,0:T(8,128)(2,1)} %bitcast.50), channel_id=1, replica_groups=mesh['x'=4,'y_lo'=2,'core'=2,'y_hi'=2,'z'=4] {'y_hi','z'}, dimensions={0} | all-to-all | bytes 4194304 | tf_op jit(solution)/shard_map/all_to_all | solution.py:292
  156.8 1.5 copy.25
  (33 shorter events, 5.5 us)
Async XLA Ops:
  3.3 18.1 %all-to-all-start = ((bf16[8,128,256]{1,2,0:T(8,128)(2,1)}), bf16[8,128,256]{1,2,0:T(8,128)(2,1)S(1)}, u32[]{:S(2)}, u32[]{:S(2)}) async-start(bf16[8,128,256]{1,2,0:T(8,128)(2,1)} %pad_maximum_fusion), calls=%async_computation | async-start | bytes 1048576 | tf_op jit(solution)/shard_map/all_to_all | solution.py:277
  21.6 19.3 %collective-permute-start = (bf16[1024,256]{1,0:T(8,128)(2,1)S(1)}, bf16[1024,256]{1,0:T(8,128)(2,1)S(1)}, u32[]{:S(2)}, u32[]{:S(2)}) collective-permute-start(bf16[1024,256]{1,0:T(8,128)(2,1)S(1)} %bitcast.37), channel_id=1, source_target_pairs={{0,32},{32,64},{64,96},{96,0},{1,33},{33,65},{65,97},{97,1},{2,34}... | collective-permute-start | bytes 1572872 | tf_op jit(solution)/shard_map/ppermute | solution.py:255
  23.2 17.7 %collective-permute-start.1 = (bf16[1024,256]{1,0:T(8,128)(2,1)S(1)}, bf16[1024,256]{1,0:T(8,128)(2,1)S(1)}, u32[]{:S(2)}, u32[]{:S(2)}) collective-permute-start(bf16[1024,256]{1,0:T(8,128)(2,1)S(1)} %bitcast.38), channel_id=1, source_target_pairs={{0,16},{16,0},{1,17},{17,1},{2,18},{18,2},{3,19},{19,3},{4,20},{20... | collective-permute-start | bytes 1572872 | tf_op jit(solution)/shard_map/ppermute | solution.py:255
  27.7 43.1 %all-to-all-start.1 = ((bf16[8,128,1024]{2,1,0:T(8,128)(2,1)}), bf16[8,128,1024]{2,1,0:T(8,128)(2,1)}, u32[]{:S(2)}, u32[]{:S(2)}) async-start(bf16[8,128,1024]{2,1,0:T(8,128)(2,1)} %bitcast.47), calls=%async_computation.1 | async-start | bytes 4194304 | tf_op jit(solution)/shard_map/all_to_all | solution.py:277
  32.0 11.3 %collective-permute-start.2 = (bf16[1024,256]{1,0:T(8,128)(2,1)S(1)}, bf16[1024,256]{1,0:T(8,128)(2,1)S(1)}, u32[]{:S(2)}, u32[]{:S(2)}) collective-permute-start(bf16[1024,256]{1,0:T(8,128)(2,1)S(1)} %bitcast.39), channel_id=1, source_target_pairs={{0,96},{32,0},{64,32},{96,64},{1,97},{33,1},{65,33},{97,65},{2,98}... | collective-permute-start | bytes 1572872 | tf_op jit(solution)/shard_map/ppermute | solution.py:255
  33.8 9.5 %collective-permute-start.7 = (bf16[1024,256]{1,0:T(8,128)(2,1)S(1)}, bf16[1024,256]{1,0:T(8,128)(2,1)S(1)}, u32[]{:S(2)}, u32[]{:S(2)}) collective-permute-start(bf16[1024,256]{1,0:T(8,128)(2,1)S(1)} %bitcast.40), channel_id=1, source_target_pairs={{0,8},{8,0},{1,9},{9,1},{2,10},{10,2},{3,11},{11,3},{4,12},{12,4},... | collective-permute-start | bytes 1572872 | tf_op jit(solution)/shard_map/ppermute | solution.py:255
  40.9 14.2 %collective-permute-start.4 = (bf16[1024,256]{1,0:T(8,128)(2,1)S(1)}, bf16[1024,256]{1,0:T(8,128)(2,1)S(1)}, u32[]{:S(2)}, u32[]{:S(2)}) collective-permute-start(bf16[1024,256]{1,0:T(8,128)(2,1)S(1)} %collective-permute-done.1), channel_id=1, source_target_pairs={{0,96},{32,0},{64,32},{96,64},{1,97},{33,1},{65,33},{97,65},{2,98}... | collective-permute-start | bytes 1572872 | tf_op jit(solution)/shard_map/ppermute | solution.py:255
  42.8 16.2 %collective-permute-start.3 = (bf16[1024,256]{1,0:T(8,128)(2,1)S(1)}, bf16[1024,256]{1,0:T(8,128)(2,1)}, u32[]{:S(2)}, u32[]{:S(2)}) collective-permute-start(bf16[1024,256]{1,0:T(8,128)(2,1)S(1)} %collective-permute-done), channel_id=1, source_target_pairs={{0,32},{32,64},{64,96},{96,0},{1,33},{33,65},{65,97},{97,1},{2,34}... | collective-permute-start | bytes 1572872 | tf_op jit(solution)/shard_map/ppermute | solution.py:255
  43.0 25.6 %collective-permute-start.6 = (bf16[1024,256]{1,0:T(8,128)(2,1)S(1)}, bf16[1024,256]{1,0:T(8,128)(2,1)}, u32[]{:S(2)}, u32[]{:S(2)}) collective-permute-start(bf16[1024,256]{1,0:T(8,128)(2,1)S(1)} %collective-permute-done.1), channel_id=1, source_target_pairs={{0,32},{32,64},{64,96},{96,0},{1,33},{33,65},{65,97},{97,1},{2,34}... | collective-permute-start | bytes 1572872 | tf_op jit(solution)/shard_map/ppermute | solution.py:255
  43.3 25.3 %collective-permute-start.8 = (bf16[1024,256]{1,0:T(8,128)(2,1)S(1)}, bf16[1024,256]{1,0:T(8,128)(2,1)S(1)}, u32[]{:S(2)}, u32[]{:S(2)}) collective-permute-start(bf16[1024,256]{1,0:T(8,128)(2,1)S(1)} %collective-permute-done.2), channel_id=1, source_target_pairs={{0,8},{8,0},{1,9},{9,1},{2,10},{10,2},{3,11},{11,3},{4,12},{12,4},... | collective-permute-start | bytes 1572872 | tf_op jit(solution)/shard_map/ppermute | solution.py:255
  43.3 26.6 %collective-permute-start.10 = (bf16[1024,256]{1,0:T(8,128)(2,1)S(1)}, bf16[1024,256]{1,0:T(8,128)(2,1)S(1)}, u32[]{:S(2)}, u32[]{:S(2)}) collective-permute-start(bf16[1024,256]{1,0:T(8,128)(2,1)S(1)} %collective-permute-done), channel_id=1, source_target_pairs={{0,8},{8,0},{1,9},{9,1},{2,10},{10,2},{3,11},{11,3},{4,12},{12,4},... | collective-permute-start | bytes 1572872 | tf_op jit(solution)/shard_map/ppermute | solution.py:255
  55.1 14.9 %collective-permute-start.5 = (bf16[1024,256]{1,0:T(8,128)(2,1)S(1)}, bf16[1024,256]{1,0:T(8,128)(2,1)}, u32[]{:S(2)}, u32[]{:S(2)}) collective-permute-start(bf16[1024,256]{1,0:T(8,128)(2,1)S(1)} %collective-permute-done.4), channel_id=1, source_target_pairs={{0,96},{32,0},{64,32},{96,64},{1,97},{33,1},{65,33},{97,65},{2,98}... | collective-permute-start | bytes 1572872 | tf_op jit(solution)/shard_map/ppermute | solution.py:255
  58.9 11.8 %collective-permute-start.11 = (bf16[1024,256]{1,0:T(8,128)(2,1)S(1)}, bf16[1024,256]{1,0:T(8,128)(2,1)}, u32[]{:S(2)}, u32[]{:S(2)}) collective-permute-start(bf16[1024,256]{1,0:T(8,128)(2,1)S(1)} %collective-permute-done.1), channel_id=1, source_target_pairs={{0,8},{8,0},{1,9},{9,1},{2,10},{10,2},{3,11},{11,3},{4,12},{12,4},... | collective-permute-start | bytes 1572872 | tf_op jit(solution)/shard_map/ppermute | solution.py:255
  68.6 3.2 %collective-permute-start.12 = (bf16[1024,256]{1,0:T(8,128)(2,1)S(1)}, bf16[1024,256]{1,0:T(8,128)(2,1)}, u32[]{:S(2)}, u32[]{:S(2)}) collective-permute-start(bf16[1024,256]{1,0:T(8,128)(2,1)S(1)} %collective-permute-done.4), channel_id=1, source_target_pairs={{0,8},{8,0},{1,9},{9,1},{2,10},{10,2},{3,11},{11,3},{4,12},{12,4},... | collective-permute-start | bytes 1572872 | tf_op jit(solution)/shard_map/ppermute | solution.py:255
  68.6 0.8 copy-start
  69.4 2.4 %collective-permute-start.9 = (bf16[1024,256]{1,0:T(8,128)(2,1)}, bf16[1024,256]{1,0:T(8,128)(2,1)}, u32[]{:S(2)}, u32[]{:S(2)}) collective-permute-start(bf16[1024,256]{1,0:T(8,128)(2,1)} %collective-permute-done.3), channel_id=1, source_target_pairs={{0,8},{8,0},{1,9},{9,1},{2,10},{10,2},{3,11},{11,3},{4,12},{12,4},... | collective-permute-start | bytes 1572872 | tf_op jit(solution)/shard_map/ppermute | solution.py:255
  69.9 0.8 copy-start.5
  69.9 2.6 %collective-permute-start.14 = (bf16[1024,256]{1,0:T(8,128)(2,1)}, bf16[1024,256]{1,0:T(8,128)(2,1)}, u32[]{:S(2)}, u32[]{:S(2)}) collective-permute-start(bf16[1024,256]{1,0:T(8,128)(2,1)} %collective-permute-done.6), channel_id=1, source_target_pairs={{0,8},{8,0},{1,9},{9,1},{2,10},{10,2},{3,11},{11,3},{4,12},{12,4},... | collective-permute-start | bytes 1572872 | tf_op jit(solution)/shard_map/ppermute | solution.py:255
  70.7 2.6 %collective-permute-start.13 = (bf16[1024,256]{1,0:T(8,128)(2,1)}, bf16[1024,256]{1,0:T(8,128)(2,1)}, u32[]{:S(2)}, u32[]{:S(2)}) collective-permute-start(bf16[1024,256]{1,0:T(8,128)(2,1)} %collective-permute-done.5), channel_id=1, source_target_pairs={{0,8},{8,0},{1,9},{9,1},{2,10},{10,2},{3,11},{11,3},{4,12},{12,4},... | collective-permute-start | bytes 1572872 | tf_op jit(solution)/shard_map/ppermute | solution.py:255
  73.3 1.0 copy-start.1
  74.3 0.7 copy-start.2
  75.0 0.7 copy-start.3
  75.7 0.7 copy-start.4
where the time goes:
time: 160 us; the launch traced here: 158 us
  Pallas kernels  53.2 us (33%)
  waiting for transfers between devices  35.7 us (22%)
  blocking collectives  34.2 us (21%)
  starting transfers between devices  21.8 us (14%)
  local copies, waits for them, and re-layouts  11.9 us (7%)
    pallas_call x1, Pallas kernels, attend(): pl.pallas_call(functools.partial(attend_kernel, heads=heads, shards=shard...  46.1 us
    all_to_all x1, blocking collectives, local(): lax.all_to_all(attended.reshape(parts, tokens, -1), head_axes, split_axis...  34.2 us
    ppermute x15, waiting for transfers between devices, shift(): lax.ppermute(array, axis, [(i, (i + step) % size) for i in range(size)])  25.2 us
    all_to_all x2, starting transfers between devices, exchange(): lax.all_to_all(cut, head_axes, split_axis=0, concat_axis=0, tiled=True)  11.4 us
    all_to_all x2, waiting for transfers between devices, exchange(): lax.all_to_all(cut, head_axes, split_axis=0, concat_axis=0, tiled=True)  10.5 us
    ppermute x15, starting transfers between devices, shift(): lax.ppermute(array, axis, [(i, (i + step) % size) for i in range(size)])  10.4 us
    pallas_call x1, Pallas kernels, plan(): pl.pallas_call(functools.partial(plan_kernel, blocks=blocks, sizes=sizes,...  7.04 us
    unnamed x14, local copies, waits for them, and re-layouts  6.85 us
  transfers between devices with their start and end apart: 17, of which 8 were waited for; matrix products, arithmetic and copies ran while one was open for 2% of the time, Pallas kernels for 4%

commit v1 on v0

--- a/solution.py
+++ b/solution.py
@@ -18,13 +18,13 @@
 PIECE = 512
 
 
-def plan_kernel(place_ref, codes_ref, counts_ref, key_ref, value_ref, chunks_ref, fill_ref, *, blocks, sizes, zero):
+def plan_kernel(place_ref, codes_ref, counts_ref, list_ref, fill_ref, *, blocks, sizes, zero):
     x_size, y_size, core_size = sizes
     x, y, core = place_ref[0], place_ref[1], place_ref[2]
     shard = (x * y_size + y) * core_size + core
     for a in range(blocks):
-        key_ref[a, 0] = a
-        value_ref[a, 0] = a
+        list_ref[a, 0] = a
+        list_ref[blocks + a, 0] = a
         fill_ref[a] = 1
 
     def visit_shard(slot, _):
@@ -38,8 +38,8 @@
             a = lax.div(code, blocks)
             block = slot * blocks + lax.rem(code, blocks)
             at = fill_ref[a]
-            key_ref[a, at] = block
-            value_ref[a, at] = block
+            list_ref[a, at] = block
+            list_ref[blocks + a, at] = block
             fill_ref[a] = at + 1
             return 0
 
@@ -49,11 +49,11 @@
     for a in range(blocks):
         filled = fill_ref[a]
         chunks = lax.div(filled + CHUNK - 1, CHUNK)
-        chunks_ref[a] = chunks
+        list_ref[2 * blocks, a] = chunks
 
         def pad(at, _):
-            key_ref[a, at] = a
-            value_ref[a, at] = zero
+            list_ref[a, at] = a
+            list_ref[blocks + a, at] = zero
             return 0
 
         lax.fori_loop(filled, chunks * CHUNK, pad, 0)
@@ -66,22 +66,18 @@
     return pl.pallas_call(
         functools.partial(plan_kernel, blocks=blocks, sizes=sizes, zero=zero),
         in_specs=[smem] * 3,
-        out_specs=[smem] * 3,
-        out_shape=[
-            jax.ShapeDtypeStruct((blocks, width), jnp.int32),
-            jax.ShapeDtypeStruct((blocks, width), jnp.int32),
-            jax.ShapeDtypeStruct((blocks,), jnp.int32),
-        ],
+        out_specs=smem,
+        out_shape=jax.ShapeDtypeStruct((2 * blocks + 1, width), jnp.int32),
         scratch_shapes=[pltpu.SMEM((blocks,), jnp.int32)],
         cost_estimate=pl.CostEstimate(flops=0, bytes_accessed=20_000_000, transcendentals=0),
     )(place, live_keys, live_count)
 
 
-def attend_kernel(key_at, value_at, chunks, queries, *refs, heads, shards):
+def attend_kernel(listed, queries, *refs, heads, shards):
     pieces, (out, pairs, ones, total, peak, scaled, *rest) = refs[:shards], refs[shards:]
     groups = heads // GROUP_HEADS
     raw, soft, (level, fade, late_fade, ready, sem) = rest[:groups], rest[groups : groups + 2], rest[groups + 2 :]
-    b = pl.program_id(0)
+    b, blocks = pl.program_id(0), pl.num_programs(0)
     count = pairs.shape[0] - 1
     span = count // shards
     width = GROUP_HEADS * BLOCK
@@ -102,8 +98,8 @@
     def arrive(i):
         @pl.when(b == 0)
         def _():
-            last = lax.div(key_at[b, i * CHUNK + CHUNK - 1], span) + 1
-            needed = jnp.where(i >= chunks[b] - 1, shards, last)
+            last = lax.div(listed[b, i * CHUNK + CHUNK - 1], span) + 1
+            needed = jnp.where(i >= listed[2 * blocks, b] - 1, shards, last)
             for j in range(shards):
 
                 @pl.when((j >= ready[0]) & (j < needed))
@@ -114,11 +110,11 @@
 
     def keys_of(i):
         return jnp.concatenate(
-            [pairs[key_at[b, i * CHUNK + c], :, :HEAD_DIM] for c in range(CHUNK)], axis=0
+            [pairs[listed[b, i * CHUNK + c], :, :HEAD_DIM] for c in range(CHUNK)], axis=0
         )
 
     def values_of(i):
-        slots = [value_at[b, i * CHUNK + c] for c in range(CHUNK)]
+        slots = [listed[blocks + b, i * CHUNK + c] for c in range(CHUNK)]
         return jnp.concatenate(
             [
                 jnp.concatenate([pairs[s, :, HEAD_DIM:] for s in slots], axis=1),
@@ -160,7 +156,7 @@
     level[...] = jnp.max(partial_max(raw[0][...]), axis=0, keepdims=True)
     peak[:, columns(0)] = level[...]
     fade[...] = jnp.zeros(fade.shape, jnp.float32)
-    end = chunks[b]
+    end = listed[2 * blocks, b]
 
     def visit(i, _):
         following = jnp.minimum(i + 1, end - 1)
@@ -219,12 +215,12 @@
     shards = len(pieces)
     span = pieces[0].shape[0] // BLOCK
     count = shards * span
-    pieces = [piece.reshape(span, BLOCK, -1) for piece in pieces]
+    pieces = [pltpu.with_memory_space_constraint(piece.reshape(span, BLOCK, -1), pltpu.HBM) for piece in pieces]
     pair_estimate = 180 * 2 * 2 * heads * BLOCK * BLOCK * HEAD_DIM
     return pl.pallas_call(
         functools.partial(attend_kernel, heads=heads, shards=shards),
         grid_spec=pltpu.PrefetchScalarGridSpec(
-            num_scalar_prefetch=3,
+            num_scalar_prefetch=1,
             grid=(rows // BLOCK,),
             in_specs=[pl.BlockSpec((BLOCK, width), lambda b, *_: (b, 0))]
             + [pl.BlockSpec(memory_space=pl.ANY)] * shards,
@@ -247,7 +243,7 @@
         out_shape=jax.ShapeDtypeStruct((rows, width), jnp.bfloat16),
         compiler_params=pltpu.CompilerParams(vmem_limit_bytes=48 * 1024 * 1024),
         cost_estimate=pl.CostEstimate(flops=pair_estimate * 3, bytes_accessed=12_000_000, transcendentals=0),
-    )(*lists, queries, *pieces)
+    )(lists, queries, *pieces)
 
 
 def shift(array, axis, step):
@@ -255,15 +251,14 @@
     return lax.ppermute(array, axis, [(i, (i + step) % size) for i in range(size)])
 
 
-def gather_shards(own, meanwhile):
+def gather_shards(own):
+    across = shift(own, "y_lo", 1)
     here = [own, shift(own, "x", -1), None, shift(own, "x", 1)]
-    across = shift(own, "y_lo", 1)
-    here[3], across, result = lax.optimization_barrier((here[3], across, meanwhile()))
     here[2] = shift(here[3], "x", 1)
     there = [across, shift(across, "x", -1), None, shift(across, "x", 1)]
     there[2] = shift(there[1], "x", -1)
     near = here + there
-    return near + [shift(piece, "core", 1) for piece in near], result
+    return near + [shift(piece, "core", 1) for piece in near]
 
 
 def local(queries, keys, values, live_keys, live_count):
@@ -284,11 +279,10 @@
         jnp.concatenate([cut(keys).transpose(1, 0, 2), cut(values).transpose(1, 2, 0)], axis=2)
     )
     place = jnp.stack([lax.axis_index(axis) for axis in blk_axes]).astype(jnp.int32)
-    own, place = lax.optimization_barrier((own, place))
-    zero = live_keys.shape[0] * blocks
-    pieces, lists = gather_shards(own, lambda: plan(place, live_keys, live_count, blocks, sizes, zero))
-    query_local = exchange(cut(queries).transpose(1, 0, 2))
-    attended = attend(query_local, pieces, lists)
+    lists = plan(place, live_keys, live_count, blocks, sizes, live_keys.shape[0] * blocks)
+    own, lists, query_parts = lax.optimization_barrier((own, lists, cut(queries).transpose(1, 0, 2)))
+    pieces = gather_shards(own)
+    attended = attend(exchange(query_parts), pieces, lists)
     back = lax.all_to_all(
         attended.reshape(parts, tokens, -1), head_axes, split_axis=0, concat_axis=0, tiled=True
     )

time: 160 us -> 158 us (0.988)
  the two profiles are of different devices: /device:TPU:8 before, /device:TPU:1 now
where the time goes in v1:
time: 158 us
  Pallas kernels  57.7 us (37%)
  starting transfers between devices  36.3 us (23%)
  blocking collectives  33.2 us (21%)
  waiting for transfers between devices  21.6 us (14%)
  local copies, waits for them, and re-layouts  7.57 us (5%)
    pallas_call x1, Pallas kernels, attend(): pl.pallas_call(functools.partial(attend_kernel, heads=heads, shards=shard...  49.7 us
    all_to_all x1, blocking collectives, local(): lax.all_to_all(attended.reshape(parts, tokens, -1), head_axes, split_axis...  33.2 us
    ppermute x15, waiting for transfers between devices, shift(): lax.ppermute(array, axis, [(i, (i + step) % size) for i in range(size)])  21.6 us
    ppermute x15, starting transfers between devices, shift(): lax.ppermute(array, axis, [(i, (i + step) % size) for i in range(size)])  20.6 us
    all_to_all x2, starting transfers between devices, exchange(): lax.all_to_all(cut, head_axes, split_axis=0, concat_axis=0, tiled=True)  15.7 us
    pallas_call x1, Pallas kernels, plan(): pl.pallas_call(functools.partial(plan_kernel, blocks=blocks, sizes=sizes,...  7.99 us
    unnamed x32, local copies, waits for them, and re-layouts  4.17 us
  transfers between devices with their start and end apart: 17, of which 4 were waited for; matrix products, arithmetic and copies ran while one was open for 1% of the time, Pallas kernels for 5%

profile of v1, /device:TPU:1, one launch (start us, length us, event | category | flops | bytes accessed | tf_op | source)
XLA Modules:
  0.0 158.0 jit_solution(13117885578716109984)
XLA Ops:
  0.0 1.3 copy.18
  1.3 1.1 copy.19
  2.6 0.8 pad_maximum_fusion
  3.4 8.5 %all-to-all-start = ((bf16[8,128,256]{1,2,0:T(8,128)(2,1)}), bf16[8,128,256]{1,2,0:T(8,128)(2,1)S(1)}, u32[]{:S(2)}, u32[]{:S(2)}) async-start(bf16[8,128,256]{1,2,0:T(8,128)(2,1)} %pad_maximum_fusion), calls=%async_computation | async-start | bytes 1048576 | tf_op jit(solution)/shard_map/all_to_all | solution.py:272
  11.9 1.5 copy.27
  14.0 8.0 %shard_map.55.listed = s32[17,132]{1,0:T(8,128)} custom-call(s32[3]{0:T(128)} %pad_add_fusion.place_ref, s32[16,16,16]{2,1,0:T(8,128)} %codes_ref.1, s32[16,16]{1,0:T(8,128)} %counts_ref.1), custom_call_target="tpu_custom_call" | custom-call | bytes 20000000 | tf_op jit(solution)/shard_map/pallas_call | solution.py:66
  22.4 7.2 %all-to-all-start.1 = ((bf16[8,128,1024]{2,1,0:T(8,128)(2,1)}), bf16[8,128,1024]{2,1,0:T(8,128)(2,1)S(1)}, u32[]{:S(2)}, u32[]{:S(2)}) async-start(bf16[8,128,1024]{2,1,0:T(8,128)(2,1)} %bitcast.39), calls=%async_computation.1 | async-start | bytes 4194304 | tf_op jit(solution)/shard_map/all_to_all | solution.py:272
  29.7 1.6 collective-permute-start.7
  31.2 1.0 collective-permute-start.1
  32.2 1.7 %collective-permute-start = (bf16[1024,256]{1,0:T(8,128)(2,1)S(1)}, bf16[1024,256]{1,0:T(8,128)(2,1)S(1)}, u32[]{:S(2)}, u32[]{:S(2)}) collective-permute-start(bf16[1024,256]{1,0:T(8,128)(2,1)S(1)} %bitcast.48), channel_id=1, source_target_pairs={{0,96},{32,0},{64,32},{96,64},{1,97},{33,1},{65,33},{97,65},{2,98}... | collective-permute-start | bytes 1572872 | tf_op jit(solution)/shard_map/ppermute | solution.py:251
  33.9 2.1 %collective-permute-start.4 = (bf16[1024,256]{1,0:T(8,128)(2,1)S(1)}, bf16[1024,256]{1,0:T(8,128)(2,1)S(1)}, u32[]{:S(2)}, u32[]{:S(2)}) collective-permute-start(bf16[1024,256]{1,0:T(8,128)(2,1)S(1)} %collective-permute-done.3), channel_id=1, source_target_pairs={{0,96},{32,0},{64,32},{96,64},{1,97},{33,1},{65,33},{97,65},{2,98}... | collective-permute-start | bytes 1572872 | tf_op jit(solution)/shard_map/ppermute | solution.py:251
  36.1 5.8 %collective-permute-start.11 = (bf16[1024,256]{1,0:T(8,128)(2,1)S(1)}, bf16[1024,256]{1,0:T(8,128)(2,1)S(1)}, u32[]{:S(2)}, u32[]{:S(2)}) collective-permute-start(bf16[1024,256]{1,0:T(8,128)(2,1)S(1)} %collective-permute-done.3), channel_id=1, source_target_pairs={{0,8},{8,0},{1,9},{9,1},{2,10},{10,2},{3,11},{11,3},{4,12},{12,4},... | collective-permute-start | bytes 1572872 | tf_op jit(solution)/shard_map/ppermute | solution.py:251
  41.9 4.1 %collective-permute-done.1 = bf16[1024,256]{1,0:T(8,128)(2,1)S(1)} collective-permute-done((bf16[1024,256]{1,0:T(8,128)(2,1)S(1)}, bf16[1024,256]{1,0:T(8,128)(2,1)S(1)}, u32[]{:S(2)}, u32[]{:S(2)}) %collective-permute-start.1) | collective-permute-done | bytes 524320 | tf_op jit(solution)/shard_map/ppermute | solution.py:251
  46.0 1.3 collective-permute-start.10
  47.3 9.9 %collective-permute-done.4 = bf16[1024,256]{1,0:T(8,128)(2,1)S(1)} collective-permute-done((bf16[1024,256]{1,0:T(8,128)(2,1)S(1)}, bf16[1024,256]{1,0:T(8,128)(2,1)S(1)}, u32[]{:S(2)}, u32[]{:S(2)}) %collective-permute-start.4) | collective-permute-done | bytes 524320 | tf_op jit(solution)/shard_map/ppermute | solution.py:251
  57.2 2.4 %collective-permute-start.5 = (bf16[1024,256]{1,0:T(8,128)(2,1)S(1)}, bf16[1024,256]{1,0:T(8,128)(2,1)}, u32[]{:S(2)}, u32[]{:S(2)}) collective-permute-start(bf16[1024,256]{1,0:T(8,128)(2,1)S(1)} %collective-permute-done.4), channel_id=1, source_target_pairs={{0,96},{32,0},{64,32},{96,64},{1,97},{33,1},{65,33},{97,65},{2,98}... | collective-permute-start | bytes 1572872 | tf_op jit(solution)/shard_map/ppermute | solution.py:251
  59.6 1.5 collective-permute-start.8
  61.5 6.9 %collective-permute-done.2 = bf16[1024,256]{1,0:T(8,128)(2,1)S(1)} collective-permute-done((bf16[1024,256]{1,0:T(8,128)(2,1)S(1)}, bf16[1024,256]{1,0:T(8,128)(2,1)S(1)}, u32[]{:S(2)}, u32[]{:S(2)}) %collective-permute-start.2) | collective-permute-done | bytes 524320 | tf_op jit(solution)/shard_map/ppermute | solution.py:251
  68.4 0.8 collective-permute-start.9
  69.9 1.8 %collective-permute-start.13 = (bf16[1024,256]{1,0:T(8,128)(2,1)}, bf16[1024,256]{1,0:T(8,128)(2,1)}, u32[]{:S(2)}, u32[]{:S(2)}) collective-permute-start(bf16[1024,256]{1,0:T(8,128)(2,1)} %collective-permute-done.5), channel_id=1, source_target_pairs={{0,8},{8,0},{1,9},{9,1},{2,10},{10,2},{3,11},{11,3},{4,12},{12,4},... | collective-permute-start | bytes 1572872 | tf_op jit(solution)/shard_map/ppermute | solution.py:251
  72.8 0.8 copy-done.13
  73.6 49.7 %shard_map.56 = bf16[1024,1024]{1,0:T(8,128)(2,1)S(1)} custom-call(s32[17,132]{1,0:T(8,128)S(1)} %copy-done, bf16[1024,1024]{1,0:T(8,128)(2,1)S(1)} %bitcast.37, bf16[8,128,256]{2,1,0:T(8,128)(2,1)} %copy-done.2, bf16[8,128,256]{2,1,0:T(8,128)(2,1)} %bitcast.52, bf16[8,128,256]{2,1,0:T(8,128)(2,1)} %bitcast.57, bf16[8,128,256]{2,1,0:T(8,128)(2,1)} %bitcast.51, ...), custom_call_target="tpu_custom_call" | custom-call | flops 36238786560 | bytes 12000000 | tf_op jit(solution)/shard_map/pallas_call | solution.py:220
  123.3 33.2 %all_to_all.15 = bf16[8,128,1024]{2,1,0:T(8,128)(2,1)S(1)} all-to-all(bf16[8,128,1024]{2,1,0:T(8,128)(2,1)S(1)} %bitcast.38), channel_id=1, replica_groups=mesh['x'=4,'y_lo'=2,'core'=2,'y_hi'=2,'z'=4] {'y_hi','z'}, dimensions={0} | all-to-all | bytes 4194304 | tf_op jit(solution)/shard_map/all_to_all | solution.py:286
  156.5 1.5 copy.25
  (51 shorter events, 3.4 us)
Async XLA Ops:
  3.4 18.6 %all-to-all-start = ((bf16[8,128,256]{1,2,0:T(8,128)(2,1)}), bf16[8,128,256]{1,2,0:T(8,128)(2,1)S(1)}, u32[]{:S(2)}, u32[]{:S(2)}) async-start(bf16[8,128,256]{1,2,0:T(8,128)(2,1)} %pad_maximum_fusion), calls=%async_computation | async-start | bytes 1048576 | tf_op jit(solution)/shard_map/all_to_all | solution.py:272
  22.3 51.3 %copy-start = (s32[17,132]{1,0:T(8,128)S(1)}, s32[17,132]{1,0:T(8,128)}, u32[]{:S(2)}) copy-start(s32[17,132]{1,0:T(8,128)} %shard_map.55.listed) | copy-start | bytes 26932
  22.3 11.7 %collective-permute-start.3 = (bf16[1024,256]{1,0:T(8,128)(2,1)S(1)}, bf16[1024,256]{1,0:T(8,128)(2,1)S(1)}, u32[]{:S(2)}, u32[]{:S(2)}) collective-permute-start(bf16[1024,256]{1,0:T(8,128)(2,1)S(1)} %bitcast.45), channel_id=1, source_target_pairs={{0,16},{16,0},{1,17},{17,1},{2,18},{18,2},{3,19},{19,3},{4,20},{20... | collective-permute-start | bytes 1572872 | tf_op jit(solution)/shard_map/ppermute | solution.py:251
  22.4 51.1 %all-to-all-start.1 = ((bf16[8,128,1024]{2,1,0:T(8,128)(2,1)}), bf16[8,128,1024]{2,1,0:T(8,128)(2,1)S(1)}, u32[]{:S(2)}, u32[]{:S(2)}) async-start(bf16[8,128,1024]{2,1,0:T(8,128)(2,1)} %bitcast.39), calls=%async_computation.1 | async-start | bytes 4194304 | tf_op jit(solution)/shard_map/all_to_all | solution.py:272
  29.7 12.2 %collective-permute-start.7 = (bf16[1024,256]{1,0:T(8,128)(2,1)S(1)}, bf16[1024,256]{1,0:T(8,128)(2,1)S(1)}, u32[]{:S(2)}, u32[]{:S(2)}) collective-permute-start(bf16[1024,256]{1,0:T(8,128)(2,1)S(1)} %bitcast.46), channel_id=1, source_target_pairs={{0,8},{8,0},{1,9},{9,1},{2,10},{10,2},{3,11},{11,3},{4,12},{12,4},... | collective-permute-start | bytes 1572872 | tf_op jit(solution)/shard_map/ppermute | solution.py:251
  31.2 14.7 %collective-permute-start.1 = (bf16[1024,256]{1,0:T(8,128)(2,1)S(1)}, bf16[1024,256]{1,0:T(8,128)(2,1)S(1)}, u32[]{:S(2)}, u32[]{:S(2)}) collective-permute-start(bf16[1024,256]{1,0:T(8,128)(2,1)S(1)} %bitcast.47), channel_id=1, source_target_pairs={{0,32},{32,64},{64,96},{96,0},{1,33},{33,65},{65,97},{97,1},{2,34}... | collective-permute-start | bytes 1572872 | tf_op jit(solution)/shard_map/ppermute | solution.py:251
  32.2 15.1 %collective-permute-start = (bf16[1024,256]{1,0:T(8,128)(2,1)S(1)}, bf16[1024,256]{1,0:T(8,128)(2,1)S(1)}, u32[]{:S(2)}, u32[]{:S(2)}) collective-permute-start(bf16[1024,256]{1,0:T(8,128)(2,1)S(1)} %bitcast.48), channel_id=1, source_target_pairs={{0,96},{32,0},{64,32},{96,64},{1,97},{33,1},{65,33},{97,65},{2,98}... | collective-permute-start | bytes 1572872 | tf_op jit(solution)/shard_map/ppermute | solution.py:251
  33.9 39.6 %copy-start.3 = (bf16[1024,256]{1,0:T(8,128)(2,1)}, bf16[1024,256]{1,0:T(8,128)(2,1)S(1)}, u32[]{:S(2)}) copy-start(bf16[1024,256]{1,0:T(8,128)(2,1)S(1)} %collective-permute-done.3) | copy-start | bytes 1572868
  33.9 23.3 %collective-permute-start.4 = (bf16[1024,256]{1,0:T(8,128)(2,1)S(1)}, bf16[1024,256]{1,0:T(8,128)(2,1)S(1)}, u32[]{:S(2)}, u32[]{:S(2)}) collective-permute-start(bf16[1024,256]{1,0:T(8,128)(2,1)S(1)} %collective-permute-done.3), channel_id=1, source_target_pairs={{0,96},{32,0},{64,32},{96,64},{1,97},{33,1},{65,33},{97,65},{2,98}... | collective-permute-start | bytes 1572872 | tf_op jit(solution)/shard_map/ppermute | solution.py:251
  36.1 23.5 %collective-permute-start.11 = (bf16[1024,256]{1,0:T(8,128)(2,1)S(1)}, bf16[1024,256]{1,0:T(8,128)(2,1)S(1)}, u32[]{:S(2)}, u32[]{:S(2)}) collective-permute-start(bf16[1024,256]{1,0:T(8,128)(2,1)S(1)} %collective-permute-done.3), channel_id=1, source_target_pairs={{0,8},{8,0},{1,9},{9,1},{2,10},{10,2},{3,11},{11,3},{4,12},{12,4},... | collective-permute-start | bytes 1572872 | tf_op jit(solution)/shard_map/ppermute | solution.py:251
  41.9 29.8 %copy-start.4 = (bf16[1024,256]{1,0:T(8,128)(2,1)}, bf16[1024,256]{1,0:T(8,128)(2,1)S(1)}, u32[]{:S(2)}) copy-start(bf16[1024,256]{1,0:T(8,128)(2,1)S(1)} %collective-permute-done.7) | copy-start | bytes 1572868
  41.9 19.1 %collective-permute-start.6 = (bf16[1024,256]{1,0:T(8,128)(2,1)S(1)}, bf16[1024,256]{1,0:T(8,128)(2,1)S(1)}, u32[]{:S(2)}, u32[]{:S(2)}) collective-permute-start(bf16[1024,256]{1,0:T(8,128)(2,1)S(1)} %collective-permute-done.3), channel_id=1, source_target_pairs={{0,32},{32,64},{64,96},{96,0},{1,33},{33,65},{65,97},{97,1},{2,34}... | collective-permute-start | bytes 1572872 | tf_op jit(solution)/shard_map/ppermute | solution.py:251
  46.0 25.8 %copy-start.5 = (bf16[1024,256]{1,0:T(8,128)(2,1)}, bf16[1024,256]{1,0:T(8,128)(2,1)S(1)}, u32[]{:S(2)}) copy-start(bf16[1024,256]{1,0:T(8,128)(2,1)S(1)} %collective-permute-done.1) | copy-start | bytes 1572868
  46.0 15.2 %collective-permute-start.10 = (bf16[1024,256]{1,0:T(8,128)(2,1)S(1)}, bf16[1024,256]{1,0:T(8,128)(2,1)S(1)}, u32[]{:S(2)}, u32[]{:S(2)}) collective-permute-start(bf16[1024,256]{1,0:T(8,128)(2,1)S(1)} %collective-permute-done.1), channel_id=1, source_target_pairs={{0,8},{8,0},{1,9},{9,1},{2,10},{10,2},{3,11},{11,3},{4,12},{12,4},... | collective-permute-start | bytes 1572872 | tf_op jit(solution)/shard_map/ppermute | solution.py:251
  47.3 24.5 %copy-start.6 = (bf16[1024,256]{1,0:T(8,128)(2,1)}, bf16[1024,256]{1,0:T(8,128)(2,1)S(1)}, u32[]{:S(2)}) copy-start(bf16[1024,256]{1,0:T(8,128)(2,1)S(1)} %collective-permute-done) | copy-start | bytes 1572868
  47.3 21.2 %collective-permute-start.2 = (bf16[1024,256]{1,0:T(8,128)(2,1)S(1)}, bf16[1024,256]{1,0:T(8,128)(2,1)S(1)}, u32[]{:S(2)}, u32[]{:S(2)}) collective-permute-start(bf16[1024,256]{1,0:T(8,128)(2,1)S(1)} %collective-permute-done.1), channel_id=1, source_target_pairs={{0,32},{32,64},{64,96},{96,0},{1,33},{33,65},{65,97},{97,1},{2,34}... | collective-permute-start | bytes 1572872 | tf_op jit(solution)/shard_map/ppermute | solution.py:251
  57.2 14.6 %copy-start.7 = (bf16[1024,256]{1,0:T(8,128)(2,1)}, bf16[1024,256]{1,0:T(8,128)(2,1)S(1)}, u32[]{:S(2)}) copy-start(bf16[1024,256]{1,0:T(8,128)(2,1)S(1)} %collective-permute-done.4) | copy-start | bytes 1572868
  57.2 12.7 %collective-permute-start.5 = (bf16[1024,256]{1,0:T(8,128)(2,1)S(1)}, bf16[1024,256]{1,0:T(8,128)(2,1)}, u32[]{:S(2)}, u32[]{:S(2)}) collective-permute-start(bf16[1024,256]{1,0:T(8,128)(2,1)S(1)} %collective-permute-done.4), channel_id=1, source_target_pairs={{0,96},{32,0},{64,32},{96,64},{1,97},{33,1},{65,33},{97,65},{2,98}... | collective-permute-start | bytes 1572872 | tf_op jit(solution)/shard_map/ppermute | solution.py:251
  59.6 12.2 %copy-start.8 = (bf16[1024,256]{1,0:T(8,128)(2,1)}, bf16[1024,256]{1,0:T(8,128)(2,1)S(1)}, u32[]{:S(2)}) copy-start(bf16[1024,256]{1,0:T(8,128)(2,1)S(1)} %collective-permute-done.11) | copy-start | bytes 1572868
  59.6 12.1 %collective-permute-start.8 = (bf16[1024,256]{1,0:T(8,128)(2,1)S(1)}, bf16[1024,256]{1,0:T(8,128)(2,1)S(1)}, u32[]{:S(2)}, u32[]{:S(2)}) collective-permute-start(bf16[1024,256]{1,0:T(8,128)(2,1)S(1)} %collective-permute-done), channel_id=1, source_target_pairs={{0,8},{8,0},{1,9},{9,1},{2,10},{10,2},{3,11},{11,3},{4,12},{12,4},... | collective-permute-start | bytes 1572872 | tf_op jit(solution)/shard_map/ppermute | solution.py:251
  61.0 10.7 %collective-permute-start.12 = (bf16[1024,256]{1,0:T(8,128)(2,1)S(1)}, bf16[1024,256]{1,0:T(8,128)(2,1)S(1)}, u32[]{:S(2)}, u32[]{:S(2)}) collective-permute-start(bf16[1024,256]{1,0:T(8,128)(2,1)S(1)} %collective-permute-done.4), channel_id=1, source_target_pairs={{0,8},{8,0},{1,9},{9,1},{2,10},{10,2},{3,11},{11,3},{4,12},{12,4},... | collective-permute-start | bytes 1572872 | tf_op jit(solution)/shard_map/ppermute | solution.py:251
  61.1 10.6 %collective-permute-start.14 = (bf16[1024,256]{1,0:T(8,128)(2,1)S(1)}, bf16[1024,256]{1,0:T(8,128)(2,1)S(1)}, u32[]{:S(2)}, u32[]{:S(2)}) collective-permute-start(bf16[1024,256]{1,0:T(8,128)(2,1)S(1)} %collective-permute-done.6), channel_id=1, source_target_pairs={{0,8},{8,0},{1,9},{9,1},{2,10},{10,2},{3,11},{11,3},{4,12},{12,4},... | collective-permute-start | bytes 1572872 | tf_op jit(solution)/shard_map/ppermute | solution.py:251
  68.4 5.1 %collective-permute-start.9 = (bf16[1024,256]{1,0:T(8,128)(2,1)S(1)}, bf16[1024,256]{1,0:T(8,128)(2,1)}, u32[]{:S(2)}, u32[]{:S(2)}) collective-permute-start(bf16[1024,256]{1,0:T(8,128)(2,1)S(1)} %collective-permute-done.2), channel_id=1, source_target_pairs={{0,8},{8,0},{1,9},{9,1},{2,10},{10,2},{3,11},{11,3},{4,12},{12,4},... | collective-permute-start | bytes 1572872 | tf_op jit(solution)/shard_map/ppermute | solution.py:251
  69.9 3.7 %collective-permute-start.13 = (bf16[1024,256]{1,0:T(8,128)(2,1)}, bf16[1024,256]{1,0:T(8,128)(2,1)}, u32[]{:S(2)}, u32[]{:S(2)}) collective-permute-start(bf16[1024,256]{1,0:T(8,128)(2,1)} %collective-permute-done.5), channel_id=1, source_target_pairs={{0,8},{8,0},{1,9},{9,1},{2,10},{10,2},{3,11},{11,3},{4,12},{12,4},... | collective-permute-start | bytes 1572872 | tf_op jit(solution)/shard_map/ppermute | solution.py:251
  (8 other events, 51.1 us)

commit v2 on v1

--- a/solution.py
+++ b/solution.py
@@ -16,6 +16,7 @@
 CHUNK = 4
 GROUP_HEADS = 2
 PIECE = 512
+WAVE = 4
 
 
 def plan_kernel(place_ref, codes_ref, counts_ref, list_ref, fill_ref, *, blocks, sizes, zero):
@@ -74,7 +75,7 @@
 
 
 def attend_kernel(listed, queries, *refs, heads, shards):
-    pieces, (out, pairs, ones, total, peak, scaled, *rest) = refs[:shards], refs[shards:]
+    pieces, (out, pairs, ones, total, peak, *rest) = refs[:shards], refs[shards:]
     groups = heads // GROUP_HEADS
     raw, soft, (level, fade, late_fade, ready, sem) = rest[:groups], rest[groups : groups + 2], rest[groups + 2 :]
     b, blocks = pl.program_id(0), pl.num_programs(0)
@@ -88,7 +89,7 @@
 
     @pl.when(b == 0)
     def _():
-        for j in range(shards):
+        for j in range(WAVE):
             arrival(j).start()
         ready[0] = 0
         ones[0] = jnp.ones(ones.shape[1:], jnp.bfloat16)
@@ -105,6 +106,8 @@
                 @pl.when((j >= ready[0]) & (j < needed))
                 def _():
                     arrival(j).wait()
+                    if j + WAVE < shards:
+                        arrival(j + WAVE).start()
 
             ready[0] = jnp.maximum(ready[0], needed)
 
@@ -129,22 +132,15 @@
         return slice(g * width, (g + 1) * width)
 
     def score(keys, g):
-        return lax.dot_general(
-            jnp.concatenate([keys, keys], axis=1),
-            scaled[columns(g), :],
-            (((1,), (1,)), ((), ())),
-            preferred_element_type=jnp.float32,
-        )
+        first = g * GROUP_HEADS
+        tile = jnp.concatenate(
+            [queries[:, h * HEAD_DIM : (h + 1) * HEAD_DIM] for h in range(first, first + GROUP_HEADS)], axis=0
+        )
+        return lax.dot_general(keys, tile, (((1,), (1,)), ((), ())), preferred_element_type=jnp.float32)
 
     def partial_max(piece):
         return jnp.max(piece.reshape(-1, 8, width), axis=0)
 
-    for h in range(heads):
-        at = slice(h * BLOCK, (h + 1) * BLOCK)
-        exact = queries[:, h * HEAD_DIM : (h + 1) * HEAD_DIM].astype(jnp.float32) * scale
-        high = exact.astype(jnp.bfloat16)
-        scaled[at, :HEAD_DIM] = high
-        scaled[at, HEAD_DIM:] = (exact - high.astype(jnp.float32)).astype(jnp.bfloat16)
     total[...] = jnp.zeros(total.shape, jnp.float32)
     peak[...] = jnp.full(peak.shape, -jnp.inf, jnp.float32)
     soft[1][...] = jnp.zeros(soft[1].shape, jnp.bfloat16)
@@ -153,7 +149,7 @@
     keys = keys_of(0)
     for g in range(2):
         raw[g][...] = score(keys, g)
-    level[...] = jnp.max(partial_max(raw[0][...]), axis=0, keepdims=True)
+    level[...] = jnp.max(partial_max(raw[0][...]), axis=0, keepdims=True) * scale
     peak[:, columns(0)] = level[...]
     fade[...] = jnp.zeros(fade.shape, jnp.float32)
     end = listed[2 * blocks, b]
@@ -175,7 +171,7 @@
             tops = None
             for cut in cuts:
                 raw[ahead][cut, :] = score(source[cut, :], ahead)
-                soft[g % 2][cut, :] = jnp.exp2(raw[g][cut, :] - new).astype(jnp.bfloat16)
+                soft[g % 2][cut, :] = jnp.exp2(raw[g][cut, :] * scale - new).astype(jnp.bfloat16)
                 total[:, into] += jnp.dot(
                     multiplier[:, cut], soft[(g + 1) % 2][cut, :], preferred_element_type=jnp.float32
                 )
@@ -183,7 +179,7 @@
                 tops = most if tops is None else jnp.maximum(tops, most)
             at = columns(upcoming)
             old = peak[:, at]
-            new = jnp.maximum(old, jnp.max(tops, axis=0, keepdims=True))
+            new = jnp.maximum(old, jnp.max(tops, axis=0, keepdims=True) * scale)
             peak[:, at] = new
             factor, late = jnp.exp2(old - new), factor
         level[...] = new
@@ -230,7 +226,6 @@
                 pltpu.VMEM((2, 16, BLOCK), jnp.bfloat16),
                 pltpu.VMEM((HEAD_DIM + 16, heads * BLOCK), jnp.float32),
                 pltpu.VMEM((1, heads * BLOCK), jnp.float32),
-                pltpu.VMEM((heads * BLOCK, 2 * HEAD_DIM), jnp.bfloat16),
             ]
             + [pltpu.VMEM((CHUNK * BLOCK, GROUP_HEADS * BLOCK), jnp.float32)] * (heads // GROUP_HEADS)
             + [pltpu.VMEM((CHUNK * BLOCK, GROUP_HEADS * BLOCK), jnp.bfloat16)] * 2
@@ -253,7 +248,9 @@
 
 def gather_shards(own):
     across = shift(own, "y_lo", 1)
-    here = [own, shift(own, "x", -1), None, shift(own, "x", 1)]
+    up, down = shift(own, "x", -1), shift(own, "x", 1)
+    across, up, down = lax.optimization_barrier((across, up, down))
+    here = [own, up, None, down]
     here[2] = shift(here[3], "x", 1)
     there = [across, shift(across, "x", -1), None, shift(across, "x", 1)]
     there[2] = shift(there[1], "x", -1)

time: 158 us -> 153 us (0.968); the launches traced: 158 us -> 151 us
  starting transfers between devices: 36.3 us -> 45.1 us
  waiting for transfers between devices: 21.6 us -> 14.5 us
  Pallas kernels: 57.7 us -> 51.6 us
  blocking collectives: 33.2 us -> 31 us
    ppermute x15, starting transfers between devices: 20.6 us -> 29.4 us  [shift(): lax.ppermute(array, axis, [(i, (i + step) % size) for i in range(size)])]
    ppermute x15, waiting for transfers between devices: 21.6 us -> 14.5 us  [shift(): lax.ppermute(array, axis, [(i, (i + step) % size) for i in range(size)])]
    pallas_call x1, Pallas kernels: 49.7 us -> 43.9 us  [attend(): pl.pallas_call(functools.partial(attend_kernel, heads=heads, shards=shard...]
    all_to_all x1, blocking collectives: 33.2 us -> 31 us  [local(): lax.all_to_all(attended.reshape(parts, tokens, -1), head_axes, split_axis...]
    unnamed x32 -> x28, local copies, waits for them, and re-layouts: 4.17 us -> 3.27 us
  transfers between devices with their start and end apart: 17 -> 17, of which waited for: 4 -> 7; matrix products, arithmetic and copies ran while one was open for 1% -> 1% of each run, Pallas kernels for 5% -> 5%
where the time goes in v2:
time: 153 us; the launch traced here: 151 us
  Pallas kernels  51.6 us (34%)
  starting transfers between devices  45.1 us (29%)
  blocking collectives  31 us (20%)
  waiting for transfers between devices  14.5 us (9%)
  local copies, waits for them, and re-layouts  6.74 us (4%)
    pallas_call x1, Pallas kernels, attend(): pl.pallas_call(functools.partial(attend_kernel, heads=heads, shards=shard...  43.9 us
    all_to_all x1, blocking collectives, local(): lax.all_to_all(attended.reshape(parts, tokens, -1), head_axes, split_axis...  31 us
    ppermute x15, starting transfers between devices, shift(): lax.ppermute(array, axis, [(i, (i + step) % size) for i in range(size)])  29.4 us
    all_to_all x2, starting transfers between devices, exchange(): lax.all_to_all(cut, head_axes, split_axis=0, concat_axis=0, tiled=True)  15.7 us
    ppermute x15, waiting for transfers between devices, shift(): lax.ppermute(array, axis, [(i, (i + step) % size) for i in range(size)])  14.5 us
    pallas_call x1, Pallas kernels, plan(): pl.pallas_call(functools.partial(plan_kernel, blocks=blocks, sizes=sizes,...  7.72 us
    unnamed x28, local copies, waits for them, and re-layouts  3.27 us
  transfers between devices with their start and end apart: 17, of which 7 were waited for; matrix products, arithmetic and copies ran while one was open for 1% of the time, Pallas kernels for 5%

profile of v2, /device:TPU:1, one launch (start us, length us, event | category | flops | bytes accessed | tf_op | source)
XLA Modules:
  0.0 150.7 jit_solution(11502442925792657208)
XLA Ops:
  0.0 1.3 copy.18
  1.3 1.1 copy.19
  2.6 0.9 pad_maximum_fusion
  3.4 8.5 %all-to-all-start = ((bf16[8,128,256]{1,2,0:T(8,128)(2,1)}), bf16[8,128,256]{1,2,0:T(8,128)(2,1)S(1)}, u32[]{:S(2)}, u32[]{:S(2)}) async-start(bf16[8,128,256]{1,2,0:T(8,128)(2,1)} %pad_maximum_fusion), calls=%async_computation | async-start | bytes 1048576 | tf_op jit(solution)/shard_map/all_to_all | solution.py:269
  11.9 1.6 %copy.27 = bf16[16,8,8,1024]{3,2,0,1:T(8,128)(2,1)} copy(bf16[16,8,8,1024]{3,2,1,0:T(8,128)(2,1)S(1)} %bitcast.41) | data formatting | bytes 4194304 | tf_op jit(solution)/shard_map/reshape | solution.py:273
  13.5 0.7 pad_add_fusion.place_ref
  14.2 7.7 %shard_map.55.listed = s32[17,132]{1,0:T(8,128)} custom-call(s32[3]{0:T(128)} %pad_add_fusion.place_ref, s32[16,16,16]{2,1,0:T(8,128)} %codes_ref.1, s32[16,16]{1,0:T(8,128)} %counts_ref.1), custom_call_target="tpu_custom_call" | custom-call | bytes 20000000 | tf_op jit(solution)/shard_map/pallas_call | solution.py:67
  22.5 2.5 %collective-permute-start.1 = (bf16[1024,256]{1,0:T(8,128)(2,1)S(1)}, bf16[1024,256]{1,0:T(8,128)(2,1)}, u32[]{:S(2)}, u32[]{:S(2)}) collective-permute-start(bf16[1024,256]{1,0:T(8,128)(2,1)S(1)} %bitcast.46), channel_id=1, source_target_pairs={{0,96},{32,0},{64,32},{96,64},{1,97},{33,1},{65,33},{97,65},{2,98}... | collective-permute-start | bytes 1572872 | tf_op jit(solution)/shard_map/ppermute | solution.py:246
  25.2 7.2 %all-to-all-start.1 = ((bf16[8,128,1024]{2,1,0:T(8,128)(2,1)}), bf16[8,128,1024]{2,1,0:T(8,128)(2,1)S(1)}, u32[]{:S(2)}, u32[]{:S(2)}) async-start(bf16[8,128,1024]{2,1,0:T(8,128)(2,1)} %bitcast.39), calls=%async_computation.1 | async-start | bytes 4194304 | tf_op jit(solution)/shard_map/all_to_all | solution.py:269
  32.5 2.6 %collective-permute-start.7 = (bf16[1024,256]{1,0:T(8,128)(2,1)S(1)}, bf16[1024,256]{1,0:T(8,128)(2,1)S(1)}, u32[]{:S(2)}, u32[]{:S(2)}) collective-permute-start(bf16[1024,256]{1,0:T(8,128)(2,1)S(1)} %bitcast.48), channel_id=1, source_target_pairs={{0,8},{8,0},{1,9},{9,1},{2,10},{10,2},{3,11},{11,3},{4,12},{12,4},... | collective-permute-start | bytes 1572872 | tf_op jit(solution)/shard_map/ppermute | solution.py:246
  35.8 1.5 collective-permute-start.4
  37.3 6.7 %collective-permute-start.8 = (bf16[1024,256]{1,0:T(8,128)(2,1)}, bf16[1024,256]{1,0:T(8,128)(2,1)S(1)}, u32[]{:S(2)}, u32[]{:S(2)}) collective-permute-start(bf16[1024,256]{1,0:T(8,128)(2,1)} %collective-permute-done.1), channel_id=1, source_target_pairs={{0,8},{8,0},{1,9},{9,1},{2,10},{10,2},{3,11},{11,3},{4,12},{12,4},... | collective-permute-start | bytes 1572872 | tf_op jit(solution)/shard_map/ppermute | solution.py:246
  44.8 2.7 %collective-permute-start.5 = (bf16[1024,256]{1,0:T(8,128)(2,1)S(1)}, bf16[1024,256]{1,0:T(8,128)(2,1)}, u32[]{:S(2)}, u32[]{:S(2)}) collective-permute-start(bf16[1024,256]{1,0:T(8,128)(2,1)S(1)} %collective-permute-done.4), channel_id=1, source_target_pairs={{0,96},{32,0},{64,32},{96,64},{1,97},{33,1},{65,33},{97,65},{2,98}... | collective-permute-start | bytes 1572872 | tf_op jit(solution)/shard_map/ppermute | solution.py:246
  47.5 9.6 %collective-permute-start.11 = (bf16[1024,256]{1,0:T(8,128)(2,1)}, bf16[1024,256]{1,0:T(8,128)(2,1)S(1)}, u32[]{:S(2)}, u32[]{:S(2)}) collective-permute-start(bf16[1024,256]{1,0:T(8,128)(2,1)} %collective-permute-done), channel_id=1, source_target_pairs={{0,8},{8,0},{1,9},{9,1},{2,10},{10,2},{3,11},{11,3},{4,12},{12,4},... | collective-permute-start | bytes 1572872 | tf_op jit(solution)/shard_map/ppermute | solution.py:246
  57.1 1.7 %collective-permute-done.3 = bf16[1024,256]{1,0:T(8,128)(2,1)S(1)} collective-permute-done((bf16[1024,256]{1,0:T(8,128)(2,1)S(1)}, bf16[1024,256]{1,0:T(8,128)(2,1)S(1)}, u32[]{:S(2)}, u32[]{:S(2)}) %collective-permute-start.3) | collective-permute-done | bytes 524320 | tf_op jit(solution)/shard_map/ppermute | solution.py:246
  58.8 1.2 collective-permute-start.9
  60.0 10.1 %collective-permute-done.6 = bf16[1024,256]{1,0:T(8,128)(2,1)S(1)} collective-permute-done((bf16[1024,256]{1,0:T(8,128)(2,1)}, bf16[1024,256]{1,0:T(8,128)(2,1)S(1)}, u32[]{:S(2)}, u32[]{:S(2)}) %collective-permute-start.6) | collective-permute-done | bytes 524320 | tf_op jit(solution)/shard_map/ppermute | solution.py:246
  70.0 0.8 collective-permute-start.14
  71.4 1.0 collective-permute-done.14
  72.4 0.8 copy-done.12
  73.3 0.7 collective-permute-done.12
  74.2 43.9 %shard_map.56 = bf16[1024,1024]{1,0:T(8,128)(2,1)S(1)} custom-call(s32[17,132]{1,0:T(8,128)S(1)} %copy-done, bf16[1024,1024]{1,0:T(8,128)(2,1)S(1)} %bitcast.37, bf16[8,128,256]{2,1,0:T(8,128)(2,1)} %copy-done.2, bf16[8,128,256]{2,1,0:T(8,128)(2,1)} %bitcast.11.refs_1_, bf16[8,128,256]{2,1,0:T(8,128)(2,1)} %bitcast.53, bf16[8,128,256]{2,1,0:T(8,128)(2,1)} %bitcast.49, ...), custom_call_target="tpu_custom_call" | custom-call | flops 36238786560 | bytes 12000000 | tf_op jit(solution)/shard_map/pallas_call | solution.py:216
  118.2 31.0 %all_to_all.15 = bf16[8,128,1024]{2,1,0:T(8,128)(2,1)S(1)} all-to-all(bf16[8,128,1024]{2,1,0:T(8,128)(2,1)S(1)} %bitcast.38), channel_id=1, replica_groups=mesh['x'=4,'y_lo'=2,'core'=2,'y_hi'=2,'z'=4] {'y_hi','z'}, dimensions={0} | all-to-all | bytes 4194304 | tf_op jit(solution)/shard_map/all_to_all | solution.py:283
  149.2 1.5 copy.25
  (47 shorter events, 3.3 us)
Async XLA Ops:
  0.0 11.9 %copy-start.1 = (bf16[128,8192]{1,0:T(8,128)(2,1)S(1)}, bf16[128,8192]{1,0:T(8,128)(2,1)}, u32[]{:S(2)}) copy-start(bf16[128,8192]{1,0:T(8,128)(2,1)} %param.5) | copy-start | bytes 6291460
  3.4 18.5 %all-to-all-start = ((bf16[8,128,256]{1,2,0:T(8,128)(2,1)}), bf16[8,128,256]{1,2,0:T(8,128)(2,1)S(1)}, u32[]{:S(2)}, u32[]{:S(2)}) async-start(bf16[8,128,256]{1,2,0:T(8,128)(2,1)} %pad_maximum_fusion), calls=%async_computation | async-start | bytes 1048576 | tf_op jit(solution)/shard_map/all_to_all | solution.py:269
  22.2 52.1 %copy-start = (s32[17,132]{1,0:T(8,128)S(1)}, s32[17,132]{1,0:T(8,128)}, u32[]{:S(2)}) copy-start(s32[17,132]{1,0:T(8,128)} %shard_map.55.listed) | copy-start | bytes 26932
  22.2 12.9 %collective-permute-start.2 = (bf16[1024,256]{1,0:T(8,128)(2,1)S(1)}, bf16[1024,256]{1,0:T(8,128)(2,1)S(1)}, u32[]{:S(2)}, u32[]{:S(2)}) collective-permute-start(bf16[1024,256]{1,0:T(8,128)(2,1)S(1)} %bitcast.45), channel_id=1, source_target_pairs={{0,32},{32,64},{64,96},{96,0},{1,33},{33,65},{65,97},{97,1},{2,34}... | collective-permute-start | bytes 1572872 | tf_op jit(solution)/shard_map/ppermute | solution.py:246
  22.5 12.9 %collective-permute-start.1 = (bf16[1024,256]{1,0:T(8,128)(2,1)S(1)}, bf16[1024,256]{1,0:T(8,128)(2,1)}, u32[]{:S(2)}, u32[]{:S(2)}) collective-permute-start(bf16[1024,256]{1,0:T(8,128)(2,1)S(1)} %bitcast.46), channel_id=1, source_target_pairs={{0,96},{32,0},{64,32},{96,64},{1,97},{33,1},{65,33},{97,65},{2,98}... | collective-permute-start | bytes 1572872 | tf_op jit(solution)/shard_map/ppermute | solution.py:246
  24.9 10.9 %collective-permute-start = (bf16[1024,256]{1,0:T(8,128)(2,1)S(1)}, bf16[1024,256]{1,0:T(8,128)(2,1)}, u32[]{:S(2)}, u32[]{:S(2)}) collective-permute-start(bf16[1024,256]{1,0:T(8,128)(2,1)S(1)} %bitcast.47), channel_id=1, source_target_pairs={{0,16},{16,0},{1,17},{17,1},{2,18},{18,2},{3,19},{19,3},{4,20},{20... | collective-permute-start | bytes 1572872 | tf_op jit(solution)/shard_map/ppermute | solution.py:246
  25.2 48.8 %all-to-all-start.1 = ((bf16[8,128,1024]{2,1,0:T(8,128)(2,1)}), bf16[8,128,1024]{2,1,0:T(8,128)(2,1)S(1)}, u32[]{:S(2)}, u32[]{:S(2)}) async-start(bf16[8,128,1024]{2,1,0:T(8,128)(2,1)} %bitcast.39), calls=%async_computation.1 | async-start | bytes 4194304 | tf_op jit(solution)/shard_map/all_to_all | solution.py:269
  32.5 11.8 %collective-permute-start.7 = (bf16[1024,256]{1,0:T(8,128)(2,1)S(1)}, bf16[1024,256]{1,0:T(8,128)(2,1)S(1)}, u32[]{:S(2)}, u32[]{:S(2)}) collective-permute-start(bf16[1024,256]{1,0:T(8,128)(2,1)S(1)} %bitcast.48), channel_id=1, source_target_pairs={{0,8},{8,0},{1,9},{9,1},{2,10},{10,2},{3,11},{11,3},{4,12},{12,4},... | collective-permute-start | bytes 1572872 | tf_op jit(solution)/shard_map/ppermute | solution.py:246
  35.1 39.1 %copy-start.3 = (bf16[1024,256]{1,0:T(8,128)(2,1)}, bf16[1024,256]{1,0:T(8,128)(2,1)S(1)}, u32[]{:S(2)}) copy-start(bf16[1024,256]{1,0:T(8,128)(2,1)S(1)} %collective-permute-done.2) | copy-start | bytes 1572868
  35.8 9.0 %collective-permute-start.4 = (bf16[1024,256]{1,0:T(8,128)(2,1)}, bf16[1024,256]{1,0:T(8,128)(2,1)S(1)}, u32[]{:S(2)}, u32[]{:S(2)}) collective-permute-start(bf16[1024,256]{1,0:T(8,128)(2,1)} %collective-permute-done), channel_id=1, source_target_pairs={{0,96},{32,0},{64,32},{96,64},{1,97},{33,1},{65,33},{97,65},{2,98}... | collective-permute-start | bytes 1572872 | tf_op jit(solution)/shard_map/ppermute | solution.py:246
  37.3 10.2 %collective-permute-start.8 = (bf16[1024,256]{1,0:T(8,128)(2,1)}, bf16[1024,256]{1,0:T(8,128)(2,1)S(1)}, u32[]{:S(2)}, u32[]{:S(2)}) collective-permute-start(bf16[1024,256]{1,0:T(8,128)(2,1)} %collective-permute-done.1), channel_id=1, source_target_pairs={{0,8},{8,0},{1,9},{9,1},{2,10},{10,2},{3,11},{11,3},{4,12},{12,4},... | collective-permute-start | bytes 1572872 | tf_op jit(solution)/shard_map/ppermute | solution.py:246
  44.0 14.8 %collective-permute-start.3 = (bf16[1024,256]{1,0:T(8,128)(2,1)S(1)}, bf16[1024,256]{1,0:T(8,128)(2,1)S(1)}, u32[]{:S(2)}, u32[]{:S(2)}) collective-permute-start(bf16[1024,256]{1,0:T(8,128)(2,1)S(1)} %collective-permute-done.2), channel_id=1, source_target_pairs={{0,32},{32,64},{64,96},{96,0},{1,33},{33,65},{65,97},{97,1},{2,34}... | collective-permute-start | bytes 1572872 | tf_op jit(solution)/shard_map/ppermute | solution.py:246
  44.2 25.8 %collective-permute-start.6 = (bf16[1024,256]{1,0:T(8,128)(2,1)}, bf16[1024,256]{1,0:T(8,128)(2,1)S(1)}, u32[]{:S(2)}, u32[]{:S(2)}) collective-permute-start(bf16[1024,256]{1,0:T(8,128)(2,1)} %collective-permute-done), channel_id=1, source_target_pairs={{0,32},{32,64},{64,96},{96,0},{1,33},{33,65},{65,97},{97,1},{2,34}... | collective-permute-start | bytes 1572872 | tf_op jit(solution)/shard_map/ppermute | solution.py:246
  44.3 28.1 %copy-start.4 = (bf16[1024,256]{1,0:T(8,128)(2,1)}, bf16[1024,256]{1,0:T(8,128)(2,1)S(1)}, u32[]{:S(2)}) copy-start(bf16[1024,256]{1,0:T(8,128)(2,1)S(1)} %collective-permute-done.7) | copy-start | bytes 1572868
  44.3 26.6 %collective-permute-start.10 = (bf16[1024,256]{1,0:T(8,128)(2,1)S(1)}, bf16[1024,256]{1,0:T(8,128)(2,1)S(1)}, u32[]{:S(2)}, u32[]{:S(2)}) collective-permute-start(bf16[1024,256]{1,0:T(8,128)(2,1)S(1)} %collective-permute-done.2), channel_id=1, source_target_pairs={{0,8},{8,0},{1,9},{9,1},{2,10},{10,2},{3,11},{11,3},{4,12},{12,4},... | collective-permute-start | bytes 1572872 | tf_op jit(solution)/shard_map/ppermute | solution.py:246
  44.8 27.6 %copy-start.5 = (bf16[1024,256]{1,0:T(8,128)(2,1)}, bf16[1024,256]{1,0:T(8,128)(2,1)S(1)}, u32[]{:S(2)}) copy-start(bf16[1024,256]{1,0:T(8,128)(2,1)S(1)} %collective-permute-done.4) | copy-start | bytes 1572868
  44.8 26.1 %collective-permute-start.5 = (bf16[1024,256]{1,0:T(8,128)(2,1)S(1)}, bf16[1024,256]{1,0:T(8,128)(2,1)}, u32[]{:S(2)}, u32[]{:S(2)}) collective-permute-start(bf16[1024,256]{1,0:T(8,128)(2,1)S(1)} %collective-permute-done.4), channel_id=1, source_target_pairs={{0,96},{32,0},{64,32},{96,64},{1,97},{33,1},{65,33},{97,65},{2,98}... | collective-permute-start | bytes 1572872 | tf_op jit(solution)/shard_map/ppermute | solution.py:246
  47.5 24.9 %copy-start.6 = (bf16[1024,256]{1,0:T(8,128)(2,1)}, bf16[1024,256]{1,0:T(8,128)(2,1)S(1)}, u32[]{:S(2)}) copy-start(bf16[1024,256]{1,0:T(8,128)(2,1)S(1)} %collective-permute-done.8) | copy-start | bytes 1572868
  47.5 23.9 %collective-permute-start.11 = (bf16[1024,256]{1,0:T(8,128)(2,1)}, bf16[1024,256]{1,0:T(8,128)(2,1)S(1)}, u32[]{:S(2)}, u32[]{:S(2)}) collective-permute-start(bf16[1024,256]{1,0:T(8,128)(2,1)} %collective-permute-done), channel_id=1, source_target_pairs={{0,8},{8,0},{1,9},{9,1},{2,10},{10,2},{3,11},{11,3},{4,12},{12,4},... | collective-permute-start | bytes 1572872 | tf_op jit(solution)/shard_map/ppermute | solution.py:246
  58.8 13.6 %copy-start.7 = (bf16[1024,256]{1,0:T(8,128)(2,1)}, bf16[1024,256]{1,0:T(8,128)(2,1)S(1)}, u32[]{:S(2)}) copy-start(bf16[1024,256]{1,0:T(8,128)(2,1)S(1)} %collective-permute-done.3) | copy-start | bytes 1572868
  58.8 12.5 %collective-permute-start.9 = (bf16[1024,256]{1,0:T(8,128)(2,1)S(1)}, bf16[1024,256]{1,0:T(8,128)(2,1)S(1)}, u32[]{:S(2)}, u32[]{:S(2)}) collective-permute-start(bf16[1024,256]{1,0:T(8,128)(2,1)S(1)} %collective-permute-done.3), channel_id=1, source_target_pairs={{0,8},{8,0},{1,9},{9,1},{2,10},{10,2},{3,11},{11,3},{4,12},{12,4},... | collective-permute-start | bytes 1572872 | tf_op jit(solution)/shard_map/ppermute | solution.py:246
  70.0 2.3 %collective-permute-start.14 = (bf16[1024,256]{1,0:T(8,128)(2,1)S(1)}, bf16[1024,256]{1,0:T(8,128)(2,1)S(1)}, u32[]{:S(2)}, u32[]{:S(2)}) collective-permute-start(bf16[1024,256]{1,0:T(8,128)(2,1)S(1)} %collective-permute-done.6), channel_id=1, source_target_pairs={{0,8},{8,0},{1,9},{9,1},{2,10},{10,2},{3,11},{11,3},{4,12},{12,4},... | collective-permute-start | bytes 1572872 | tf_op jit(solution)/shard_map/ppermute | solution.py:246
  70.8 3.2 %collective-permute-start.12 = (bf16[1024,256]{1,0:T(8,128)(2,1)S(1)}, bf16[1024,256]{1,0:T(8,128)(2,1)}, u32[]{:S(2)}, u32[]{:S(2)}) collective-permute-start(bf16[1024,256]{1,0:T(8,128)(2,1)S(1)} %collective-permute-done.4), channel_id=1, source_target_pairs={{0,8},{8,0},{1,9},{9,1},{2,10},{10,2},{3,11},{11,3},{4,12},{12,4},... | collective-permute-start | bytes 1572872 | tf_op jit(solution)/shard_map/ppermute | solution.py:246
  70.9 3.3 %collective-permute-start.13 = (bf16[1024,256]{1,0:T(8,128)(2,1)}, bf16[1024,256]{1,0:T(8,128)(2,1)}, u32[]{:S(2)}, u32[]{:S(2)}) collective-permute-start(bf16[1024,256]{1,0:T(8,128)(2,1)} %collective-permute-done.5), channel_id=1, source_target_pairs={{0,8},{8,0},{1,9},{9,1},{2,10},{10,2},{3,11},{11,3},{4,12},{12,4},... | collective-permute-start | bytes 1572872 | tf_op jit(solution)/shard_map/ppermute | solution.py:246
  (6 other events, 19.0 us)

commit v3 on v2

v3 whole, which is shorter than its diff:
```python
import functools

import jax
import jax.numpy as jnp
from jax import lax
from jax.experimental import pallas as pl
from jax.experimental.pallas import tpu as pltpu
from jax.sharding import Mesh
from jax.sharding import PartitionSpec as P

HEADS = 64
KV_HEADS = 8
HEAD_DIM = 128
BLOCK = 128
LOG2E = 1.4426950408889634
CHUNK = 4
GROUP_HEADS = 2
PIECE = 512
WAVE = 8
FIRST_STEPS = 5


def plan_kernel(place_ref, codes_ref, counts_ref, list_ref, fill_ref, *, blocks, sizes, zero, far):
    x_size, y_lo_size, core_size = sizes[:3]
    x, y, core = place_ref[0], place_ref[1], place_ref[2]
    shard = (x * y_lo_size + y) * core_size + core
    for a in range(blocks):
        list_ref[a, 0] = a
        list_ref[blocks + a, 0] = a
        fill_ref[a] = 1

    y_hi, z = place_ref[3], place_ref[4]
    y_size, z_size = sizes[3:]
    for step, (dy, dz) in enumerate(far):
        for row, sign in ((1, 1), (2, -1)):
            to_y = lax.rem(y_hi + sign * dy + y_size, y_size)
            to_z = lax.rem(z + sign * dz + z_size, z_size)
            list_ref[2 * blocks + row, step] = to_y * z_size + to_z

    def visit_shard(slot, _):
        from_x = lax.rem(x + lax.rem(slot, x_size), x_size)
        from_y = lax.rem(y + lax.rem(lax.div(slot, x_size), y_lo_size), y_lo_size)
        from_core = lax.rem(core + lax.div(slot, x_size * y_lo_size), core_size)
        j = (from_x * y_lo_size + from_y) * core_size + from_core

        def visit_entry(c, _):
            code = codes_ref[shard, j, c]
            a = lax.div(code, blocks)
            block = slot * blocks + lax.rem(code, blocks)
            at = fill_ref[a]
            list_ref[a, at] = block
            list_ref[blocks + a, at] = block
            fill_ref[a] = at + 1
            return 0

        return lax.fori_loop(0, counts_ref[shard, j], visit_entry, 0)

    lax.fori_loop(0, x_size * y_lo_size * core_size, visit_shard, 0)
    for a in range(blocks):
        filled = fill_ref[a]
        chunks = lax.div(filled + CHUNK - 1, CHUNK)
        list_ref[2 * blocks, a] = chunks

        def pad(at, _):
            list_ref[a, at] = a
            list_ref[blocks + a, at] = zero
            return 0

        lax.fori_loop(filled, chunks * CHUNK, pad, 0)


def plan(place, live_keys, live_count, blocks, sizes, zero, far):
    shards = live_keys.shape[0]
    width = -(-(shards * blocks + 1) // CHUNK) * CHUNK
    smem = pl.BlockSpec(memory_space=pltpu.SMEM)
    return pl.pallas_call(
        functools.partial(plan_kernel, blocks=blocks, sizes=sizes, zero=zero, far=far),
        in_specs=[smem] * 3,
        out_specs=smem,
        out_shape=jax.ShapeDtypeStruct((2 * blocks + 3, width), jnp.int32),
        scratch_shapes=[pltpu.SMEM((blocks,), jnp.int32)],
        cost_estimate=pl.CostEstimate(flops=0, bytes_accessed=20_000_000, transcendentals=0),
    )(place, live_keys, live_count)


def attend_kernel(listed, queries, *refs, blocks, steps, heads, shards, loads):
    if loads:
        pieces, (out, pairs, *rest) = refs[:shards], refs[shards:]
    else:
        pairs, out, *rest = refs
    ones, total, peak, *rest = rest
    groups = heads // GROUP_HEADS
    raw, soft, (level, fade, late_fade, *loading) = rest[:groups], rest[groups : groups + 2], rest[groups + 2 :]
    count = pairs.shape[0] - 1
    span = count // shards
    width = GROUP_HEADS * BLOCK
    scale = HEAD_DIM**-0.5 * LOG2E
    cuts = [slice(j * PIECE, (j + 1) * PIECE) for j in range(CHUNK * BLOCK // PIECE)]
    square = (BLOCK, BLOCK)
    unit = (
        lax.broadcasted_iota(jnp.int32, square, 0) == lax.broadcasted_iota(jnp.int32, square, 1)
    ).astype(jnp.bfloat16)

    def block_of(step):
        return listed[2 * blocks + 1, step]

    def arrival(j):
        return pltpu.make_async_copy(pieces[j], pairs.at[pl.ds(j * span, span)], loading[1].at[j])

    def arrive(b, i):
        ready = loading[0]
        last = lax.div(listed[b, i * CHUNK + CHUNK - 1], span) + 1
        needed = jnp.where(i >= listed[2 * blocks, b] - 1, shards, last)
        for j in range(shards):

            @pl.when((j >= ready[0]) & (j < needed))
            def _():
                arrival(j).wait()
                if j + WAVE < shards:
                    arrival(j + WAVE).start()

        ready[0] = jnp.maximum(ready[0], needed)

    def rows_of(b):
        return pl.ds(pl.multiple_of(b * BLOCK, BLOCK), BLOCK)

    def columns(g):
        return slice(g * width, (g + 1) * width)

    def keys_of(b, i):
        return jnp.concatenate([pairs[listed[b, i * CHUNK + c], :, :HEAD_DIM] for c in range(CHUNK)], axis=0)

    def values_of(b, i):
        slots = [listed[blocks + b, i * CHUNK + c] for c in range(CHUNK)]
        return jnp.concatenate(
            [
                jnp.concatenate([pairs[s, :, HEAD_DIM:] for s in slots], axis=1),
                jnp.concatenate([ones[(s == count).astype(jnp.int32)] for s in slots], axis=1),
            ],
            axis=0,
        )

    def score(b, keys, g):
        first = g * GROUP_HEADS
        tile = jnp.concatenate(
            [
                queries[rows_of(b), h * HEAD_DIM : (h + 1) * HEAD_DIM]
                for h in range(first, first + GROUP_HEADS)
            ],
            axis=0,
        )
        return lax.dot_general(keys, tile, (((1,), (1,)), ((), ())), preferred_element_type=jnp.float32)

    def partial_max(piece):
        return jnp.max(piece.reshape(-1, 8, width), axis=0)

    def first_scores(b):
        keys = keys_of(b, 0)
        for g in range(2):
            raw[g][...] = score(b, keys, g)

    def reset():
        total[...] = jnp.zeros(total.shape, jnp.float32)
        peak[...] = jnp.full(peak.shape, -jnp.inf, jnp.float32)
        soft[1][...] = jnp.zeros(soft[1].shape, jnp.bfloat16)
        late_fade[...] = jnp.ones(late_fade.shape, jnp.float32)
        level[...] = jnp.max(partial_max(raw[0][...]), axis=0, keepdims=True) * scale
        peak[:, columns(0)] = level[...]
        fade[...] = jnp.zeros(fade.shape, jnp.float32)

    ones[0] = jnp.ones(ones.shape[1:], jnp.bfloat16)
    ones[1] = jnp.zeros(ones.shape[1:], jnp.bfloat16)
    if loads:
        for j in range(WAVE):
            arrival(j).start()
        loading[0][0] = 0
        pairs[count] = jnp.zeros(pairs.shape[1:], jnp.bfloat16)
        arrive(block_of(steps[0]), 0)
    first_scores(block_of(steps[0]))
    reset()

    def visit_block(step, _):
        b = block_of(step)
        end = listed[2 * blocks, b]

        def visit(i, _):
            following = jnp.minimum(i + 1, end - 1)

            if loads:

                @pl.when(step == steps[0])
                def _():
                    arrive(b, following)

            keys = keys_of(b, i)
            next_keys = keys_of(b, following)
            values = values_of(b, i)
            before = values_of(b, jnp.maximum(i - 1, 0))
            new, factor, late = level[...], fade[...], late_fade[...]
            for g in range(groups):
                ahead, upcoming, done = (g + 2) % groups, (g + 1) % groups, (g - 1) % groups
                source = keys if g + 2 < groups else next_keys
                multiplier = values if g else before
                into = columns(done)
                total[:, into] = total[:, into] * late
                tops = None
                for cut in cuts:
                    raw[ahead][cut, :] = score(b, source[cut, :], ahead)
                    soft[g % 2][cut, :] = jnp.exp2(raw[g][cut, :] * scale - new).astype(jnp.bfloat16)
                    total[:, into] += jnp.dot(
                        multiplier[:, cut], soft[(g + 1) % 2][cut, :], preferred_element_type=jnp.float32
                    )
                    most = partial_max(raw[upcoming][cut, :])
                    tops = most if tops is None else jnp.maximum(tops, most)
                at = columns(upcoming)
                old = peak[:, at]
                new = jnp.maximum(old, jnp.max(tops, axis=0, keepdims=True) * scale)
                peak[:, at] = new
                factor, late = jnp.exp2(old - new), factor
            level[...] = new
            fade[...] = factor
            late_fade[...] = late
            return 0

        lax.fori_loop(0, end, visit, 0)
        at = columns(groups - 1)
        total[:, at] = total[:, at] * late_fade[...] + jnp.dot(
            values_of(b, end - 1), soft[1][...], preferred_element_type=jnp.float32
        )
        first_scores(block_of(jnp.minimum(step + 1, steps[1] - 1)))
        for h in range(heads):
            at = slice(h * BLOCK, (h + 1) * BLOCK)
            inverse = 1.0 / total[HEAD_DIM : HEAD_DIM + 1, at]
            normed = (total[:HEAD_DIM, at] * inverse).astype(jnp.bfloat16)
            turned = lax.dot_general(
                unit, normed, (((1,), (1,)), ((), ())), preferred_element_type=jnp.float32
            )
            out[rows_of(step - steps[0]), h * HEAD_DIM : (h + 1) * HEAD_DIM] = turned.astype(jnp.bfloat16)
        reset()
        return 0

    lax.fori_loop(*steps, visit_block, 0)


def attend(queries, sources, lists, steps):
    rows, width = queries.shape
    heads = width // HEAD_DIM
    blocks = rows // BLOCK
    loads = isinstance(sources, list)
    pair_estimate = 22 * (steps[1] - steps[0]) * 2 * 2 * heads * BLOCK * BLOCK * HEAD_DIM
    vmem = pl.BlockSpec(memory_space=pltpu.VMEM)
    out_specs, out_shape = [vmem], [jax.ShapeDtypeStruct(((steps[1] - steps[0]) * BLOCK, width), jnp.bfloat16)]
    if loads:
        shards = len(sources)
        span = sources[0].shape[0] // BLOCK
        count = shards * span
        sources = [
            pltpu.with_memory_space_constraint(piece.reshape(span, BLOCK, -1), pltpu.HBM) for piece in sources
        ]
        in_specs = [pl.BlockSpec(memory_space=pl.ANY)] * shards
        loading = [pltpu.SMEM((1,), jnp.int32), pltpu.SemaphoreType.DMA((shards,))]
        out_specs.append(vmem)
        out_shape.append(jax.ShapeDtypeStruct((count + 1, BLOCK, 2 * HEAD_DIM), jnp.bfloat16))
    else:
        shards = (sources.shape[0] - 1) // blocks
        sources, in_specs, loading = [sources], [vmem], []
    return pl.pallas_call(
        functools.partial(
            attend_kernel, blocks=blocks, steps=steps, heads=heads, shards=shards, loads=loads
        ),
        in_specs=[pl.BlockSpec(memory_space=pltpu.SMEM), vmem, *in_specs],
        out_specs=out_specs,
        scratch_shapes=[
            pltpu.VMEM((2, 16, BLOCK), jnp.bfloat16),
            pltpu.VMEM((HEAD_DIM + 16, heads * BLOCK), jnp.float32),
            pltpu.VMEM((1, heads * BLOCK), jnp.float32),
        ]
        + [pltpu.VMEM((CHUNK * BLOCK, GROUP_HEADS * BLOCK), jnp.float32)] * (heads // GROUP_HEADS)
        + [pltpu.VMEM((CHUNK * BLOCK, GROUP_HEADS * BLOCK), jnp.bfloat16)] * 2
        + [pltpu.VMEM((1, GROUP_HEADS * BLOCK), jnp.float32)] * 3
        + loading,
        out_shape=out_shape,
        compiler_params=pltpu.CompilerParams(vmem_limit_bytes=32 * 1024 * 1024),
        cost_estimate=pl.CostEstimate(flops=pair_estimate * 3, bytes_accessed=6_000_000, transcendentals=0),
    )(lists, queries, *sources)


def assemble_kernel(listed, *refs):
    *parts, out, sem = refs
    width = parts[0].shape[1]
    copies = [
        pltpu.make_async_copy(
            part, out.at[:, pl.ds(pl.multiple_of(listed[2 * len(parts) + 2, r] * width, width), width)], sem.at[r]
        )
        for r, part in enumerate(parts)
    ]
    for copy in copies:
        copy.start()
    for copy in copies:
        copy.wait()


def assemble(lists, parts):
    rows, width = parts[0].shape
    return pl.pallas_call(
        assemble_kernel,
        in_specs=[pl.BlockSpec(memory_space=pltpu.SMEM)] + [pl.BlockSpec(memory_space=pltpu.VMEM)] * len(parts),
        out_specs=pl.BlockSpec(memory_space=pl.ANY),
        out_shape=jax.ShapeDtypeStruct((rows, width * len(parts)), parts[0].dtype),
        scratch_shapes=[pltpu.SemaphoreType.DMA((len(parts),))],
    )(lists, *parts)


def shift(array, axis, step):
    size = lax.axis_size(axis)
    return lax.ppermute(array, axis, [(i, (i + step) % size) for i in range(size)])


def gather_shards(own):
    across = shift(own, "y_lo", 1)
    up, down = shift(own, "x", -1), shift(own, "x", 1)
    across, up, down = lax.optimization_barrier((across, up, down))
    here = [own, up, None, down]
    here[2] = shift(here[3], "x", 1)
    there = [across, shift(across, "x", -1), None, shift(across, "x", 1)]
    there[2] = shift(there[1], "x", -1)
    near = here + there
    return near + [shift(piece, "core", 1) for piece in near]


def local(queries, keys, values, live_keys, live_count):
    head_axes, blk_axes = ("y_hi", "z"), ("x", "y_lo", "core")
    parts = lax.axis_size(head_axes)
    tokens = queries.shape[0]
    sizes = tuple(lax.axis_size(axis) for axis in blk_axes + head_axes)
    blocks = parts * tokens // BLOCK

    def exchange(cut):
        moved = lax.all_to_all(cut, head_axes, split_axis=0, concat_axis=0, tiled=True)
        return moved.reshape(parts * tokens, -1)

    def cut(array):
        return array.reshape(tokens, parts, -1)

    own = exchange(
        jnp.concatenate([cut(keys).transpose(1, 0, 2), cut(values).transpose(1, 2, 0)], axis=2)
    )
    y_size, z_size = (lax.axis_size(axis) for axis in head_axes)
    far = [(dy, dz) for dy in range(y_size) for dz in range(z_size)]
    far.sort(key=lambda d: (d[0] + min(d[1], z_size - d[1]), d[0]), reverse=True)

    def at_distance(y, z, dy, dz):
        return (y + dy) % y_size * z_size + (z + dz) % z_size

    place = jnp.stack([lax.axis_index(axis) for axis in blk_axes + head_axes]).astype(jnp.int32)
    lists = plan(place, live_keys, live_count, blocks, sizes, live_keys.shape[0] * blocks, far)
    own, lists, query_parts = lax.optimization_barrier((own, lists, cut(queries).transpose(1, 0, 2)))
    pieces = gather_shards(own)
    query_local = exchange(query_parts)

    def send(attended, steps):
        sent = []
        for step in range(*steps):
            part = attended[(step - steps[0]) * tokens : (step - steps[0] + 1) * tokens]
            if any(far[step]):
                pairs = [
                    (k, at_distance(k // z_size, k % z_size, *far[step])) for k in range(y_size * z_size)
                ]
                part = lax.ppermute(part, head_axes, pairs)
            sent.append(part)
        return sent

    early, late = (0, FIRST_STEPS), (FIRST_STEPS, parts)
    attended, gathered = attend(query_local, pieces, lists, early)
    received = send(attended, early)
    (attended,) = attend(query_local, gathered, lists, late)
    received += send(attended, late)
    return assemble(lists, received)


def solution(mesh):
    fine = Mesh(mesh.devices.reshape(4, 2, 2, 2, 4), ("x", "y_lo", "core", "y_hi", "z"))
    rows = P(("x", "y_lo", "core", "y_hi", "z"), None)
    return jax.shard_map(
        local,
        mesh=fine,
        in_specs=(rows, rows, rows, P(), P()),
        out_specs=rows,
        check_vma=False,
    )
```

time: 153 us -> 154 us (level)
  the two profiles are of different devices: /device:TPU:1 before, /device:TPU:22 now
where the time goes in v3:
time: 154 us; the launch traced here: 153 us
  waiting for transfers between devices  53.2 us (35%)
  Pallas kernels  50.7 us (33%)
  starting transfers between devices  40.5 us (26%)
  local copies, waits for them, and re-layouts  7.4 us (5%)
    pallas_call x2, Pallas kernels, attend(): pl.pallas_call(functools.partial(attend_kernel, blocks=blocks, steps=step...  40.6 us
    ppermute x15, waiting for transfers between devices, shift(): lax.ppermute(array, axis, [(i, (i + step) % size) for i in range(size)])  31.6 us
    ppermute x7, waiting for transfers between devices, send(): part = lax.ppermute(part, head_axes, pairs)  21.6 us
    ppermute x7, starting transfers between devices, send(): part = lax.ppermute(part, head_axes, pairs)  17.4 us
    all_to_all x2, starting transfers between devices, exchange(): lax.all_to_all(cut, head_axes, split_axis=0, concat_axis=0, tiled=True)  15.5 us
    ppermute x15, starting transfers between devices, shift(): lax.ppermute(array, axis, [(i, (i + step) % size) for i in range(size)])  7.57 us
    pallas_call x1, Pallas kernels, plan(): pl.pallas_call(functools.partial(plan_kernel, blocks=blocks, sizes=sizes,...  7.26 us
    unnamed x42, local copies, waits for them, and re-layouts  3.94 us
  transfers between devices with their start and end apart: 24, of which 11 were waited for; matrix products, arithmetic and copies ran while one was open for 1% of the time, Pallas kernels for 5%

profile of v3, /device:TPU:22, one launch (start us, length us, event | category | flops | bytes accessed | tf_op | source)
XLA Modules:
  0.0 152.9 jit_solution(8825392310886320905)
XLA Ops:
  0.0 1.3 copy.15
  3.4 8.3 %all-to-all-start = ((bf16[8,128,256]{1,2,0:T(8,128)(2,1)}), bf16[8,128,256]{1,2,0:T(8,128)(2,1)S(1)}, u32[]{:S(2)}, u32[]{:S(2)}) async-start(bf16[8,128,256]{1,2,0:T(8,128)(2,1)} %pad_maximum_fusion), calls=%async_computation | async-start | bytes 1048576 | tf_op jit(solution)/shard_map/all_to_all | solution.py:339
  11.7 1.6 %copy.22 = bf16[16,8,8,1024]{3,2,0,1:T(8,128)(2,1)} copy(bf16[16,8,8,1024]{3,2,1,0:T(8,128)(2,1)S(1)} %bitcast.38) | data formatting | bytes 4194304 | tf_op jit(solution)/shard_map/reshape | solution.py:343
  13.9 7.3 %shard_map.55.listed = s32[19,132]{1,0:T(8,128)} custom-call(s32[5]{0:T(128)} %stack.23.place_ref, s32[16,16,16]{2,1,0:T(8,128)} %codes_ref.1, s32[16,16]{1,0:T(8,128)} %counts_ref.1), custom_call_target="tpu_custom_call" | custom-call | bytes 20000000 | tf_op jit(solution)/shard_map/pallas_call | solution.py:76
  21.6 1.9 %collective-permute-start.1 = (bf16[1024,256]{1,0:T(8,128)(2,1)S(1)}, bf16[1024,256]{1,0:T(8,128)(2,1)}, u32[]{:S(2)}, u32[]{:S(2)}) collective-permute-start(bf16[1024,256]{1,0:T(8,128)(2,1)S(1)} %bitcast.43), channel_id=1, source_target_pairs={{0,96},{32,0},{64,32},{96,64},{1,97},{33,1},{65,33},{97,65},{2,98}... | collective-permute-start | bytes 1572872 | tf_op jit(solution)/shard_map/ppermute | solution.py:316
  24.7 7.2 %all-to-all-start.1 = ((bf16[8,128,1024]{2,1,0:T(8,128)(2,1)}), bf16[8,128,1024]{2,1,0:T(8,128)(2,1)S(1)}, u32[]{:S(2)}, u32[]{:S(2)}) async-start(bf16[8,128,1024]{2,1,0:T(8,128)(2,1)} %bitcast.37), calls=%async_computation.1 | async-start | bytes 4194304 | tf_op jit(solution)/shard_map/all_to_all | solution.py:339
  32.0 2.8 %collective-permute-done.2 = bf16[1024,256]{1,0:T(8,128)(2,1)} collective-permute-done((bf16[1024,256]{1,0:T(8,128)(2,1)S(1)}, bf16[1024,256]{1,0:T(8,128)(2,1)}, u32[]{:S(2)}, u32[]{:S(2)}) %collective-permute-start.2) | collective-permute-done | bytes 524320 | tf_op jit(solution)/shard_map/ppermute | solution.py:316
  34.7 1.3 collective-permute-done.1
  36.0 2.5 %collective-permute-done = bf16[1024,256]{1,0:T(8,128)(2,1)} collective-permute-done((bf16[1024,256]{1,0:T(8,128)(2,1)S(1)}, bf16[1024,256]{1,0:T(8,128)(2,1)}, u32[]{:S(2)}, u32[]{:S(2)}) %collective-permute-start) | collective-permute-done | bytes 524320 | tf_op jit(solution)/shard_map/ppermute | solution.py:316
  39.4 2.3 %collective-permute-start.3 = (bf16[1024,256]{1,0:T(8,128)(2,1)}, bf16[1024,256]{1,0:T(8,128)(2,1)S(1)}, u32[]{:S(2)}, u32[]{:S(2)}) collective-permute-start(bf16[1024,256]{1,0:T(8,128)(2,1)} %collective-permute-done.2), channel_id=1, source_target_pairs={{0,32},{32,64},{64,96},{96,0},{1,33},{33,65},{65,97},{97,1},{2,34}... | collective-permute-start | bytes 1572872 | tf_op jit(solution)/shard_map/ppermute | solution.py:316
  42.0 8.7 %collective-permute-done.4 = bf16[1024,256]{1,0:T(8,128)(2,1)S(1)} collective-permute-done((bf16[1024,256]{1,0:T(8,128)(2,1)}, bf16[1024,256]{1,0:T(8,128)(2,1)S(1)}, u32[]{:S(2)}, u32[]{:S(2)}) %collective-permute-start.4) | collective-permute-done | bytes 524320 | tf_op jit(solution)/shard_map/ppermute | solution.py:316
  50.9 3.4 %collective-permute-done.3 = bf16[1024,256]{1,0:T(8,128)(2,1)S(1)} collective-permute-done((bf16[1024,256]{1,0:T(8,128)(2,1)}, bf16[1024,256]{1,0:T(8,128)(2,1)S(1)}, u32[]{:S(2)}, u32[]{:S(2)}) %collective-permute-start.3) | collective-permute-done | bytes 524320 | tf_op jit(solution)/shard_map/ppermute | solution.py:316
  54.3 10.8 %collective-permute-done.6 = bf16[1024,256]{1,0:T(8,128)(2,1)S(1)} collective-permute-done((bf16[1024,256]{1,0:T(8,128)(2,1)}, bf16[1024,256]{1,0:T(8,128)(2,1)S(1)}, u32[]{:S(2)}, u32[]{:S(2)}) %collective-permute-start.6) | collective-permute-done | bytes 524320 | tf_op jit(solution)/shard_map/ppermute | solution.py:316
  65.8 1.3 collective-permute-done.14
  68.7 25.9 %shard_map.56 = (bf16[640,1024]{1,0:T(8,128)(2,1)S(1)}, bf16[129,128,256]{2,1,0:T(8,128)(2,1)S(1)}) custom-call(s32[19,132]{1,0:T(8,128)S(1)} %copy-done, bf16[1024,1024]{1,0:T(8,128)(2,1)S(1)} %bitcast.35, bf16[8,128,256]{2,1,0:T(8,128)(2,1)} %copy-done.2, bf16[8,128,256]{2,1,0:T(8,128)(2,1)} %bitcast.13.refs_1_, bf16[8,128,256]{2,1,0:T(8,128)(2,1)} %bitcast.49, ...), custom_call_target="tpu_custom_call" | custom-call | flops 22145925120 | bytes 6000000 | tf_op jit(solution)/shard_map/pallas_call | solution.py:267
  94.6 14.7 %shard_map.57 = bf16[384,1024]{1,0:T(8,128)(2,1)S(1)} custom-call(s32[19,132]{1,0:T(8,128)S(1)} %copy-done, bf16[1024,1024]{1,0:T(8,128)(2,1)S(1)} %bitcast.36, bf16[129,128,256]{2,1,0:T(8,128)(2,1)S(1)} %get-tuple-element.20.refs_0_), custom_call_target="tpu_custom_call" | custom-call | flops 13287555072 | bytes 6000000 | tf_op jit(solution)/shard_map/pallas_call | solution.py:267
  110.1 3.0 %collective-permute-start.21 = (bf16[128,1024]{1,0:T(8,128)(2,1)S(1)}, bf16[128,1024]{1,0:T(8,128)(2,1)S(1)}, u32[]{:S(2)}, u32[]{:S(2)}) collective-permute-start(bf16[128,1024]{1,0:T(8,128)(2,1)S(1)} %get-tuple-element.27), channel_id=1, source_target_pairs={{0,3},{1,0},{2,1},{3,2},{4,7},{5,4},{6,5},{7,6},{8,11},{9,8},{10,9... | collective-permute-start | bytes 786440 | tf_op jit(solution)/shard_map/ppermute | solution.py:369
  114.5 1.8 %collective-permute-start.18 = (bf16[128,1024]{1,0:T(8,128)(2,1)S(1)}, bf16[128,1024]{1,0:T(8,128)(2,1)S(1)}, u32[]{:S(2)}, u32[]{:S(2)}) collective-permute-start(bf16[128,1024]{1,0:T(8,128)(2,1)S(1)} %get-tuple-element.22), channel_id=1, source_target_pairs={{0,2},{1,3},{2,0},{3,1},{4,6},{5,7},{6,4},{7,5},{8,10},{9,11},{10,... | collective-permute-start | bytes 786440 | tf_op jit(solution)/shard_map/ppermute | solution.py:369
  116.3 3.9 %collective-permute-start.17 = (bf16[128,1024]{1,0:T(8,128)(2,1)S(1)}, bf16[128,1024]{1,0:T(8,128)(2,1)S(1)}, u32[]{:S(2)}, u32[]{:S(2)}) collective-permute-start(bf16[128,1024]{1,0:T(8,128)(2,1)S(1)} %get-tuple-element.23), channel_id=1, source_target_pairs={{0,7},{1,4},{2,5},{3,6},{4,3},{5,0},{6,1},{7,2},{8,15},{9,12},{10,... | collective-permute-start | bytes 786440 | tf_op jit(solution)/shard_map/ppermute | solution.py:369
  120.1 10.3 %collective-permute-done.21.refs_6_ = bf16[128,1024]{1,0:T(8,128)(2,1)S(1)} collective-permute-done((bf16[128,1024]{1,0:T(8,128)(2,1)S(1)}, bf16[128,1024]{1,0:T(8,128)(2,1)S(1)}, u32[]{:S(2)}, u32[]{:S(2)}) %collective-permute-start.21) | collective-permute-done | bytes 262176 | tf_op jit(solution)/shard_map/ppermute | solution.py:369
  130.4 7.5 %collective-permute-start.15 = (bf16[128,1024]{1,0:T(8,128)(2,1)S(1)}, bf16[128,1024]{1,0:T(8,128)(2,1)S(1)}, u32[]{:S(2)}, u32[]{:S(2)}) collective-permute-start(bf16[128,1024]{1,0:T(8,128)(2,1)S(1)} %get-tuple-element.25), channel_id=1, source_target_pairs={{0,6},{1,7},{2,4},{3,5},{4,2},{5,3},{6,0},{7,1},{8,14},{9,15},{10,... | collective-permute-start | bytes 786440 | tf_op jit(solution)/shard_map/ppermute | solution.py:369
  138.0 2.4 %collective-permute-done.16.refs_1_ = bf16[128,1024]{1,0:T(8,128)(2,1)S(1)} collective-permute-done((bf16[128,1024]{1,0:T(8,128)(2,1)S(1)}, bf16[128,1024]{1,0:T(8,128)(2,1)S(1)}, u32[]{:S(2)}, u32[]{:S(2)}) %collective-permute-start.16) | collective-permute-done | bytes 262176 | tf_op jit(solution)/shard_map/ppermute | solution.py:369
  140.4 8.9 %collective-permute-done.15.refs_0_ = bf16[128,1024]{1,0:T(8,128)(2,1)S(1)} collective-permute-done((bf16[128,1024]{1,0:T(8,128)(2,1)S(1)}, bf16[128,1024]{1,0:T(8,128)(2,1)S(1)}, u32[]{:S(2)}, u32[]{:S(2)}) %collective-permute-start.15) | collective-permute-done | bytes 262176 | tf_op jit(solution)/shard_map/ppermute | solution.py:369
  150.0 2.9 %shard_map.58 = bf16[128,8192]{1,0:T(8,128)(2,1)} custom-call(s32[19,132]{1,0:T(8,128)} %shard_map.55.listed, bf16[128,1024]{1,0:T(8,128)(2,1)} %copy-done.9, bf16[128,1024]{1,0:T(8,128)(2,1)} %copy-done.8, bf16[128,1024]{1,0:T(8,128)(2,1)} %copy-done.7, bf16[128,1024]{1,0:T(8,128)(2,1)} %copy-done.6, bf16[128,1024]{1,0:T(8,128)(2,1)} %copy-done.5, ...), custom_call_target="tpu_custom_call" | custom-call | tf_op jit(solution)/shard_map/pallas_call | solution.py:305
  (77 shorter events, 10.8 us)
Async XLA Ops:
  3.4 17.7 %all-to-all-start = ((bf16[8,128,256]{1,2,0:T(8,128)(2,1)}), bf16[8,128,256]{1,2,0:T(8,128)(2,1)S(1)}, u32[]{:S(2)}, u32[]{:S(2)}) async-start(bf16[8,128,256]{1,2,0:T(8,128)(2,1)} %pad_maximum_fusion), calls=%async_computation | async-start | bytes 1048576 | tf_op jit(solution)/shard_map/all_to_all | solution.py:339
  21.4 13.3 %collective-permute-start.2 = (bf16[1024,256]{1,0:T(8,128)(2,1)S(1)}, bf16[1024,256]{1,0:T(8,128)(2,1)}, u32[]{:S(2)}, u32[]{:S(2)}) collective-permute-start(bf16[1024,256]{1,0:T(8,128)(2,1)S(1)} %bitcast.42), channel_id=1, source_target_pairs={{0,32},{32,64},{64,96},{96,0},{1,33},{33,65},{65,97},{97,1},{2,34}... | collective-permute-start | bytes 1572872 | tf_op jit(solution)/shard_map/ppermute | solution.py:316
  21.6 14.4 %collective-permute-start.1 = (bf16[1024,256]{1,0:T(8,128)(2,1)S(1)}, bf16[1024,256]{1,0:T(8,128)(2,1)}, u32[]{:S(2)}, u32[]{:S(2)}) collective-permute-start(bf16[1024,256]{1,0:T(8,128)(2,1)S(1)} %bitcast.43), channel_id=1, source_target_pairs={{0,96},{32,0},{64,32},{96,64},{1,97},{33,1},{65,33},{97,65},{2,98}... | collective-permute-start | bytes 1572872 | tf_op jit(solution)/shard_map/ppermute | solution.py:316
  23.5 15.0 %collective-permute-start = (bf16[1024,256]{1,0:T(8,128)(2,1)S(1)}, bf16[1024,256]{1,0:T(8,128)(2,1)}, u32[]{:S(2)}, u32[]{:S(2)}) collective-permute-start(bf16[1024,256]{1,0:T(8,128)(2,1)S(1)} %bitcast.44), channel_id=1, source_target_pairs={{0,16},{16,0},{1,17},{17,1},{2,18},{18,2},{3,19},{19,3},{4,20},{20... | collective-permute-start | bytes 1572872 | tf_op jit(solution)/shard_map/ppermute | solution.py:316
  24.7 43.2 %all-to-all-start.1 = ((bf16[8,128,1024]{2,1,0:T(8,128)(2,1)}), bf16[8,128,1024]{2,1,0:T(8,128)(2,1)S(1)}, u32[]{:S(2)}, u32[]{:S(2)}) async-start(bf16[8,128,1024]{2,1,0:T(8,128)(2,1)} %bitcast.37), calls=%async_computation.1 | async-start | bytes 4194304 | tf_op jit(solution)/shard_map/all_to_all | solution.py:339
  31.9 9.9 %collective-permute-start.7 = (bf16[1024,256]{1,0:T(8,128)(2,1)S(1)}, bf16[1024,256]{1,0:T(8,128)(2,1)S(1)}, u32[]{:S(2)}, u32[]{:S(2)}) collective-permute-start(bf16[1024,256]{1,0:T(8,128)(2,1)S(1)} %bitcast.45), channel_id=1, source_target_pairs={{0,8},{8,0},{1,9},{9,1},{2,10},{10,2},{3,11},{11,3},{4,12},{12,4},... | collective-permute-start | bytes 1572872 | tf_op jit(solution)/shard_map/ppermute | solution.py:316
  38.5 12.3 %collective-permute-start.4 = (bf16[1024,256]{1,0:T(8,128)(2,1)}, bf16[1024,256]{1,0:T(8,128)(2,1)S(1)}, u32[]{:S(2)}, u32[]{:S(2)}) collective-permute-start(bf16[1024,256]{1,0:T(8,128)(2,1)} %collective-permute-done), channel_id=1, source_target_pairs={{0,96},{32,0},{64,32},{96,64},{1,97},{33,1},{65,33},{97,65},{2,98}... | collective-permute-start | bytes 1572872 | tf_op jit(solution)/shard_map/ppermute | solution.py:316
  39.4 11.4 %collective-permute-start.8 = (bf16[1024,256]{1,0:T(8,128)(2,1)}, bf16[1024,256]{1,0:T(8,128)(2,1)S(1)}, u32[]{:S(2)}, u32[]{:S(2)}) collective-permute-start(bf16[1024,256]{1,0:T(8,128)(2,1)} %collective-permute-done.1), channel_id=1, source_target_pairs={{0,8},{8,0},{1,9},{9,1},{2,10},{10,2},{3,11},{11,3},{4,12},{12,4},... | collective-permute-start | bytes 1572872 | tf_op jit(solution)/shard_map/ppermute | solution.py:316
  39.4 14.9 %collective-permute-start.3 = (bf16[1024,256]{1,0:T(8,128)(2,1)}, bf16[1024,256]{1,0:T(8,128)(2,1)S(1)}, u32[]{:S(2)}, u32[]{:S(2)}) collective-permute-start(bf16[1024,256]{1,0:T(8,128)(2,1)} %collective-permute-done.2), channel_id=1, source_target_pairs={{0,32},{32,64},{64,96},{96,0},{1,33},{33,65},{65,97},{97,1},{2,34}... | collective-permute-start | bytes 1572872 | tf_op jit(solution)/shard_map/ppermute | solution.py:316
  41.7 23.5 %collective-permute-start.6 = (bf16[1024,256]{1,0:T(8,128)(2,1)}, bf16[1024,256]{1,0:T(8,128)(2,1)S(1)}, u32[]{:S(2)}, u32[]{:S(2)}) collective-permute-start(bf16[1024,256]{1,0:T(8,128)(2,1)} %collective-permute-done), channel_id=1, source_target_pairs={{0,32},{32,64},{64,96},{96,0},{1,33},{33,65},{65,97},{97,1},{2,34}... | collective-permute-start | bytes 1572872 | tf_op jit(solution)/shard_map/ppermute | solution.py:316
  41.9 23.3 %collective-permute-start.10 = (bf16[1024,256]{1,0:T(8,128)(2,1)}, bf16[1024,256]{1,0:T(8,128)(2,1)S(1)}, u32[]{:S(2)}, u32[]{:S(2)}) collective-permute-start(bf16[1024,256]{1,0:T(8,128)(2,1)} %collective-permute-done.2), channel_id=1, source_target_pairs={{0,8},{8,0},{1,9},{9,1},{2,10},{10,2},{3,11},{11,3},{4,12},{12,4},... | collective-permute-start | bytes 1572872 | tf_op jit(solution)/shard_map/ppermute | solution.py:316
  50.8 14.9 %collective-permute-start.5 = (bf16[1024,256]{1,0:T(8,128)(2,1)S(1)}, bf16[1024,256]{1,0:T(8,128)(2,1)S(1)}, u32[]{:S(2)}, u32[]{:S(2)}) collective-permute-start(bf16[1024,256]{1,0:T(8,128)(2,1)S(1)} %collective-permute-done.4), channel_id=1, source_target_pairs={{0,96},{32,0},{64,32},{96,64},{1,97},{33,1},{65,33},{97,65},{2,98}... | collective-permute-start | bytes 1572872 | tf_op jit(solution)/shard_map/ppermute | solution.py:316
  50.8 15.0 %collective-permute-start.11 = (bf16[1024,256]{1,0:T(8,128)(2,1)}, bf16[1024,256]{1,0:T(8,128)(2,1)S(1)}, u32[]{:S(2)}, u32[]{:S(2)}) collective-permute-start(bf16[1024,256]{1,0:T(8,128)(2,1)} %collective-permute-done), channel_id=1, source_target_pairs={{0,8},{8,0},{1,9},{9,1},{2,10},{10,2},{3,11},{11,3},{4,12},{12,4},... | collective-permute-start | bytes 1572872 | tf_op jit(solution)/shard_map/ppermute | solution.py:316
  54.3 11.5 %collective-permute-start.9 = (bf16[1024,256]{1,0:T(8,128)(2,1)S(1)}, bf16[1024,256]{1,0:T(8,128)(2,1)S(1)}, u32[]{:S(2)}, u32[]{:S(2)}) collective-permute-start(bf16[1024,256]{1,0:T(8,128)(2,1)S(1)} %collective-permute-done.3), channel_id=1, source_target_pairs={{0,8},{8,0},{1,9},{9,1},{2,10},{10,2},{3,11},{11,3},{4,12},{12,4},... | collective-permute-start | bytes 1572872 | tf_op jit(solution)/shard_map/ppermute | solution.py:316
  65.2 1.9 %collective-permute-start.14 = (bf16[1024,256]{1,0:T(8,128)(2,1)S(1)}, bf16[1024,256]{1,0:T(8,128)(2,1)S(1)}, u32[]{:S(2)}, u32[]{:S(2)}) collective-permute-start(bf16[1024,256]{1,0:T(8,128)(2,1)S(1)} %collective-permute-done.6), channel_id=1, source_target_pairs={{0,8},{8,0},{1,9},{9,1},{2,10},{10,2},{3,11},{11,3},{4,12},{12,4},... | collective-permute-start | bytes 1572872 | tf_op jit(solution)/shard_map/ppermute | solution.py:316
  65.2 2.8 %collective-permute-start.12 = (bf16[1024,256]{1,0:T(8,128)(2,1)S(1)}, bf16[1024,256]{1,0:T(8,128)(2,1)}, u32[]{:S(2)}, u32[]{:S(2)}) collective-permute-start(bf16[1024,256]{1,0:T(8,128)(2,1)S(1)} %collective-permute-done.4), channel_id=1, source_target_pairs={{0,8},{8,0},{1,9},{9,1},{2,10},{10,2},{3,11},{11,3},{4,12},{12,4},... | collective-permute-start | bytes 1572872 | tf_op jit(solution)/shard_map/ppermute | solution.py:316
  65.7 3.0 %collective-permute-start.13 = (bf16[1024,256]{1,0:T(8,128)(2,1)S(1)}, bf16[1024,256]{1,0:T(8,128)(2,1)}, u32[]{:S(2)}, u32[]{:S(2)}) collective-permute-start(bf16[1024,256]{1,0:T(8,128)(2,1)S(1)} %collective-permute-done.5), channel_id=1, source_target_pairs={{0,8},{8,0},{1,9},{9,1},{2,10},{10,2},{3,11},{11,3},{4,12},{12,4},... | collective-permute-start | bytes 1572872 | tf_op jit(solution)/shard_map/ppermute | solution.py:316
  110.1 20.3 %collective-permute-start.21 = (bf16[128,1024]{1,0:T(8,128)(2,1)S(1)}, bf16[128,1024]{1,0:T(8,128)(2,1)S(1)}, u32[]{:S(2)}, u32[]{:S(2)}) collective-permute-start(bf16[128,1024]{1,0:T(8,128)(2,1)S(1)} %get-tuple-element.27), channel_id=1, source_target_pairs={{0,3},{1,0},{2,1},{3,2},{4,7},{5,4},{6,5},{7,6},{8,11},{9,8},{10,9... | collective-permute-start | bytes 786440 | tf_op jit(solution)/shard_map/ppermute | solution.py:369
  113.1 17.3 %collective-permute-start.20 = (bf16[128,1024]{1,0:T(8,128)(2,1)S(1)}, bf16[128,1024]{1,0:T(8,128)(2,1)S(1)}, u32[]{:S(2)}, u32[]{:S(2)}) collective-permute-start(bf16[128,1024]{1,0:T(8,128)(2,1)S(1)} %get-tuple-element.28), channel_id=1, source_target_pairs={{0,1},{1,2},{2,3},{3,0},{4,5},{5,6},{6,7},{7,4},{8,9},{9,10},{10,1... | collective-permute-start | bytes 786440 | tf_op jit(solution)/shard_map/ppermute | solution.py:369
  113.2 24.8 %collective-permute-start.19 = (bf16[128,1024]{1,0:T(8,128)(2,1)S(1)}, bf16[128,1024]{1,0:T(8,128)(2,1)S(1)}, u32[]{:S(2)}, u32[]{:S(2)}) collective-permute-start(bf16[128,1024]{1,0:T(8,128)(2,1)S(1)} %get-tuple-element.21), channel_id=1, source_target_pairs={{0,4},{1,5},{2,6},{3,7},{4,0},{5,1},{6,2},{7,3},{8,12},{9,13},{10,... | collective-permute-start | bytes 786440 | tf_op jit(solution)/shard_map/ppermute | solution.py:369
  114.5 23.5 %collective-permute-start.18 = (bf16[128,1024]{1,0:T(8,128)(2,1)S(1)}, bf16[128,1024]{1,0:T(8,128)(2,1)S(1)}, u32[]{:S(2)}, u32[]{:S(2)}) collective-permute-start(bf16[128,1024]{1,0:T(8,128)(2,1)S(1)} %get-tuple-element.22), channel_id=1, source_target_pairs={{0,2},{1,3},{2,0},{3,1},{4,6},{5,7},{6,4},{7,5},{8,10},{9,11},{10,... | collective-permute-start | bytes 786440 | tf_op jit(solution)/shard_map/ppermute | solution.py:369
  116.3 21.7 %collective-permute-start.17 = (bf16[128,1024]{1,0:T(8,128)(2,1)S(1)}, bf16[128,1024]{1,0:T(8,128)(2,1)S(1)}, u32[]{:S(2)}, u32[]{:S(2)}) collective-permute-start(bf16[128,1024]{1,0:T(8,128)(2,1)S(1)} %get-tuple-element.23), channel_id=1, source_target_pairs={{0,7},{1,4},{2,5},{3,6},{4,3},{5,0},{6,1},{7,2},{8,15},{9,12},{10,... | collective-permute-start | bytes 786440 | tf_op jit(solution)/shard_map/ppermute | solution.py:369
  130.4 10.0 %collective-permute-start.16 = (bf16[128,1024]{1,0:T(8,128)(2,1)S(1)}, bf16[128,1024]{1,0:T(8,128)(2,1)S(1)}, u32[]{:S(2)}, u32[]{:S(2)}) collective-permute-start(bf16[128,1024]{1,0:T(8,128)(2,1)S(1)} %get-tuple-element.24), channel_id=1, source_target_pairs={{0,5},{1,6},{2,7},{3,4},{4,1},{5,2},{6,3},{7,0},{8,13},{9,14},{10,... | collective-permute-start | bytes 786440 | tf_op jit(solution)/shard_map/ppermute | solution.py:369
  130.4 18.8 %collective-permute-start.15 = (bf16[128,1024]{1,0:T(8,128)(2,1)S(1)}, bf16[128,1024]{1,0:T(8,128)(2,1)S(1)}, u32[]{:S(2)}, u32[]{:S(2)}) collective-permute-start(bf16[128,1024]{1,0:T(8,128)(2,1)S(1)} %get-tuple-element.25), channel_id=1, source_target_pairs={{0,6},{1,7},{2,4},{3,5},{4,2},{5,3},{6,0},{7,1},{8,14},{9,15},{10,... | collective-permute-start | bytes 786440 | tf_op jit(solution)/shard_map/ppermute | solution.py:369
  (20 other events, 233.5 us)

commit v4 on v3

--- a/solution.py
+++ b/solution.py
@@ -374,6 +374,7 @@
     attended, gathered = attend(query_local, pieces, lists, early)
     received = send(attended, early)
     (attended,) = attend(query_local, gathered, lists, late)
+    attended, received = lax.optimization_barrier((attended, received))
     received += send(attended, late)
     return assemble(lists, received)
 

time: 154 us -> 145 us (0.942)
  the two profiles are of different devices: /device:TPU:22 before, /device:TPU:1 now
where the time goes in v4:
time: 145 us
  starting transfers between devices  57.4 us (40%)
  Pallas kernels  55.6 us (38%)
  waiting for transfers between devices  23.4 us (16%)
  local copies, waits for them, and re-layouts  7.52 us (5%)
    pallas_call x2, Pallas kernels, attend(): pl.pallas_call(functools.partial(attend_kernel, blocks=blocks, steps=step...  45.2 us
    ppermute x15, starting transfers between devices, shift(): lax.ppermute(array, axis, [(i, (i + step) % size) for i in range(size)])  29.7 us
    all_to_all x2, starting transfers between devices, exchange(): lax.all_to_all(cut, head_axes, split_axis=0, concat_axis=0, tiled=True)  15.7 us
    ppermute x15, waiting for transfers between devices, shift(): lax.ppermute(array, axis, [(i, (i + step) % size) for i in range(size)])  14.4 us
    ppermute x7, starting transfers between devices, send(): part = lax.ppermute(part, head_axes, pairs)  11.9 us
    ppermute x7, waiting for transfers between devices, send(): part = lax.ppermute(part, head_axes, pairs)  8.99 us
    pallas_call x1, Pallas kernels, plan(): pl.pallas_call(functools.partial(plan_kernel, blocks=blocks, sizes=sizes,...  7.49 us
    unnamed x42, local copies, waits for them, and re-layouts  3.95 us
  transfers between devices with their start and end apart: 24, of which 9 were waited for; matrix products, arithmetic and copies ran while one was open for 1% of the time, Pallas kernels for 18%

profile of v4, /device:TPU:1, one launch (start us, length us, event | category | flops | bytes accessed | tf_op | source)
XLA Modules:
  0.0 145.0 jit_solution(15230276593965524855)
XLA Ops:
  0.0 1.3 copy.15
  3.4 8.5 %all-to-all-start = ((bf16[8,128,256]{1,2,0:T(8,128)(2,1)}), bf16[8,128,256]{1,2,0:T(8,128)(2,1)S(1)}, u32[]{:S(2)}, u32[]{:S(2)}) async-start(bf16[8,128,256]{1,2,0:T(8,128)(2,1)} %pad_maximum_fusion), calls=%async_computation | async-start | bytes 1048576 | tf_op jit(solution)/shard_map/all_to_all | solution.py:339
  11.9 1.6 %copy.22 = bf16[16,8,8,1024]{3,2,0,1:T(8,128)(2,1)} copy(bf16[16,8,8,1024]{3,2,1,0:T(8,128)(2,1)S(1)} %bitcast.38) | data formatting | bytes 4194304 | tf_op jit(solution)/shard_map/reshape | solution.py:343
  14.1 7.5 %shard_map.55.listed = s32[19,132]{1,0:T(8,128)} custom-call(s32[5]{0:T(128)} %stack.23.place_ref, s32[16,16,16]{2,1,0:T(8,128)} %codes_ref.1, s32[16,16]{1,0:T(8,128)} %counts_ref.1), custom_call_target="tpu_custom_call" | custom-call | bytes 20000000 | tf_op jit(solution)/shard_map/pallas_call | solution.py:76
  22.5 2.1 %collective-permute-start.1 = (bf16[1024,256]{1,0:T(8,128)(2,1)S(1)}, bf16[1024,256]{1,0:T(8,128)(2,1)}, u32[]{:S(2)}, u32[]{:S(2)}) collective-permute-start(bf16[1024,256]{1,0:T(8,128)(2,1)S(1)} %bitcast.43), channel_id=1, source_target_pairs={{0,96},{32,0},{64,32},{96,64},{1,97},{33,1},{65,33},{97,65},{2,98}... | collective-permute-start | bytes 1572872 | tf_op jit(solution)/shard_map/ppermute | solution.py:316
  24.7 7.2 %all-to-all-start.1 = ((bf16[8,128,1024]{2,1,0:T(8,128)(2,1)}), bf16[8,128,1024]{2,1,0:T(8,128)(2,1)S(1)}, u32[]{:S(2)}, u32[]{:S(2)}) async-start(bf16[8,128,1024]{2,1,0:T(8,128)(2,1)} %bitcast.37), calls=%async_computation.1 | async-start | bytes 4194304 | tf_op jit(solution)/shard_map/all_to_all | solution.py:339
  31.9 2.6 %collective-permute-start.7 = (bf16[1024,256]{1,0:T(8,128)(2,1)S(1)}, bf16[1024,256]{1,0:T(8,128)(2,1)S(1)}, u32[]{:S(2)}, u32[]{:S(2)}) collective-permute-start(bf16[1024,256]{1,0:T(8,128)(2,1)S(1)} %bitcast.45), channel_id=1, source_target_pairs={{0,8},{8,0},{1,9},{9,1},{2,10},{10,2},{3,11},{11,3},{4,12},{12,4},... | collective-permute-start | bytes 1572872 | tf_op jit(solution)/shard_map/ppermute | solution.py:316
  35.3 1.5 %collective-permute-start.4 = (bf16[1024,256]{1,0:T(8,128)(2,1)}, bf16[1024,256]{1,0:T(8,128)(2,1)S(1)}, u32[]{:S(2)}, u32[]{:S(2)}) collective-permute-start(bf16[1024,256]{1,0:T(8,128)(2,1)} %collective-permute-done), channel_id=1, source_target_pairs={{0,96},{32,0},{64,32},{96,64},{1,97},{33,1},{65,33},{97,65},{2,98}... | collective-permute-start | bytes 1572872 | tf_op jit(solution)/shard_map/ppermute | solution.py:316
  36.7 7.3 %collective-permute-start.8 = (bf16[1024,256]{1,0:T(8,128)(2,1)}, bf16[1024,256]{1,0:T(8,128)(2,1)S(1)}, u32[]{:S(2)}, u32[]{:S(2)}) collective-permute-start(bf16[1024,256]{1,0:T(8,128)(2,1)} %collective-permute-done.1), channel_id=1, source_target_pairs={{0,8},{8,0},{1,9},{9,1},{2,10},{10,2},{3,11},{11,3},{4,12},{12,4},... | collective-permute-start | bytes 1572872 | tf_op jit(solution)/shard_map/ppermute | solution.py:316
  44.8 2.7 %collective-permute-start.5 = (bf16[1024,256]{1,0:T(8,128)(2,1)S(1)}, bf16[1024,256]{1,0:T(8,128)(2,1)}, u32[]{:S(2)}, u32[]{:S(2)}) collective-permute-start(bf16[1024,256]{1,0:T(8,128)(2,1)S(1)} %collective-permute-done.4), channel_id=1, source_target_pairs={{0,96},{32,0},{64,32},{96,64},{1,97},{33,1},{65,33},{97,65},{2,98}... | collective-permute-start | bytes 1572872 | tf_op jit(solution)/shard_map/ppermute | solution.py:316
  47.5 9.6 %collective-permute-start.11 = (bf16[1024,256]{1,0:T(8,128)(2,1)}, bf16[1024,256]{1,0:T(8,128)(2,1)S(1)}, u32[]{:S(2)}, u32[]{:S(2)}) collective-permute-start(bf16[1024,256]{1,0:T(8,128)(2,1)} %collective-permute-done), channel_id=1, source_target_pairs={{0,8},{8,0},{1,9},{9,1},{2,10},{10,2},{3,11},{11,3},{4,12},{12,4},... | collective-permute-start | bytes 1572872 | tf_op jit(solution)/shard_map/ppermute | solution.py:316
  57.1 1.7 %collective-permute-done.3 = bf16[1024,256]{1,0:T(8,128)(2,1)S(1)} collective-permute-done((bf16[1024,256]{1,0:T(8,128)(2,1)S(1)}, bf16[1024,256]{1,0:T(8,128)(2,1)S(1)}, u32[]{:S(2)}, u32[]{:S(2)}) %collective-permute-start.3) | collective-permute-done | bytes 524320 | tf_op jit(solution)/shard_map/ppermute | solution.py:316
  58.8 1.2 collective-permute-start.9
  60.0 10.1 %collective-permute-done.6 = bf16[1024,256]{1,0:T(8,128)(2,1)S(1)} collective-permute-done((bf16[1024,256]{1,0:T(8,128)(2,1)}, bf16[1024,256]{1,0:T(8,128)(2,1)S(1)}, u32[]{:S(2)}, u32[]{:S(2)}) %collective-permute-start.6) | collective-permute-done | bytes 524320 | tf_op jit(solution)/shard_map/ppermute | solution.py:316
  74.2 27.3 %shard_map.56 = (bf16[640,1024]{1,0:T(8,128)(2,1)S(1)}, bf16[129,128,256]{2,1,0:T(8,128)(2,1)S(1)}) custom-call(s32[19,132]{1,0:T(8,128)S(1)} %copy-done, bf16[1024,1024]{1,0:T(8,128)(2,1)S(1)} %bitcast.35, bf16[8,128,256]{2,1,0:T(8,128)(2,1)} %copy-done.2, bf16[8,128,256]{2,1,0:T(8,128)(2,1)} %bitcast.13.refs_1_, bf16[8,128,256]{2,1,0:T(8,128)(2,1)} %bitcast.50, ...), custom_call_target="tpu_custom_call" | custom-call | flops 22145925120 | bytes 6000000 | tf_op jit(solution)/shard_map/pallas_call | solution.py:267
  101.6 3.4 %collective-permute-start.19 = (bf16[128,1024]{1,0:T(8,128)(2,1)S(1)}, bf16[128,1024]{1,0:T(8,128)(2,1)S(1)}, u32[]{:S(2)}, u32[]{:S(2)}) collective-permute-start(bf16[128,1024]{1,0:T(8,128)(2,1)S(1)} %get-tuple-element.33), channel_id=1, source_target_pairs={{0,4},{1,5},{2,6},{3,7},{4,0},{5,1},{6,2},{7,3},{8,12},{9,13},{10,... | collective-permute-start | bytes 786440 | tf_op jit(solution)/shard_map/ppermute | solution.py:369
  105.0 2.5 %collective-permute-start.18 = (bf16[128,1024]{1,0:T(8,128)(2,1)S(1)}, bf16[128,1024]{1,0:T(8,128)(2,1)S(1)}, u32[]{:S(2)}, u32[]{:S(2)}) collective-permute-start(bf16[128,1024]{1,0:T(8,128)(2,1)S(1)} %get-tuple-element.34), channel_id=1, source_target_pairs={{0,2},{1,3},{2,0},{3,1},{4,6},{5,7},{6,4},{7,5},{8,10},{9,11},{10,... | collective-permute-start | bytes 786440 | tf_op jit(solution)/shard_map/ppermute | solution.py:369
  108.2 3.2 %collective-permute-start.16 = (bf16[128,1024]{1,0:T(8,128)(2,1)S(1)}, bf16[128,1024]{1,0:T(8,128)(2,1)S(1)}, u32[]{:S(2)}, u32[]{:S(2)}) collective-permute-start(bf16[128,1024]{1,0:T(8,128)(2,1)S(1)} %get-tuple-element.36), channel_id=1, source_target_pairs={{0,5},{1,6},{2,7},{3,4},{4,1},{5,2},{6,3},{7,0},{8,13},{9,14},{10,... | collective-permute-start | bytes 786440 | tf_op jit(solution)/shard_map/ppermute | solution.py:369
  112.1 18.0 %shard_map.57 = bf16[384,1024]{1,0:T(8,128)(2,1)S(1)} custom-call(s32[19,132]{1,0:T(8,128)S(1)} %copy-done, bf16[1024,1024]{1,0:T(8,128)(2,1)S(1)} %bitcast.36, bf16[129,128,256]{2,1,0:T(8,128)(2,1)S(1)} %get-tuple-element.25.refs_0_), custom_call_target="tpu_custom_call" | custom-call | flops 13287555072 | bytes 6000000 | tf_op jit(solution)/shard_map/pallas_call | solution.py:267
  130.1 2.0 %collective-permute-done.15.refs_0_ = bf16[128,1024]{1,0:T(8,128)(2,1)S(1)} collective-permute-done((bf16[128,1024]{1,0:T(8,128)(2,1)S(1)}, bf16[128,1024]{1,0:T(8,128)(2,1)S(1)}, u32[]{:S(2)}, u32[]{:S(2)}) %collective-permute-start.15) | collective-permute-done | bytes 262176 | tf_op jit(solution)/shard_map/ppermute | solution.py:369
  132.9 1.5 %collective-permute-start.20 = (bf16[128,1024]{1,0:T(8,128)(2,1)S(1)}, bf16[128,1024]{1,0:T(8,128)(2,1)S(1)}, u32[]{:S(2)}, u32[]{:S(2)}) collective-permute-start(bf16[128,1024]{1,0:T(8,128)(2,1)S(1)} %get-tuple-element.40), channel_id=1, source_target_pairs={{0,1},{1,2},{2,3},{3,0},{4,5},{5,6},{6,7},{7,4},{8,9},{9,10},{10,1... | collective-permute-start | bytes 786440 | tf_op jit(solution)/shard_map/ppermute | solution.py:369
  134.4 5.8 %collective-permute-done.21.refs_6_ = bf16[128,1024]{1,0:T(8,128)(2,1)S(1)} collective-permute-done((bf16[128,1024]{1,0:T(8,128)(2,1)S(1)}, bf16[128,1024]{1,0:T(8,128)(2,1)S(1)}, u32[]{:S(2)}, u32[]{:S(2)}) %collective-permute-start.21) | collective-permute-done | bytes 262176 | tf_op jit(solution)/shard_map/ppermute | solution.py:369
  140.2 1.2 collective-permute-done.20.refs_5_
  142.1 2.9 %shard_map.58 = bf16[128,8192]{1,0:T(8,128)(2,1)} custom-call(s32[19,132]{1,0:T(8,128)} %shard_map.55.listed, bf16[128,1024]{1,0:T(8,128)(2,1)} %copy-done.7, bf16[128,1024]{1,0:T(8,128)(2,1)} %copy-done.6, bf16[128,1024]{1,0:T(8,128)(2,1)} %copy-done.5, bf16[128,1024]{1,0:T(8,128)(2,1)} %copy-done.4, bf16[128,1024]{1,0:T(8,128)(2,1)} %copy-done.3, ...), custom_call_target="tpu_custom_call" | custom-call | tf_op jit(solution)/shard_map/pallas_call | solution.py:305
  (77 shorter events, 12.3 us)
Async XLA Ops:
  3.4 18.2 %all-to-all-start = ((bf16[8,128,256]{1,2,0:T(8,128)(2,1)}), bf16[8,128,256]{1,2,0:T(8,128)(2,1)S(1)}, u32[]{:S(2)}, u32[]{:S(2)}) async-start(bf16[8,128,256]{1,2,0:T(8,128)(2,1)} %pad_maximum_fusion), calls=%async_computation | async-start | bytes 1048576 | tf_op jit(solution)/shard_map/all_to_all | solution.py:339
  21.9 12.7 %collective-permute-start.2 = (bf16[1024,256]{1,0:T(8,128)(2,1)S(1)}, bf16[1024,256]{1,0:T(8,128)(2,1)S(1)}, u32[]{:S(2)}, u32[]{:S(2)}) collective-permute-start(bf16[1024,256]{1,0:T(8,128)(2,1)S(1)} %bitcast.42), channel_id=1, source_target_pairs={{0,32},{32,64},{64,96},{96,0},{1,33},{33,65},{65,97},{97,1},{2,34}... | collective-permute-start | bytes 1572872 | tf_op jit(solution)/shard_map/ppermute | solution.py:316
  22.5 12.0 %collective-permute-start.1 = (bf16[1024,256]{1,0:T(8,128)(2,1)S(1)}, bf16[1024,256]{1,0:T(8,128)(2,1)}, u32[]{:S(2)}, u32[]{:S(2)}) collective-permute-start(bf16[1024,256]{1,0:T(8,128)(2,1)S(1)} %bitcast.43), channel_id=1, source_target_pairs={{0,96},{32,0},{64,32},{96,64},{1,97},{33,1},{65,33},{97,65},{2,98}... | collective-permute-start | bytes 1572872 | tf_op jit(solution)/shard_map/ppermute | solution.py:316
  24.6 10.6 %collective-permute-start = (bf16[1024,256]{1,0:T(8,128)(2,1)S(1)}, bf16[1024,256]{1,0:T(8,128)(2,1)}, u32[]{:S(2)}, u32[]{:S(2)}) collective-permute-start(bf16[1024,256]{1,0:T(8,128)(2,1)S(1)} %bitcast.44), channel_id=1, source_target_pairs={{0,16},{16,0},{1,17},{17,1},{2,18},{18,2},{3,19},{19,3},{4,20},{20... | collective-permute-start | bytes 1572872 | tf_op jit(solution)/shard_map/ppermute | solution.py:316
  24.7 49.3 %all-to-all-start.1 = ((bf16[8,128,1024]{2,1,0:T(8,128)(2,1)}), bf16[8,128,1024]{2,1,0:T(8,128)(2,1)S(1)}, u32[]{:S(2)}, u32[]{:S(2)}) async-start(bf16[8,128,1024]{2,1,0:T(8,128)(2,1)} %bitcast.37), calls=%async_computation.1 | async-start | bytes 4194304 | tf_op jit(solution)/shard_map/all_to_all | solution.py:339
  31.9 12.3 %collective-permute-start.7 = (bf16[1024,256]{1,0:T(8,128)(2,1)S(1)}, bf16[1024,256]{1,0:T(8,128)(2,1)S(1)}, u32[]{:S(2)}, u32[]{:S(2)}) collective-permute-start(bf16[1024,256]{1,0:T(8,128)(2,1)S(1)} %bitcast.45), channel_id=1, source_target_pairs={{0,8},{8,0},{1,9},{9,1},{2,10},{10,2},{3,11},{11,3},{4,12},{12,4},... | collective-permute-start | bytes 1572872 | tf_op jit(solution)/shard_map/ppermute | solution.py:316
  35.3 9.5 %collective-permute-start.4 = (bf16[1024,256]{1,0:T(8,128)(2,1)}, bf16[1024,256]{1,0:T(8,128)(2,1)S(1)}, u32[]{:S(2)}, u32[]{:S(2)}) collective-permute-start(bf16[1024,256]{1,0:T(8,128)(2,1)} %collective-permute-done), channel_id=1, source_target_pairs={{0,96},{32,0},{64,32},{96,64},{1,97},{33,1},{65,33},{97,65},{2,98}... | collective-permute-start | bytes 1572872 | tf_op jit(solution)/shard_map/ppermute | solution.py:316
  36.7 10.7 %collective-permute-start.8 = (bf16[1024,256]{1,0:T(8,128)(2,1)}, bf16[1024,256]{1,0:T(8,128)(2,1)S(1)}, u32[]{:S(2)}, u32[]{:S(2)}) collective-permute-start(bf16[1024,256]{1,0:T(8,128)(2,1)} %collective-permute-done.1), channel_id=1, source_target_pairs={{0,8},{8,0},{1,9},{9,1},{2,10},{10,2},{3,11},{11,3},{4,12},{12,4},... | collective-permute-start | bytes 1572872 | tf_op jit(solution)/shard_map/ppermute | solution.py:316
  44.0 14.8 %collective-permute-start.3 = (bf16[1024,256]{1,0:T(8,128)(2,1)S(1)}, bf16[1024,256]{1,0:T(8,128)(2,1)S(1)}, u32[]{:S(2)}, u32[]{:S(2)}) collective-permute-start(bf16[1024,256]{1,0:T(8,128)(2,1)S(1)} %collective-permute-done.2), channel_id=1, source_target_pairs={{0,32},{32,64},{64,96},{96,0},{1,33},{33,65},{65,97},{97,1},{2,34}... | collective-permute-start | bytes 1572872 | tf_op jit(solution)/shard_map/ppermute | solution.py:316
  44.2 25.8 %collective-permute-start.6 = (bf16[1024,256]{1,0:T(8,128)(2,1)}, bf16[1024,256]{1,0:T(8,128)(2,1)S(1)}, u32[]{:S(2)}, u32[]{:S(2)}) collective-permute-start(bf16[1024,256]{1,0:T(8,128)(2,1)} %collective-permute-done), channel_id=1, source_target_pairs={{0,32},{32,64},{64,96},{96,0},{1,33},{33,65},{65,97},{97,1},{2,34}... | collective-permute-start | bytes 1572872 | tf_op jit(solution)/shard_map/ppermute | solution.py:316
  44.3 26.6 %collective-permute-start.10 = (bf16[1024,256]{1,0:T(8,128)(2,1)S(1)}, bf16[1024,256]{1,0:T(8,128)(2,1)S(1)}, u32[]{:S(2)}, u32[]{:S(2)}) collective-permute-start(bf16[1024,256]{1,0:T(8,128)(2,1)S(1)} %collective-permute-done.2), channel_id=1, source_target_pairs={{0,8},{8,0},{1,9},{9,1},{2,10},{10,2},{3,11},{11,3},{4,12},{12,4},... | collective-permute-start | bytes 1572872 | tf_op jit(solution)/shard_map/ppermute | solution.py:316
  44.8 26.1 %collective-permute-start.5 = (bf16[1024,256]{1,0:T(8,128)(2,1)S(1)}, bf16[1024,256]{1,0:T(8,128)(2,1)}, u32[]{:S(2)}, u32[]{:S(2)}) collective-permute-start(bf16[1024,256]{1,0:T(8,128)(2,1)S(1)} %collective-permute-done.4), channel_id=1, source_target_pairs={{0,96},{32,0},{64,32},{96,64},{1,97},{33,1},{65,33},{97,65},{2,98}... | collective-permute-start | bytes 1572872 | tf_op jit(solution)/shard_map/ppermute | solution.py:316
  47.5 23.9 %collective-permute-start.11 = (bf16[1024,256]{1,0:T(8,128)(2,1)}, bf16[1024,256]{1,0:T(8,128)(2,1)S(1)}, u32[]{:S(2)}, u32[]{:S(2)}) collective-permute-start(bf16[1024,256]{1,0:T(8,128)(2,1)} %collective-permute-done), channel_id=1, source_target_pairs={{0,8},{8,0},{1,9},{9,1},{2,10},{10,2},{3,11},{11,3},{4,12},{12,4},... | collective-permute-start | bytes 1572872 | tf_op jit(solution)/shard_map/ppermute | solution.py:316
  58.8 12.5 %collective-permute-start.9 = (bf16[1024,256]{1,0:T(8,128)(2,1)S(1)}, bf16[1024,256]{1,0:T(8,128)(2,1)S(1)}, u32[]{:S(2)}, u32[]{:S(2)}) collective-permute-start(bf16[1024,256]{1,0:T(8,128)(2,1)S(1)} %collective-permute-done.3), channel_id=1, source_target_pairs={{0,8},{8,0},{1,9},{9,1},{2,10},{10,2},{3,11},{11,3},{4,12},{12,4},... | collective-permute-start | bytes 1572872 | tf_op jit(solution)/shard_map/ppermute | solution.py:316
  70.0 2.3 %collective-permute-start.14 = (bf16[1024,256]{1,0:T(8,128)(2,1)S(1)}, bf16[1024,256]{1,0:T(8,128)(2,1)S(1)}, u32[]{:S(2)}, u32[]{:S(2)}) collective-permute-start(bf16[1024,256]{1,0:T(8,128)(2,1)S(1)} %collective-permute-done.6), channel_id=1, source_target_pairs={{0,8},{8,0},{1,9},{9,1},{2,10},{10,2},{3,11},{11,3},{4,12},{12,4},... | collective-permute-start | bytes 1572872 | tf_op jit(solution)/shard_map/ppermute | solution.py:316
  70.8 3.2 %collective-permute-start.12 = (bf16[1024,256]{1,0:T(8,128)(2,1)S(1)}, bf16[1024,256]{1,0:T(8,128)(2,1)}, u32[]{:S(2)}, u32[]{:S(2)}) collective-permute-start(bf16[1024,256]{1,0:T(8,128)(2,1)S(1)} %collective-permute-done.4), channel_id=1, source_target_pairs={{0,8},{8,0},{1,9},{9,1},{2,10},{10,2},{3,11},{11,3},{4,12},{12,4},... | collective-permute-start | bytes 1572872 | tf_op jit(solution)/shard_map/ppermute | solution.py:316
  70.9 3.3 %collective-permute-start.13 = (bf16[1024,256]{1,0:T(8,128)(2,1)}, bf16[1024,256]{1,0:T(8,128)(2,1)}, u32[]{:S(2)}, u32[]{:S(2)}) collective-permute-start(bf16[1024,256]{1,0:T(8,128)(2,1)} %collective-permute-done.5), channel_id=1, source_target_pairs={{0,8},{8,0},{1,9},{9,1},{2,10},{10,2},{3,11},{11,3},{4,12},{12,4},... | collective-permute-start | bytes 1572872 | tf_op jit(solution)/shard_map/ppermute | solution.py:316
  101.6 28.4 %collective-permute-start.19 = (bf16[128,1024]{1,0:T(8,128)(2,1)S(1)}, bf16[128,1024]{1,0:T(8,128)(2,1)S(1)}, u32[]{:S(2)}, u32[]{:S(2)}) collective-permute-start(bf16[128,1024]{1,0:T(8,128)(2,1)S(1)} %get-tuple-element.33), channel_id=1, source_target_pairs={{0,4},{1,5},{2,6},{3,7},{4,0},{5,1},{6,2},{7,3},{8,12},{9,13},{10,... | collective-permute-start | bytes 786440 | tf_op jit(solution)/shard_map/ppermute | solution.py:369
  105.0 25.0 %collective-permute-start.18 = (bf16[128,1024]{1,0:T(8,128)(2,1)S(1)}, bf16[128,1024]{1,0:T(8,128)(2,1)S(1)}, u32[]{:S(2)}, u32[]{:S(2)}) collective-permute-start(bf16[128,1024]{1,0:T(8,128)(2,1)S(1)} %get-tuple-element.34), channel_id=1, source_target_pairs={{0,2},{1,3},{2,0},{3,1},{4,6},{5,7},{6,4},{7,5},{8,10},{9,11},{10,... | collective-permute-start | bytes 786440 | tf_op jit(solution)/shard_map/ppermute | solution.py:369
  107.5 22.5 %collective-permute-start.17 = (bf16[128,1024]{1,0:T(8,128)(2,1)S(1)}, bf16[128,1024]{1,0:T(8,128)(2,1)S(1)}, u32[]{:S(2)}, u32[]{:S(2)}) collective-permute-start(bf16[128,1024]{1,0:T(8,128)(2,1)S(1)} %get-tuple-element.35), channel_id=1, source_target_pairs={{0,7},{1,4},{2,5},{3,6},{4,3},{5,0},{6,1},{7,2},{8,15},{9,12},{10,... | collective-permute-start | bytes 786440 | tf_op jit(solution)/shard_map/ppermute | solution.py:369
  108.2 21.9 %collective-permute-start.16 = (bf16[128,1024]{1,0:T(8,128)(2,1)S(1)}, bf16[128,1024]{1,0:T(8,128)(2,1)S(1)}, u32[]{:S(2)}, u32[]{:S(2)}) collective-permute-start(bf16[128,1024]{1,0:T(8,128)(2,1)S(1)} %get-tuple-element.36), channel_id=1, source_target_pairs={{0,5},{1,6},{2,7},{3,4},{4,1},{5,2},{6,3},{7,0},{8,13},{9,14},{10,... | collective-permute-start | bytes 786440 | tf_op jit(solution)/shard_map/ppermute | solution.py:369
  111.4 20.7 %collective-permute-start.15 = (bf16[128,1024]{1,0:T(8,128)(2,1)S(1)}, bf16[128,1024]{1,0:T(8,128)(2,1)S(1)}, u32[]{:S(2)}, u32[]{:S(2)}) collective-permute-start(bf16[128,1024]{1,0:T(8,128)(2,1)S(1)} %get-tuple-element.37), channel_id=1, source_target_pairs={{0,6},{1,7},{2,4},{3,5},{4,2},{5,3},{6,0},{7,1},{8,14},{9,15},{10,... | collective-permute-start | bytes 786440 | tf_op jit(solution)/shard_map/ppermute | solution.py:369
  132.9 7.3 %collective-permute-start.21 = (bf16[128,1024]{1,0:T(8,128)(2,1)S(1)}, bf16[128,1024]{1,0:T(8,128)(2,1)S(1)}, u32[]{:S(2)}, u32[]{:S(2)}) collective-permute-start(bf16[128,1024]{1,0:T(8,128)(2,1)S(1)} %get-tuple-element.39), channel_id=1, source_target_pairs={{0,3},{1,0},{2,1},{3,2},{4,7},{5,4},{6,5},{7,6},{8,11},{9,8},{10,9... | collective-permute-start | bytes 786440 | tf_op jit(solution)/shard_map/ppermute | solution.py:369
  132.9 8.5 %collective-permute-start.20 = (bf16[128,1024]{1,0:T(8,128)(2,1)S(1)}, bf16[128,1024]{1,0:T(8,128)(2,1)S(1)}, u32[]{:S(2)}, u32[]{:S(2)}) collective-permute-start(bf16[128,1024]{1,0:T(8,128)(2,1)S(1)} %get-tuple-element.40), channel_id=1, source_target_pairs={{0,1},{1,2},{2,3},{3,0},{4,5},{5,6},{6,7},{7,4},{8,9},{9,10},{10,1... | collective-permute-start | bytes 786440 | tf_op jit(solution)/shard_map/ppermute | solution.py:369
  (20 other events, 273.4 us)

commit v5 on v4

--- a/solution.py
+++ b/solution.py
@@ -18,6 +18,24 @@
 PIECE = 512
 WAVE = 8
 FIRST_STEPS = 5
+
+
+def pack_kernel(keys, values, out):
+    for h in range(out.shape[0]):
+        at = slice(h * HEAD_DIM, (h + 1) * HEAD_DIM)
+        out[h, :, :HEAD_DIM] = keys[:, at]
+        out[h, :, HEAD_DIM:] = values[:, at].T
+
+
+def pack(keys, values, parts):
+    tokens = keys.shape[0]
+    vmem = pl.BlockSpec(memory_space=pltpu.VMEM)
+    return pl.pallas_call(
+        pack_kernel,
+        in_specs=[vmem, vmem],
+        out_specs=vmem,
+        out_shape=jax.ShapeDtypeStruct((parts, tokens, 2 * HEAD_DIM), keys.dtype),
+    )(keys, values)
 
 
 def plan_kernel(place_ref, codes_ref, counts_ref, list_ref, fill_ref, *, blocks, sizes, zero, far):
@@ -319,13 +337,13 @@
 def gather_shards(own):
     across = shift(own, "y_lo", 1)
     up, down = shift(own, "x", -1), shift(own, "x", 1)
-    across, up, down = lax.optimization_barrier((across, up, down))
-    here = [own, up, None, down]
-    here[2] = shift(here[3], "x", 1)
+    here = [own, up, shift(down, "x", 1), down]
     there = [across, shift(across, "x", -1), None, shift(across, "x", 1)]
+    up_too, down_too = shift(up, "core", 1), shift(down, "core", 1)
+    there[1], up_too, down_too = lax.optimization_barrier((there[1], up_too, down_too))
     there[2] = shift(there[1], "x", -1)
-    near = here + there
-    return near + [shift(piece, "core", 1) for piece in near]
+    other = [shift(own, "core", 1), up_too, shift(here[2], "core", 1), down_too]
+    return here + there + other + [shift(piece, "core", 1) for piece in there]
 
 
 def local(queries, keys, values, live_keys, live_count):
@@ -342,9 +360,7 @@
     def cut(array):
         return array.reshape(tokens, parts, -1)
 
-    own = exchange(
-        jnp.concatenate([cut(keys).transpose(1, 0, 2), cut(values).transpose(1, 2, 0)], axis=2)
-    )
+    own = exchange(pack(keys, values, parts))
     y_size, z_size = (lax.axis_size(axis) for axis in head_axes)
     far = [(dy, dz) for dy in range(y_size) for dz in range(z_size)]
     far.sort(key=lambda d: (d[0] + min(d[1], z_size - d[1]), d[0]), reverse=True)

time: 145 us -> 141 us (0.972); the launches traced: 145 us -> 139 us
  waiting for transfers between devices: 23.4 us -> 30.2 us
  starting transfers between devices: 57.4 us -> 52.3 us
  Pallas kernels: 55.6 us -> 50.8 us
  local copies, waits for them, and re-layouts: 7.52 us -> 5.19 us
    pallas_call x2, Pallas kernels: 45.2 us -> 39 us  [attend(): pl.pallas_call(functools.partial(attend_kernel, blocks=blocks, steps=step...]
    ppermute x15, starting transfers between devices: 29.7 us -> 24.1 us  [shift(): lax.ppermute(array, axis, [(i, (i + step) % size) for i in range(size)])]
    ppermute x15, waiting for transfers between devices: 14.4 us -> 18.9 us  [shift(): lax.ppermute(array, axis, [(i, (i + step) % size) for i in range(size)])]
    ppermute x7, waiting for transfers between devices: 8.99 us -> 11.3 us  [send(): part = lax.ppermute(part, head_axes, pairs)]
    pallas_call x0 -> x1, Pallas kernels: none -> 2.11 us  [pack(): pl.pallas_call(pack_kernel, in_specs=[vmem, vmem], out_specs=vmem, out_sh...]
    unnamed x42, local copies, waits for them, and re-layouts: 3.95 us -> 2 us
  transfers between devices with their start and end apart: 24 -> 24, of which waited for: 9 -> 10; matrix products, arithmetic and copies ran while one was open for 1% -> 2% of each run, Pallas kernels for 18% -> 16%
where the time goes in v5:
time: 141 us; the launch traced here: 139 us
  starting transfers between devices  52.3 us (37%)
  Pallas kernels  50.8 us (36%)
  waiting for transfers between devices  30.2 us (21%)
  local copies, waits for them, and re-layouts  5.19 us (4%)
    pallas_call x2, Pallas kernels, attend(): pl.pallas_call(functools.partial(attend_kernel, blocks=blocks, steps=step...  39 us
    ppermute x15, starting transfers between devices, shift(): lax.ppermute(array, axis, [(i, (i + step) % size) for i in range(size)])  24.1 us
    ppermute x15, waiting for transfers between devices, shift(): lax.ppermute(array, axis, [(i, (i + step) % size) for i in range(size)])  18.9 us
    all_to_all x2, starting transfers between devices, exchange(): lax.all_to_all(cut, head_axes, split_axis=0, concat_axis=0, tiled=True)  15.7 us
    ppermute x7, starting transfers between devices, send(): part = lax.ppermute(part, head_axes, pairs)  12.5 us
    ppermute x7, waiting for transfers between devices, send(): part = lax.ppermute(part, head_axes, pairs)  11.3 us
    pallas_call x1, Pallas kernels, plan(): pl.pallas_call(functools.partial(plan_kernel, blocks=blocks, sizes=sizes,...  6.81 us
    pallas_call x1, Pallas kernels, assemble(): pl.pallas_call(assemble_kernel, in_specs=[pl.BlockSpec(memory_space=pltpu...  2.89 us
  transfers between devices with their start and end apart: 24, of which 10 were waited for; matrix products, arithmetic and copies ran while one was open for 2% of the time, Pallas kernels for 16%

profile of v5, /device:TPU:1, one launch (start us, length us, event | category | flops | bytes accessed | tf_op | source)
XLA Modules:
  0.0 138.8 jit_solution(8193316170605794054)
XLA Ops:
  0.0 2.1 %shard_map.55 = bf16[8,128,256]{2,1,0:T(8,128)(2,1)} custom-call(bf16[128,1024]{1,0:T(8,128)(2,1)} %keys.1, bf16[128,1024]{1,0:T(8,128)(2,1)} %values.1), custom_call_target="tpu_custom_call" | custom-call | tf_op jit(solution)/shard_map/pallas_call | solution.py:33
  2.1 8.5 %all-to-all-start = ((bf16[8,128,256]{2,1,0:T(8,128)(2,1)}), bf16[8,128,256]{2,1,0:T(8,128)(2,1)S(1)}, u32[]{:S(2)}, u32[]{:S(2)}) async-start(bf16[8,128,256]{2,1,0:T(8,128)(2,1)} %shard_map.55), calls=%async_computation | async-start | bytes 1048576 | tf_op jit(solution)/shard_map/all_to_all | solution.py:357
  10.6 1.6 %copy.9 = bf16[16,8,8,1024]{3,2,0,1:T(8,128)(2,1)} copy(bf16[16,8,8,1024]{3,2,1,0:T(8,128)(2,1)S(1)} %bitcast.33) | data formatting | bytes 4194304 | tf_op jit(solution)/shard_map/reshape | solution.py:361
  12.8 6.8 %shard_map.56.listed = s32[19,132]{1,0:T(8,128)} custom-call(s32[5]{0:T(128)} %stack.23.place_ref, s32[16,16,16]{2,1,0:T(8,128)} %codes_ref.1, s32[16,16]{1,0:T(8,128)} %counts_ref.1), custom_call_target="tpu_custom_call" | custom-call | bytes 20000000 | tf_op jit(solution)/shard_map/pallas_call | solution.py:94
  20.1 2.0 %collective-permute-start.1 = (bf16[1024,256]{1,0:T(8,128)(2,1)S(1)}, bf16[1024,256]{1,0:T(8,128)(2,1)}, u32[]{:S(2)}, u32[]{:S(2)}) collective-permute-start(bf16[1024,256]{1,0:T(8,128)(2,1)S(1)} %bitcast.35), channel_id=1, source_target_pairs={{0,32},{32,64},{64,96},{96,0},{1,33},{33,65},{65,97},{97,1},{2,34}... | collective-permute-start | bytes 1572872 | tf_op jit(solution)/shard_map/ppermute | solution.py:334
  22.8 7.2 %all-to-all-start.1 = ((bf16[8,128,1024]{2,1,0:T(8,128)(2,1)}), bf16[8,128,1024]{2,1,0:T(8,128)(2,1)S(1)}, u32[]{:S(2)}, u32[]{:S(2)}) async-start(bf16[8,128,1024]{2,1,0:T(8,128)(2,1)} %bitcast.32), calls=%async_computation.1 | async-start | bytes 4194304 | tf_op jit(solution)/shard_map/all_to_all | solution.py:357
  30.4 2.1 %collective-permute-start.4 = (bf16[1024,256]{1,0:T(8,128)(2,1)S(1)}, bf16[1024,256]{1,0:T(8,128)(2,1)S(1)}, u32[]{:S(2)}, u32[]{:S(2)}) collective-permute-start(bf16[1024,256]{1,0:T(8,128)(2,1)S(1)} %collective-permute-done.3), channel_id=1, source_target_pairs={{0,96},{32,0},{64,32},{96,64},{1,97},{33,1},{65,33},{97,65},{2,98}... | collective-permute-start | bytes 1572872 | tf_op jit(solution)/shard_map/ppermute | solution.py:334
  32.6 7.6 %collective-permute-start.6 = (bf16[1024,256]{1,0:T(8,128)(2,1)}, bf16[1024,256]{1,0:T(8,128)(2,1)S(1)}, u32[]{:S(2)}, u32[]{:S(2)}) collective-permute-start(bf16[1024,256]{1,0:T(8,128)(2,1)} %collective-permute-done.1), channel_id=1, source_target_pairs={{0,8},{8,0},{1,9},{9,1},{2,10},{10,2},{3,11},{11,3},{4,12},{12,4},... | collective-permute-start | bytes 1572872 | tf_op jit(solution)/shard_map/ppermute | solution.py:334
  40.7 2.7 %collective-permute-done.4 = bf16[1024,256]{1,0:T(8,128)(2,1)S(1)} collective-permute-done((bf16[1024,256]{1,0:T(8,128)(2,1)S(1)}, bf16[1024,256]{1,0:T(8,128)(2,1)S(1)}, u32[]{:S(2)}, u32[]{:S(2)}) %collective-permute-start.4) | collective-permute-done | bytes 524320 | tf_op jit(solution)/shard_map/ppermute | solution.py:334
  43.8 2.4 %collective-permute-start.7 = (bf16[1024,256]{1,0:T(8,128)(2,1)S(1)}, bf16[1024,256]{1,0:T(8,128)(2,1)}, u32[]{:S(2)}, u32[]{:S(2)}) collective-permute-start(bf16[1024,256]{1,0:T(8,128)(2,1)S(1)} %collective-permute-done.4), channel_id=1, source_target_pairs={{0,96},{32,0},{64,32},{96,64},{1,97},{33,1},{65,33},{97,65},{2,98}... | collective-permute-start | bytes 1572872 | tf_op jit(solution)/shard_map/ppermute | solution.py:334
  46.2 5.3 %collective-permute-start.11 = (bf16[1024,256]{1,0:T(8,128)(2,1)S(1)}, bf16[1024,256]{1,0:T(8,128)(2,1)S(1)}, u32[]{:S(2)}, u32[]{:S(2)}) collective-permute-start(bf16[1024,256]{1,0:T(8,128)(2,1)S(1)} %collective-permute-done.3), channel_id=1, source_target_pairs={{0,8},{8,0},{1,9},{9,1},{2,10},{10,2},{3,11},{11,3},{4,12},{12,4},... | collective-permute-start | bytes 1572872 | tf_op jit(solution)/shard_map/ppermute | solution.py:334
  51.5 3.9 %collective-permute-done.8 = bf16[1024,256]{1,0:T(8,128)(2,1)S(1)} collective-permute-done((bf16[1024,256]{1,0:T(8,128)(2,1)S(1)}, bf16[1024,256]{1,0:T(8,128)(2,1)S(1)}, u32[]{:S(2)}, u32[]{:S(2)}) %collective-permute-start.8) | collective-permute-done | bytes 524320 | tf_op jit(solution)/shard_map/ppermute | solution.py:334
  55.4 1.3 collective-permute-start.14
  56.7 9.9 %collective-permute-done.2 = bf16[1024,256]{1,0:T(8,128)(2,1)S(1)} collective-permute-done((bf16[1024,256]{1,0:T(8,128)(2,1)}, bf16[1024,256]{1,0:T(8,128)(2,1)S(1)}, u32[]{:S(2)}, u32[]{:S(2)}) %collective-permute-start.2) | collective-permute-done | bytes 524320 | tf_op jit(solution)/shard_map/ppermute | solution.py:334
  71.3 24.2 %shard_map.57 = (bf16[640,1024]{1,0:T(8,128)(2,1)S(1)}, bf16[129,128,256]{2,1,0:T(8,128)(2,1)S(1)}) custom-call(s32[19,132]{1,0:T(8,128)S(1)} %copy-done, bf16[1024,1024]{1,0:T(8,128)(2,1)S(1)} %bitcast.30, bf16[8,128,256]{2,1,0:T(8,128)(2,1)} %copy-done.2, bf16[8,128,256]{2,1,0:T(8,128)(2,1)} %bitcast.9.refs_1_, bf16[8,128,256]{2,1,0:T(8,128)(2,1)} %bitcast.44, ...), custom_call_target="tpu_custom_call" | custom-call | flops 22145925120 | bytes 6000000 | tf_op jit(solution)/shard_map/pallas_call | solution.py:285
  95.7 2.2 %collective-permute-start.19 = (bf16[128,1024]{1,0:T(8,128)(2,1)S(1)}, bf16[128,1024]{1,0:T(8,128)(2,1)S(1)}, u32[]{:S(2)}, u32[]{:S(2)}) collective-permute-start(bf16[128,1024]{1,0:T(8,128)(2,1)S(1)} %get-tuple-element.33), channel_id=1, source_target_pairs={{0,4},{1,5},{2,6},{3,7},{4,0},{5,1},{6,2},{7,3},{8,12},{9,13},{10,... | collective-permute-start | bytes 786440 | tf_op jit(solution)/shard_map/ppermute | solution.py:385
  97.9 4.3 %collective-permute-start.18 = (bf16[128,1024]{1,0:T(8,128)(2,1)S(1)}, bf16[128,1024]{1,0:T(8,128)(2,1)S(1)}, u32[]{:S(2)}, u32[]{:S(2)}) collective-permute-start(bf16[128,1024]{1,0:T(8,128)(2,1)S(1)} %get-tuple-element.34), channel_id=1, source_target_pairs={{0,2},{1,3},{2,0},{3,1},{4,6},{5,7},{6,4},{7,5},{8,10},{9,11},{10,... | collective-permute-start | bytes 786440 | tf_op jit(solution)/shard_map/ppermute | solution.py:385
  102.3 3.8 %collective-permute-start.16 = (bf16[128,1024]{1,0:T(8,128)(2,1)S(1)}, bf16[128,1024]{1,0:T(8,128)(2,1)S(1)}, u32[]{:S(2)}, u32[]{:S(2)}) collective-permute-start(bf16[128,1024]{1,0:T(8,128)(2,1)S(1)} %get-tuple-element.36), channel_id=1, source_target_pairs={{0,5},{1,6},{2,7},{3,4},{4,1},{5,2},{6,3},{7,0},{8,13},{9,14},{10,... | collective-permute-start | bytes 786440 | tf_op jit(solution)/shard_map/ppermute | solution.py:385
  106.1 14.8 %shard_map.58 = bf16[384,1024]{1,0:T(8,128)(2,1)S(1)} custom-call(s32[19,132]{1,0:T(8,128)S(1)} %copy-done, bf16[1024,1024]{1,0:T(8,128)(2,1)S(1)} %bitcast.31, bf16[129,128,256]{2,1,0:T(8,128)(2,1)S(1)} %get-tuple-element.25.refs_0_), custom_call_target="tpu_custom_call" | custom-call | flops 13287555072 | bytes 6000000 | tf_op jit(solution)/shard_map/pallas_call | solution.py:285
  120.9 2.7 %collective-permute-done.15.refs_0_ = bf16[128,1024]{1,0:T(8,128)(2,1)S(1)} collective-permute-done((bf16[128,1024]{1,0:T(8,128)(2,1)S(1)}, bf16[128,1024]{1,0:T(8,128)(2,1)S(1)}, u32[]{:S(2)}, u32[]{:S(2)}) %collective-permute-start.15) | collective-permute-done | bytes 262176 | tf_op jit(solution)/shard_map/ppermute | solution.py:385
  124.5 2.1 %collective-permute-start.21 = (bf16[128,1024]{1,0:T(8,128)(2,1)S(1)}, bf16[128,1024]{1,0:T(8,128)(2,1)S(1)}, u32[]{:S(2)}, u32[]{:S(2)}) collective-permute-start(bf16[128,1024]{1,0:T(8,128)(2,1)S(1)} %get-tuple-element.39), channel_id=1, source_target_pairs={{0,3},{1,0},{2,1},{3,2},{4,7},{5,4},{6,5},{7,6},{8,11},{9,8},{10,9... | collective-permute-start | bytes 786440 | tf_op jit(solution)/shard_map/ppermute | solution.py:385
  126.6 5.5 %collective-permute-done.21.refs_6_ = bf16[128,1024]{1,0:T(8,128)(2,1)S(1)} collective-permute-done((bf16[128,1024]{1,0:T(8,128)(2,1)S(1)}, bf16[128,1024]{1,0:T(8,128)(2,1)S(1)}, u32[]{:S(2)}, u32[]{:S(2)}) %collective-permute-start.21) | collective-permute-done | bytes 262176 | tf_op jit(solution)/shard_map/ppermute | solution.py:385
  132.1 3.1 %collective-permute-done.20.refs_5_ = bf16[128,1024]{1,0:T(8,128)(2,1)S(1)} collective-permute-done((bf16[128,1024]{1,0:T(8,128)(2,1)S(1)}, bf16[128,1024]{1,0:T(8,128)(2,1)S(1)}, u32[]{:S(2)}, u32[]{:S(2)}) %collective-permute-start.20) | collective-permute-done | bytes 262176 | tf_op jit(solution)/shard_map/ppermute | solution.py:385
  135.9 2.9 %shard_map.59 = bf16[128,8192]{1,0:T(8,128)(2,1)} custom-call(s32[19,132]{1,0:T(8,128)} %shard_map.56.listed, bf16[128,1024]{1,0:T(8,128)(2,1)} %copy-done.7, bf16[128,1024]{1,0:T(8,128)(2,1)} %copy-done.6, bf16[128,1024]{1,0:T(8,128)(2,1)} %copy-done.5, bf16[128,1024]{1,0:T(8,128)(2,1)} %copy-done.4, bf16[128,1024]{1,0:T(8,128)(2,1)} %copy-done.3, ...), custom_call_target="tpu_custom_call" | custom-call | tf_op jit(solution)/shard_map/pallas_call | solution.py:323
  (75 shorter events, 9.4 us)
Async XLA Ops:
  2.1 17.5 %all-to-all-start = ((bf16[8,128,256]{2,1,0:T(8,128)(2,1)}), bf16[8,128,256]{2,1,0:T(8,128)(2,1)S(1)}, u32[]{:S(2)}, u32[]{:S(2)}) async-start(bf16[8,128,256]{2,1,0:T(8,128)(2,1)} %shard_map.55), calls=%async_computation | async-start | bytes 1048576 | tf_op jit(solution)/shard_map/all_to_all | solution.py:357
  19.7 10.7 %collective-permute-start.3 = (bf16[1024,256]{1,0:T(8,128)(2,1)S(1)}, bf16[1024,256]{1,0:T(8,128)(2,1)S(1)}, u32[]{:S(2)}, u32[]{:S(2)}) collective-permute-start(bf16[1024,256]{1,0:T(8,128)(2,1)S(1)} %bitcast.34), channel_id=1, source_target_pairs={{0,16},{16,0},{1,17},{17,1},{2,18},{18,2},{3,19},{19,3},{4,20},{20... | collective-permute-start | bytes 1572872 | tf_op jit(solution)/shard_map/ppermute | solution.py:334
  20.1 12.5 %collective-permute-start.1 = (bf16[1024,256]{1,0:T(8,128)(2,1)S(1)}, bf16[1024,256]{1,0:T(8,128)(2,1)}, u32[]{:S(2)}, u32[]{:S(2)}) collective-permute-start(bf16[1024,256]{1,0:T(8,128)(2,1)S(1)} %bitcast.35), channel_id=1, source_target_pairs={{0,32},{32,64},{64,96},{96,0},{1,33},{33,65},{65,97},{97,1},{2,34}... | collective-permute-start | bytes 1572872 | tf_op jit(solution)/shard_map/ppermute | solution.py:334
  22.0 18.1 %collective-permute-start = (bf16[1024,256]{1,0:T(8,128)(2,1)S(1)}, bf16[1024,256]{1,0:T(8,128)(2,1)}, u32[]{:S(2)}, u32[]{:S(2)}) collective-permute-start(bf16[1024,256]{1,0:T(8,128)(2,1)S(1)} %bitcast.36), channel_id=1, source_target_pairs={{0,96},{32,0},{64,32},{96,64},{1,97},{33,1},{65,33},{97,65},{2,98}... | collective-permute-start | bytes 1572872 | tf_op jit(solution)/shard_map/ppermute | solution.py:334
  22.8 47.7 %all-to-all-start.1 = ((bf16[8,128,1024]{2,1,0:T(8,128)(2,1)}), bf16[8,128,1024]{2,1,0:T(8,128)(2,1)S(1)}, u32[]{:S(2)}, u32[]{:S(2)}) async-start(bf16[8,128,1024]{2,1,0:T(8,128)(2,1)} %bitcast.32), calls=%async_computation.1 | async-start | bytes 4194304 | tf_op jit(solution)/shard_map/all_to_all | solution.py:357
  30.4 13.0 %collective-permute-start.4 = (bf16[1024,256]{1,0:T(8,128)(2,1)S(1)}, bf16[1024,256]{1,0:T(8,128)(2,1)S(1)}, u32[]{:S(2)}, u32[]{:S(2)}) collective-permute-start(bf16[1024,256]{1,0:T(8,128)(2,1)S(1)} %collective-permute-done.3), channel_id=1, source_target_pairs={{0,96},{32,0},{64,32},{96,64},{1,97},{33,1},{65,33},{97,65},{2,98}... | collective-permute-start | bytes 1572872 | tf_op jit(solution)/shard_map/ppermute | solution.py:334
  32.6 11.2 %collective-permute-start.6 = (bf16[1024,256]{1,0:T(8,128)(2,1)}, bf16[1024,256]{1,0:T(8,128)(2,1)S(1)}, u32[]{:S(2)}, u32[]{:S(2)}) collective-permute-start(bf16[1024,256]{1,0:T(8,128)(2,1)} %collective-permute-done.1), channel_id=1, source_target_pairs={{0,8},{8,0},{1,9},{9,1},{2,10},{10,2},{3,11},{11,3},{4,12},{12,4},... | collective-permute-start | bytes 1572872 | tf_op jit(solution)/shard_map/ppermute | solution.py:334
  40.2 3.6 %collective-permute-start.5 = (bf16[1024,256]{1,0:T(8,128)(2,1)}, bf16[1024,256]{1,0:T(8,128)(2,1)S(1)}, u32[]{:S(2)}, u32[]{:S(2)}) collective-permute-start(bf16[1024,256]{1,0:T(8,128)(2,1)} %collective-permute-done), channel_id=1, source_target_pairs={{0,8},{8,0},{1,9},{9,1},{2,10},{10,2},{3,11},{11,3},{4,12},{12,4},... | collective-permute-start | bytes 1572872 | tf_op jit(solution)/shard_map/ppermute | solution.py:334
  40.3 27.2 %collective-permute-start.9 = (bf16[1024,256]{1,0:T(8,128)(2,1)S(1)}, bf16[1024,256]{1,0:T(8,128)(2,1)S(1)}, u32[]{:S(2)}, u32[]{:S(2)}) collective-permute-start(bf16[1024,256]{1,0:T(8,128)(2,1)S(1)} %bitcast.37), channel_id=1, source_target_pairs={{0,8},{8,0},{1,9},{9,1},{2,10},{10,2},{3,11},{11,3},{4,12},{12,4},... | collective-permute-start | bytes 1572872 | tf_op jit(solution)/shard_map/ppermute | solution.py:334
  40.7 14.7 %collective-permute-start.8 = (bf16[1024,256]{1,0:T(8,128)(2,1)S(1)}, bf16[1024,256]{1,0:T(8,128)(2,1)S(1)}, u32[]{:S(2)}, u32[]{:S(2)}) collective-permute-start(bf16[1024,256]{1,0:T(8,128)(2,1)S(1)} %collective-permute-done.3), channel_id=1, source_target_pairs={{0,32},{32,64},{64,96},{96,0},{1,33},{33,65},{65,97},{97,1},{2,34}... | collective-permute-start | bytes 1572872 | tf_op jit(solution)/shard_map/ppermute | solution.py:334
  43.4 23.2 %collective-permute-start.2 = (bf16[1024,256]{1,0:T(8,128)(2,1)}, bf16[1024,256]{1,0:T(8,128)(2,1)S(1)}, u32[]{:S(2)}, u32[]{:S(2)}) collective-permute-start(bf16[1024,256]{1,0:T(8,128)(2,1)} %collective-permute-done.1), channel_id=1, source_target_pairs={{0,32},{32,64},{64,96},{96,0},{1,33},{33,65},{65,97},{97,1},{2,34}... | collective-permute-start | bytes 1572872 | tf_op jit(solution)/shard_map/ppermute | solution.py:334
  43.8 23.8 %collective-permute-start.7 = (bf16[1024,256]{1,0:T(8,128)(2,1)S(1)}, bf16[1024,256]{1,0:T(8,128)(2,1)}, u32[]{:S(2)}, u32[]{:S(2)}) collective-permute-start(bf16[1024,256]{1,0:T(8,128)(2,1)S(1)} %collective-permute-done.4), channel_id=1, source_target_pairs={{0,96},{32,0},{64,32},{96,64},{1,97},{33,1},{65,33},{97,65},{2,98}... | collective-permute-start | bytes 1572872 | tf_op jit(solution)/shard_map/ppermute | solution.py:334
  46.2 21.8 %collective-permute-start.11 = (bf16[1024,256]{1,0:T(8,128)(2,1)S(1)}, bf16[1024,256]{1,0:T(8,128)(2,1)S(1)}, u32[]{:S(2)}, u32[]{:S(2)}) collective-permute-start(bf16[1024,256]{1,0:T(8,128)(2,1)S(1)} %collective-permute-done.3), channel_id=1, source_target_pairs={{0,8},{8,0},{1,9},{9,1},{2,10},{10,2},{3,11},{11,3},{4,12},{12,4},... | collective-permute-start | bytes 1572872 | tf_op jit(solution)/shard_map/ppermute | solution.py:334
  55.4 12.6 %collective-permute-start.14 = (bf16[1024,256]{1,0:T(8,128)(2,1)S(1)}, bf16[1024,256]{1,0:T(8,128)(2,1)S(1)}, u32[]{:S(2)}, u32[]{:S(2)}) collective-permute-start(bf16[1024,256]{1,0:T(8,128)(2,1)S(1)} %collective-permute-done.8), channel_id=1, source_target_pairs={{0,8},{8,0},{1,9},{9,1},{2,10},{10,2},{3,11},{11,3},{4,12},{12,4},... | collective-permute-start | bytes 1572872 | tf_op jit(solution)/shard_map/ppermute | solution.py:334
  66.6 2.4 %collective-permute-start.10 = (bf16[1024,256]{1,0:T(8,128)(2,1)S(1)}, bf16[1024,256]{1,0:T(8,128)(2,1)S(1)}, u32[]{:S(2)}, u32[]{:S(2)}) collective-permute-start(bf16[1024,256]{1,0:T(8,128)(2,1)S(1)} %collective-permute-done.2), channel_id=1, source_target_pairs={{0,8},{8,0},{1,9},{9,1},{2,10},{10,2},{3,11},{11,3},{4,12},{12,4},... | collective-permute-start | bytes 1572872 | tf_op jit(solution)/shard_map/ppermute | solution.py:334
  67.5 3.0 %collective-permute-start.12 = (bf16[1024,256]{1,0:T(8,128)(2,1)S(1)}, bf16[1024,256]{1,0:T(8,128)(2,1)S(1)}, u32[]{:S(2)}, u32[]{:S(2)}) collective-permute-start(bf16[1024,256]{1,0:T(8,128)(2,1)S(1)} %collective-permute-done.4), channel_id=1, source_target_pairs={{0,8},{8,0},{1,9},{9,1},{2,10},{10,2},{3,11},{11,3},{4,12},{12,4},... | collective-permute-start | bytes 1572872 | tf_op jit(solution)/shard_map/ppermute | solution.py:334
  67.6 3.3 %collective-permute-start.13 = (bf16[1024,256]{1,0:T(8,128)(2,1)}, bf16[1024,256]{1,0:T(8,128)(2,1)}, u32[]{:S(2)}, u32[]{:S(2)}) collective-permute-start(bf16[1024,256]{1,0:T(8,128)(2,1)} %collective-permute-done.7), channel_id=1, source_target_pairs={{0,8},{8,0},{1,9},{9,1},{2,10},{10,2},{3,11},{11,3},{4,12},{12,4},... | collective-permute-start | bytes 1572872 | tf_op jit(solution)/shard_map/ppermute | solution.py:334
  95.7 25.1 %collective-permute-start.19 = (bf16[128,1024]{1,0:T(8,128)(2,1)S(1)}, bf16[128,1024]{1,0:T(8,128)(2,1)S(1)}, u32[]{:S(2)}, u32[]{:S(2)}) collective-permute-start(bf16[128,1024]{1,0:T(8,128)(2,1)S(1)} %get-tuple-element.33), channel_id=1, source_target_pairs={{0,4},{1,5},{2,6},{3,7},{4,0},{5,1},{6,2},{7,3},{8,12},{9,13},{10,... | collective-permute-start | bytes 786440 | tf_op jit(solution)/shard_map/ppermute | solution.py:385
  97.9 23.0 %collective-permute-start.18 = (bf16[128,1024]{1,0:T(8,128)(2,1)S(1)}, bf16[128,1024]{1,0:T(8,128)(2,1)S(1)}, u32[]{:S(2)}, u32[]{:S(2)}) collective-permute-start(bf16[128,1024]{1,0:T(8,128)(2,1)S(1)} %get-tuple-element.34), channel_id=1, source_target_pairs={{0,2},{1,3},{2,0},{3,1},{4,6},{5,7},{6,4},{7,5},{8,10},{9,11},{10,... | collective-permute-start | bytes 786440 | tf_op jit(solution)/shard_map/ppermute | solution.py:385
  102.2 18.7 %collective-permute-start.17 = (bf16[128,1024]{1,0:T(8,128)(2,1)S(1)}, bf16[128,1024]{1,0:T(8,128)(2,1)S(1)}, u32[]{:S(2)}, u32[]{:S(2)}) collective-permute-start(bf16[128,1024]{1,0:T(8,128)(2,1)S(1)} %get-tuple-element.35), channel_id=1, source_target_pairs={{0,7},{1,4},{2,5},{3,6},{4,3},{5,0},{6,1},{7,2},{8,15},{9,12},{10,... | collective-permute-start | bytes 786440 | tf_op jit(solution)/shard_map/ppermute | solution.py:385
  102.3 18.7 %collective-permute-start.16 = (bf16[128,1024]{1,0:T(8,128)(2,1)S(1)}, bf16[128,1024]{1,0:T(8,128)(2,1)S(1)}, u32[]{:S(2)}, u32[]{:S(2)}) collective-permute-start(bf16[128,1024]{1,0:T(8,128)(2,1)S(1)} %get-tuple-element.36), channel_id=1, source_target_pairs={{0,5},{1,6},{2,7},{3,4},{4,1},{5,2},{6,3},{7,0},{8,13},{9,14},{10,... | collective-permute-start | bytes 786440 | tf_op jit(solution)/shard_map/ppermute | solution.py:385
  106.1 17.6 %collective-permute-start.15 = (bf16[128,1024]{1,0:T(8,128)(2,1)S(1)}, bf16[128,1024]{1,0:T(8,128)(2,1)S(1)}, u32[]{:S(2)}, u32[]{:S(2)}) collective-permute-start(bf16[128,1024]{1,0:T(8,128)(2,1)S(1)} %get-tuple-element.37), channel_id=1, source_target_pairs={{0,6},{1,7},{2,4},{3,5},{4,2},{5,3},{6,0},{7,1},{8,14},{9,15},{10,... | collective-permute-start | bytes 786440 | tf_op jit(solution)/shard_map/ppermute | solution.py:385
  124.5 7.6 %collective-permute-start.21 = (bf16[128,1024]{1,0:T(8,128)(2,1)S(1)}, bf16[128,1024]{1,0:T(8,128)(2,1)S(1)}, u32[]{:S(2)}, u32[]{:S(2)}) collective-permute-start(bf16[128,1024]{1,0:T(8,128)(2,1)S(1)} %get-tuple-element.39), channel_id=1, source_target_pairs={{0,3},{1,0},{2,1},{3,2},{4,7},{5,4},{6,5},{7,6},{8,11},{9,8},{10,9... | collective-permute-start | bytes 786440 | tf_op jit(solution)/shard_map/ppermute | solution.py:385
  126.6 8.6 %collective-permute-start.20 = (bf16[128,1024]{1,0:T(8,128)(2,1)S(1)}, bf16[128,1024]{1,0:T(8,128)(2,1)S(1)}, u32[]{:S(2)}, u32[]{:S(2)}) collective-permute-start(bf16[128,1024]{1,0:T(8,128)(2,1)S(1)} %get-tuple-element.40), channel_id=1, source_target_pairs={{0,1},{1,2},{2,3},{3,0},{4,5},{5,6},{6,7},{7,4},{8,9},{9,10},{10,1... | collective-permute-start | bytes 786440 | tf_op jit(solution)/shard_map/ppermute | solution.py:385
  (21 other events, 293.5 us)

commit v6 on v5

--- a/solution.py
+++ b/solution.py
@@ -300,32 +300,38 @@
         out_shape=out_shape,
         compiler_params=pltpu.CompilerParams(vmem_limit_bytes=32 * 1024 * 1024),
         cost_estimate=pl.CostEstimate(flops=pair_estimate * 3, bytes_accessed=6_000_000, transcendentals=0),
-    )(lists, queries, *sources)
+    )(lists, pltpu.with_memory_space_constraint(queries, pltpu.VMEM), *sources)
 
 
 def assemble_kernel(listed, *refs):
-    *parts, out, sem = refs
-    width = parts[0].shape[1]
-    copies = [
-        pltpu.make_async_copy(
-            part, out.at[:, pl.ds(pl.multiple_of(listed[2 * len(parts) + 2, r] * width, width), width)], sem.at[r]
-        )
-        for r, part in enumerate(parts)
-    ]
+    *parts, late, out, sem = refs
+    tokens, width = out.shape[0], late.shape[1]
+    count = out.shape[1] // width
+    copies = []
+    for r in range(count):
+        at = pl.ds(pl.multiple_of(listed[2 * count + 2, r] * width, width), width)
+        source = parts[r] if r < len(parts) else late.at[pl.ds(late.shape[0] - tokens, tokens)]
+        copies.append(pltpu.make_async_copy(source, out.at[:, at], sem.at[r]))
     for copy in copies:
         copy.start()
     for copy in copies:
         copy.wait()
 
 
-def assemble(lists, parts):
+def assemble(lists, parts, late):
     rows, width = parts[0].shape
+    count = len(parts) + 1
+    spaces = [pltpu.HBM] * FIRST_STEPS + [pltpu.VMEM] * (count - FIRST_STEPS)
+    parts = [
+        pltpu.with_memory_space_constraint(part, space)
+        for part, space in zip([*parts, late], spaces, strict=True)
+    ]
     return pl.pallas_call(
         assemble_kernel,
-        in_specs=[pl.BlockSpec(memory_space=pltpu.SMEM)] + [pl.BlockSpec(memory_space=pltpu.VMEM)] * len(parts),
+        in_specs=[pl.BlockSpec(memory_space=pltpu.SMEM)] + [pl.BlockSpec(memory_space=pl.ANY)] * count,
         out_specs=pl.BlockSpec(memory_space=pl.ANY),
-        out_shape=jax.ShapeDtypeStruct((rows, width * len(parts)), parts[0].dtype),
-        scratch_shapes=[pltpu.SemaphoreType.DMA((len(parts),))],
+        out_shape=jax.ShapeDtypeStruct((rows, width * count), late.dtype),
+        scratch_shapes=[pltpu.SemaphoreType.DMA((count,))],
     )(lists, *parts)
 
 
@@ -378,12 +384,8 @@
         sent = []
         for step in range(*steps):
             part = attended[(step - steps[0]) * tokens : (step - steps[0] + 1) * tokens]
-            if any(far[step]):
-                pairs = [
-                    (k, at_distance(k // z_size, k % z_size, *far[step])) for k in range(y_size * z_size)
-                ]
-                part = lax.ppermute(part, head_axes, pairs)
-            sent.append(part)
+            pairs = [(k, at_distance(k // z_size, k % z_size, *far[step])) for k in range(y_size * z_size)]
+            sent.append(lax.ppermute(part, head_axes, pairs))
         return sent
 
     early, late = (0, FIRST_STEPS), (FIRST_STEPS, parts)
@@ -391,8 +393,8 @@
     received = send(attended, early)
     (attended,) = attend(query_local, gathered, lists, late)
     attended, received = lax.optimization_barrier((attended, received))
-    received += send(attended, late)
-    return assemble(lists, received)
+    received += send(attended, (FIRST_STEPS, parts - 1))
+    return assemble(lists, received, attended)
 
 
 def solution(mesh):

time: 141 us -> 180 us (1.28); the launches traced: 139 us -> 180 us
  Pallas kernels: 50.8 us -> 96.8 us
  waiting for transfers between devices: 30.2 us -> 26.7 us
    pallas_call x1, Pallas kernels: 2.89 us -> 41.9 us  [assemble(): pl.pallas_call(assemble_kernel, in_specs=[pl.BlockSpec(memory_space=pltpu...]
    pallas_call x2, Pallas kernels: 39 us -> 45.2 us  [attend(): pl.pallas_call(functools.partial(attend_kernel, blocks=blocks, steps=step...]
    ppermute x7, waiting for transfers between devices: 11.3 us -> 6.44 us  [send(): sent.append(lax.ppermute(part, head_axes, pairs))]
    ppermute x7, starting transfers between devices: 12.5 us -> 14.3 us  [send(): sent.append(lax.ppermute(part, head_axes, pairs))]
  transfers between devices with their start and end apart: 24 -> 24, of which waited for: 10 -> 10; matrix products, arithmetic and copies ran while one was open for 2% -> 1% of each run, Pallas kernels for 16% -> 14%
where the time goes in v6:
time: 180 us
  Pallas kernels  96.8 us (54%)
  starting transfers between devices  52.1 us (29%)
  waiting for transfers between devices  26.7 us (15%)
  local copies, waits for them, and re-layouts  3.73 us (2%)
    pallas_call x2, Pallas kernels, attend(): pl.pallas_call(functools.partial(attend_kernel, blocks=blocks, steps=step...  45.2 us
    pallas_call x1, Pallas kernels, assemble(): pl.pallas_call(assemble_kernel, in_specs=[pl.BlockSpec(memory_space=pltpu...  41.9 us
    ppermute x15, starting transfers between devices, shift(): lax.ppermute(array, axis, [(i, (i + step) % size) for i in range(size)])  22.5 us
    ppermute x15, waiting for transfers between devices, shift(): lax.ppermute(array, axis, [(i, (i + step) % size) for i in range(size)])  20.3 us
    all_to_all x2, starting transfers between devices, exchange(): lax.all_to_all(cut, head_axes, split_axis=0, concat_axis=0, tiled=True)  15.3 us
    ppermute x7, starting transfers between devices, send(): sent.append(lax.ppermute(part, head_axes, pairs))  14.3 us
    pallas_call x1, Pallas kernels, plan(): pl.pallas_call(functools.partial(plan_kernel, blocks=blocks, sizes=sizes,...  7.55 us
    ppermute x7, waiting for transfers between devices, send(): sent.append(lax.ppermute(part, head_axes, pairs))  6.44 us
  transfers between devices with their start and end apart: 24, of which 10 were waited for; matrix products, arithmetic and copies ran while one was open for 1% of the time, Pallas kernels for 14%

profile of v6, /device:TPU:1, one launch (start us, length us, event | category | flops | bytes accessed | tf_op | source)
XLA Modules:
  0.0 179.7 jit_solution(277253897449299626)
XLA Ops:
  0.0 2.1 %shard_map.55 = bf16[8,128,256]{2,1,0:T(8,128)(2,1)} custom-call(bf16[128,1024]{1,0:T(8,128)(2,1)} %keys.1, bf16[128,1024]{1,0:T(8,128)(2,1)} %values.1), custom_call_target="tpu_custom_call" | custom-call | tf_op jit(solution)/shard_map/pallas_call | solution.py:33
  2.1 8.5 %all-to-all-start = ((bf16[8,128,256]{2,1,0:T(8,128)(2,1)}), bf16[8,128,256]{2,1,0:T(8,128)(2,1)S(1)}, u32[]{:S(2)}, u32[]{:S(2)}) async-start(bf16[8,128,256]{2,1,0:T(8,128)(2,1)} %shard_map.55), calls=%async_computation | async-start | bytes 1048576 | tf_op jit(solution)/shard_map/all_to_all | solution.py:363
  10.6 1.6 copy.9
  12.8 7.6 %shard_map.56.listed = s32[19,132]{1,0:T(8,128)} custom-call(s32[5]{0:T(128)} %stack.23.place_ref, s32[16,16,16]{2,1,0:T(8,128)} %codes_ref.1, s32[16,16]{1,0:T(8,128)} %counts_ref.1), custom_call_target="tpu_custom_call" | custom-call | bytes 20000000 | tf_op jit(solution)/shard_map/pallas_call | solution.py:94
  20.5 1.3 collective-permute-start.1
  21.8 1.4 collective-permute-start
  23.3 6.8 %all-to-all-start.1 = ((bf16[8,128,1024]{2,1,0:T(8,128)(2,1)}), bf16[8,128,1024]{2,1,0:T(8,128)(2,1)S(1)}, u32[]{:S(2)}, u32[]{:S(2)}) async-start(bf16[8,128,1024]{2,1,0:T(8,128)(2,1)} %bitcast.32), calls=%async_computation.1 | async-start | bytes 4194304 | tf_op jit(solution)/shard_map/all_to_all | solution.py:363
  30.1 1.8 %collective-permute-done.3 = bf16[1024,256]{1,0:T(8,128)(2,1)S(1)} collective-permute-done((bf16[1024,256]{1,0:T(8,128)(2,1)S(1)}, bf16[1024,256]{1,0:T(8,128)(2,1)S(1)}, u32[]{:S(2)}, u32[]{:S(2)}) %collective-permute-start.3) | collective-permute-done | bytes 524320 | tf_op jit(solution)/shard_map/ppermute | solution.py:340
  33.2 7.1 %collective-permute-start.6 = (bf16[1024,256]{1,0:T(8,128)(2,1)}, bf16[1024,256]{1,0:T(8,128)(2,1)S(1)}, u32[]{:S(2)}, u32[]{:S(2)}) collective-permute-start(bf16[1024,256]{1,0:T(8,128)(2,1)} %collective-permute-done.1), channel_id=1, source_target_pairs={{0,8},{8,0},{1,9},{9,1},{2,10},{10,2},{3,11},{11,3},{4,12},{12,4},... | collective-permute-start | bytes 1572872 | tf_op jit(solution)/shard_map/ppermute | solution.py:340
  40.8 1.7 collective-permute-done.4
  43.5 1.7 collective-permute-start.7
  45.2 6.3 %collective-permute-start.11 = (bf16[1024,256]{1,0:T(8,128)(2,1)S(1)}, bf16[1024,256]{1,0:T(8,128)(2,1)S(1)}, u32[]{:S(2)}, u32[]{:S(2)}) collective-permute-start(bf16[1024,256]{1,0:T(8,128)(2,1)S(1)} %collective-permute-done.3), channel_id=1, source_target_pairs={{0,8},{8,0},{1,9},{9,1},{2,10},{10,2},{3,11},{11,3},{4,12},{12,4},... | collective-permute-start | bytes 1572872 | tf_op jit(solution)/shard_map/ppermute | solution.py:340
  51.5 4.0 %collective-permute-done.8 = bf16[1024,256]{1,0:T(8,128)(2,1)S(1)} collective-permute-done((bf16[1024,256]{1,0:T(8,128)(2,1)S(1)}, bf16[1024,256]{1,0:T(8,128)(2,1)S(1)}, u32[]{:S(2)}, u32[]{:S(2)}) %collective-permute-start.8) | collective-permute-done | bytes 524320 | tf_op jit(solution)/shard_map/ppermute | solution.py:340
  55.5 1.3 collective-permute-start.14
  56.8 9.9 %collective-permute-done.2 = bf16[1024,256]{1,0:T(8,128)(2,1)S(1)} collective-permute-done((bf16[1024,256]{1,0:T(8,128)(2,1)}, bf16[1024,256]{1,0:T(8,128)(2,1)S(1)}, u32[]{:S(2)}, u32[]{:S(2)}) %collective-permute-start.2) | collective-permute-done | bytes 524320 | tf_op jit(solution)/shard_map/ppermute | solution.py:340
  71.4 28.1 %shard_map.57 = (bf16[640,1024]{1,0:T(8,128)(2,1)S(1)}, bf16[129,128,256]{2,1,0:T(8,128)(2,1)S(1)}) custom-call(s32[19,132]{1,0:T(8,128)S(1)} %copy-done.2, bf16[1024,1024]{1,0:T(8,128)(2,1)S(1)} %bitcast.30, bf16[8,128,256]{2,1,0:T(8,128)(2,1)} %copy-done.4, bf16[8,128,256]{2,1,0:T(8,128)(2,1)} %bitcast.9.refs_1_, bf16[8,128,256]{2,1,0:T(8,128)(2,1)} %bitcast.44, ...), custom_call_target="tpu_custom_call" | custom-call | flops 22145925120 | bytes 6000000 | tf_op jit(solution)/shard_map/pallas_call | solution.py:285
  99.6 2.7 %collective-permute-start.19 = (bf16[128,1024]{1,0:T(8,128)(2,1)S(1)}, bf16[128,1024]{1,0:T(8,128)(2,1)S(1)}, u32[]{:S(2)}, u32[]{:S(2)}) collective-permute-start(bf16[128,1024]{1,0:T(8,128)(2,1)S(1)} %get-tuple-element.33), channel_id=1, source_target_pairs={{0,4},{1,5},{2,6},{3,7},{4,0},{5,1},{6,2},{7,3},{8,12},{9,13},{10,... | collective-permute-start | bytes 786440 | tf_op jit(solution)/shard_map/ppermute | solution.py:388
  102.4 3.2 %collective-permute-start.18 = (bf16[128,1024]{1,0:T(8,128)(2,1)S(1)}, bf16[128,1024]{1,0:T(8,128)(2,1)S(1)}, u32[]{:S(2)}, u32[]{:S(2)}) collective-permute-start(bf16[128,1024]{1,0:T(8,128)(2,1)S(1)} %get-tuple-element.34), channel_id=1, source_target_pairs={{0,2},{1,3},{2,0},{3,1},{4,6},{5,7},{6,4},{7,5},{8,10},{9,11},{10,... | collective-permute-start | bytes 786440 | tf_op jit(solution)/shard_map/ppermute | solution.py:388
  106.0 3.4 %collective-permute-start.16 = (bf16[128,1024]{1,0:T(8,128)(2,1)S(1)}, bf16[128,1024]{1,0:T(8,128)(2,1)S(1)}, u32[]{:S(2)}, u32[]{:S(2)}) collective-permute-start(bf16[128,1024]{1,0:T(8,128)(2,1)S(1)} %get-tuple-element.36), channel_id=1, source_target_pairs={{0,5},{1,6},{2,7},{3,4},{4,1},{5,2},{6,3},{7,0},{8,13},{9,14},{10,... | collective-permute-start | bytes 786440 | tf_op jit(solution)/shard_map/ppermute | solution.py:388
  110.4 17.2 %shard_map.58.refs_7_ = bf16[384,1024]{1,0:T(8,128)(2,1)S(1)} custom-call(s32[19,132]{1,0:T(8,128)S(1)} %copy-done.2, bf16[1024,1024]{1,0:T(8,128)(2,1)S(1)} %bitcast.31, bf16[129,128,256]{2,1,0:T(8,128)(2,1)S(1)} %get-tuple-element.25.refs_0_), custom_call_target="tpu_custom_call" | custom-call | flops 13287555072 | bytes 6000000 | tf_op jit(solution)/shard_map/pallas_call | solution.py:285
  127.7 3.5 %collective-permute-start.21 = (bf16[128,1024]{1,0:T(8,128)(2,1)S(1)}, bf16[128,1024]{1,0:T(8,128)(2,1)S(1)}, u32[]{:S(2)}, u32[]{:S(2)}) collective-permute-start(bf16[128,1024]{1,0:T(8,128)(2,1)S(1)} %get-tuple-element.38), channel_id=1, source_target_pairs={{0,3},{1,0},{2,1},{3,2},{4,7},{5,4},{6,5},{7,6},{8,11},{9,8},{10,9... | collective-permute-start | bytes 786440 | tf_op jit(solution)/shard_map/ppermute | solution.py:388
  131.3 3.7 %collective-permute-done.21.refs_6_ = bf16[128,1024]{1,0:T(8,128)(2,1)S(1)} collective-permute-done((bf16[128,1024]{1,0:T(8,128)(2,1)S(1)}, bf16[128,1024]{1,0:T(8,128)(2,1)S(1)}, u32[]{:S(2)}, u32[]{:S(2)}) %collective-permute-start.21) | collective-permute-done | bytes 262176 | tf_op jit(solution)/shard_map/ppermute | solution.py:388
  135.0 2.8 %collective-permute-done.20.refs_5_ = bf16[128,1024]{1,0:T(8,128)(2,1)S(1)} collective-permute-done((bf16[128,1024]{1,0:T(8,128)(2,1)S(1)}, bf16[128,1024]{1,0:T(8,128)(2,1)S(1)}, u32[]{:S(2)}, u32[]{:S(2)}) %collective-permute-start.20) | collective-permute-done | bytes 262176 | tf_op jit(solution)/shard_map/ppermute | solution.py:388
  137.7 41.9 %shard_map.59 = bf16[128,8192]{1,0:T(8,128)(2,1)} custom-call(s32[19,132]{1,0:T(8,128)} %shard_map.56.listed, bf16[128,1024]{1,0:T(8,128)(2,1)} %copy-done.9, bf16[128,1024]{1,0:T(8,128)(2,1)} %copy-done.8, bf16[128,1024]{1,0:T(8,128)(2,1)} %copy-done.7, bf16[128,1024]{1,0:T(8,128)(2,1)} %copy-done.6, bf16[128,1024]{1,0:T(8,128)(2,1)} %copy-done.5, ...), custom_call_target="tpu_custom_call" | custom-call | tf_op jit(solution)/shard_map/pallas_call | solution.py:329
  (75 shorter events, 9.8 us)
Async XLA Ops:
  2.1 18.3 %all-to-all-start = ((bf16[8,128,256]{2,1,0:T(8,128)(2,1)}), bf16[8,128,256]{2,1,0:T(8,128)(2,1)S(1)}, u32[]{:S(2)}, u32[]{:S(2)}) async-start(bf16[8,128,256]{2,1,0:T(8,128)(2,1)} %shard_map.55), calls=%async_computation | async-start | bytes 1048576 | tf_op jit(solution)/shard_map/all_to_all | solution.py:363
  20.4 11.5 %collective-permute-start.3 = (bf16[1024,256]{1,0:T(8,128)(2,1)S(1)}, bf16[1024,256]{1,0:T(8,128)(2,1)S(1)}, u32[]{:S(2)}, u32[]{:S(2)}) collective-permute-start(bf16[1024,256]{1,0:T(8,128)(2,1)S(1)} %bitcast.34), channel_id=1, source_target_pairs={{0,16},{16,0},{1,17},{17,1},{2,18},{18,2},{3,19},{19,3},{4,20},{20... | collective-permute-start | bytes 1572872 | tf_op jit(solution)/shard_map/ppermute | solution.py:340
  20.5 12.7 %collective-permute-start.1 = (bf16[1024,256]{1,0:T(8,128)(2,1)S(1)}, bf16[1024,256]{1,0:T(8,128)(2,1)}, u32[]{:S(2)}, u32[]{:S(2)}) collective-permute-start(bf16[1024,256]{1,0:T(8,128)(2,1)S(1)} %bitcast.35), channel_id=1, source_target_pairs={{0,32},{32,64},{64,96},{96,0},{1,33},{33,65},{65,97},{97,1},{2,34}... | collective-permute-start | bytes 1572872 | tf_op jit(solution)/shard_map/ppermute | solution.py:340
  21.8 18.4 %collective-permute-start = (bf16[1024,256]{1,0:T(8,128)(2,1)S(1)}, bf16[1024,256]{1,0:T(8,128)(2,1)}, u32[]{:S(2)}, u32[]{:S(2)}) collective-permute-start(bf16[1024,256]{1,0:T(8,128)(2,1)S(1)} %bitcast.36), channel_id=1, source_target_pairs={{0,96},{32,0},{64,32},{96,64},{1,97},{33,1},{65,33},{97,65},{2,98}... | collective-permute-start | bytes 1572872 | tf_op jit(solution)/shard_map/ppermute | solution.py:340
  23.3 47.3 %all-to-all-start.1 = ((bf16[8,128,1024]{2,1,0:T(8,128)(2,1)}), bf16[8,128,1024]{2,1,0:T(8,128)(2,1)S(1)}, u32[]{:S(2)}, u32[]{:S(2)}) async-start(bf16[8,128,1024]{2,1,0:T(8,128)(2,1)} %bitcast.32), calls=%async_computation.1 | async-start | bytes 4194304 | tf_op jit(solution)/shard_map/all_to_all | solution.py:363
  31.9 10.6 %collective-permute-start.4 = (bf16[1024,256]{1,0:T(8,128)(2,1)S(1)}, bf16[1024,256]{1,0:T(8,128)(2,1)S(1)}, u32[]{:S(2)}, u32[]{:S(2)}) collective-permute-start(bf16[1024,256]{1,0:T(8,128)(2,1)S(1)} %collective-permute-done.3), channel_id=1, source_target_pairs={{0,96},{32,0},{64,32},{96,64},{1,97},{33,1},{65,33},{97,65},{2,98}... | collective-permute-start | bytes 1572872 | tf_op jit(solution)/shard_map/ppermute | solution.py:340
  33.2 9.4 %collective-permute-start.6 = (bf16[1024,256]{1,0:T(8,128)(2,1)}, bf16[1024,256]{1,0:T(8,128)(2,1)S(1)}, u32[]{:S(2)}, u32[]{:S(2)}) collective-permute-start(bf16[1024,256]{1,0:T(8,128)(2,1)} %collective-permute-done.1), channel_id=1, source_target_pairs={{0,8},{8,0},{1,9},{9,1},{2,10},{10,2},{3,11},{11,3},{4,12},{12,4},... | collective-permute-start | bytes 1572872 | tf_op jit(solution)/shard_map/ppermute | solution.py:340
  40.3 3.2 %collective-permute-start.5 = (bf16[1024,256]{1,0:T(8,128)(2,1)}, bf16[1024,256]{1,0:T(8,128)(2,1)S(1)}, u32[]{:S(2)}, u32[]{:S(2)}) collective-permute-start(bf16[1024,256]{1,0:T(8,128)(2,1)} %collective-permute-done), channel_id=1, source_target_pairs={{0,8},{8,0},{1,9},{9,1},{2,10},{10,2},{3,11},{11,3},{4,12},{12,4},... | collective-permute-start | bytes 1572872 | tf_op jit(solution)/shard_map/ppermute | solution.py:340
  40.3 27.2 %collective-permute-start.9 = (bf16[1024,256]{1,0:T(8,128)(2,1)S(1)}, bf16[1024,256]{1,0:T(8,128)(2,1)S(1)}, u32[]{:S(2)}, u32[]{:S(2)}) collective-permute-start(bf16[1024,256]{1,0:T(8,128)(2,1)S(1)} %bitcast.37), channel_id=1, source_target_pairs={{0,8},{8,0},{1,9},{9,1},{2,10},{10,2},{3,11},{11,3},{4,12},{12,4},... | collective-permute-start | bytes 1572872 | tf_op jit(solution)/shard_map/ppermute | solution.py:340
  40.8 14.7 %collective-permute-start.8 = (bf16[1024,256]{1,0:T(8,128)(2,1)S(1)}, bf16[1024,256]{1,0:T(8,128)(2,1)S(1)}, u32[]{:S(2)}, u32[]{:S(2)}) collective-permute-start(bf16[1024,256]{1,0:T(8,128)(2,1)S(1)} %collective-permute-done.3), channel_id=1, source_target_pairs={{0,32},{32,64},{64,96},{96,0},{1,33},{33,65},{65,97},{97,1},{2,34}... | collective-permute-start | bytes 1572872 | tf_op jit(solution)/shard_map/ppermute | solution.py:340
  42.5 24.2 %collective-permute-start.2 = (bf16[1024,256]{1,0:T(8,128)(2,1)}, bf16[1024,256]{1,0:T(8,128)(2,1)S(1)}, u32[]{:S(2)}, u32[]{:S(2)}) collective-permute-start(bf16[1024,256]{1,0:T(8,128)(2,1)} %collective-permute-done.1), channel_id=1, source_target_pairs={{0,32},{32,64},{64,96},{96,0},{1,33},{33,65},{65,97},{97,1},{2,34}... | collective-permute-start | bytes 1572872 | tf_op jit(solution)/shard_map/ppermute | solution.py:340
  43.5 24.2 %collective-permute-start.7 = (bf16[1024,256]{1,0:T(8,128)(2,1)S(1)}, bf16[1024,256]{1,0:T(8,128)(2,1)}, u32[]{:S(2)}, u32[]{:S(2)}) collective-permute-start(bf16[1024,256]{1,0:T(8,128)(2,1)S(1)} %collective-permute-done.4), channel_id=1, source_target_pairs={{0,96},{32,0},{64,32},{96,64},{1,97},{33,1},{65,33},{97,65},{2,98}... | collective-permute-start | bytes 1572872 | tf_op jit(solution)/shard_map/ppermute | solution.py:340
  45.2 22.9 %collective-permute-start.11 = (bf16[1024,256]{1,0:T(8,128)(2,1)S(1)}, bf16[1024,256]{1,0:T(8,128)(2,1)S(1)}, u32[]{:S(2)}, u32[]{:S(2)}) collective-permute-start(bf16[1024,256]{1,0:T(8,128)(2,1)S(1)} %collective-permute-done.3), channel_id=1, source_target_pairs={{0,8},{8,0},{1,9},{9,1},{2,10},{10,2},{3,11},{11,3},{4,12},{12,4},... | collective-permute-start | bytes 1572872 | tf_op jit(solution)/shard_map/ppermute | solution.py:340
  55.5 12.6 %collective-permute-start.14 = (bf16[1024,256]{1,0:T(8,128)(2,1)S(1)}, bf16[1024,256]{1,0:T(8,128)(2,1)S(1)}, u32[]{:S(2)}, u32[]{:S(2)}) collective-permute-start(bf16[1024,256]{1,0:T(8,128)(2,1)S(1)} %collective-permute-done.8), channel_id=1, source_target_pairs={{0,8},{8,0},{1,9},{9,1},{2,10},{10,2},{3,11},{11,3},{4,12},{12,4},... | collective-permute-start | bytes 1572872 | tf_op jit(solution)/shard_map/ppermute | solution.py:340
  66.7 2.4 %collective-permute-start.10 = (bf16[1024,256]{1,0:T(8,128)(2,1)S(1)}, bf16[1024,256]{1,0:T(8,128)(2,1)S(1)}, u32[]{:S(2)}, u32[]{:S(2)}) collective-permute-start(bf16[1024,256]{1,0:T(8,128)(2,1)S(1)} %collective-permute-done.2), channel_id=1, source_target_pairs={{0,8},{8,0},{1,9},{9,1},{2,10},{10,2},{3,11},{11,3},{4,12},{12,4},... | collective-permute-start | bytes 1572872 | tf_op jit(solution)/shard_map/ppermute | solution.py:340
  67.6 3.0 %collective-permute-start.12 = (bf16[1024,256]{1,0:T(8,128)(2,1)S(1)}, bf16[1024,256]{1,0:T(8,128)(2,1)S(1)}, u32[]{:S(2)}, u32[]{:S(2)}) collective-permute-start(bf16[1024,256]{1,0:T(8,128)(2,1)S(1)} %collective-permute-done.4), channel_id=1, source_target_pairs={{0,8},{8,0},{1,9},{9,1},{2,10},{10,2},{3,11},{11,3},{4,12},{12,4},... | collective-permute-start | bytes 1572872 | tf_op jit(solution)/shard_map/ppermute | solution.py:340
  67.7 3.3 %collective-permute-start.13 = (bf16[1024,256]{1,0:T(8,128)(2,1)}, bf16[1024,256]{1,0:T(8,128)(2,1)}, u32[]{:S(2)}, u32[]{:S(2)}) collective-permute-start(bf16[1024,256]{1,0:T(8,128)(2,1)} %collective-permute-done.7), channel_id=1, source_target_pairs={{0,8},{8,0},{1,9},{9,1},{2,10},{10,2},{3,11},{11,3},{4,12},{12,4},... | collective-permute-start | bytes 1572872 | tf_op jit(solution)/shard_map/ppermute | solution.py:340
  99.6 28.0 %collective-permute-start.19 = (bf16[128,1024]{1,0:T(8,128)(2,1)S(1)}, bf16[128,1024]{1,0:T(8,128)(2,1)S(1)}, u32[]{:S(2)}, u32[]{:S(2)}) collective-permute-start(bf16[128,1024]{1,0:T(8,128)(2,1)S(1)} %get-tuple-element.33), channel_id=1, source_target_pairs={{0,4},{1,5},{2,6},{3,7},{4,0},{5,1},{6,2},{7,3},{8,12},{9,13},{10,... | collective-permute-start | bytes 786440 | tf_op jit(solution)/shard_map/ppermute | solution.py:388
  102.4 25.2 %collective-permute-start.18 = (bf16[128,1024]{1,0:T(8,128)(2,1)S(1)}, bf16[128,1024]{1,0:T(8,128)(2,1)S(1)}, u32[]{:S(2)}, u32[]{:S(2)}) collective-permute-start(bf16[128,1024]{1,0:T(8,128)(2,1)S(1)} %get-tuple-element.34), channel_id=1, source_target_pairs={{0,2},{1,3},{2,0},{3,1},{4,6},{5,7},{6,4},{7,5},{8,10},{9,11},{10,... | collective-permute-start | bytes 786440 | tf_op jit(solution)/shard_map/ppermute | solution.py:388
  105.6 22.0 %collective-permute-start.17 = (bf16[128,1024]{1,0:T(8,128)(2,1)S(1)}, bf16[128,1024]{1,0:T(8,128)(2,1)S(1)}, u32[]{:S(2)}, u32[]{:S(2)}) collective-permute-start(bf16[128,1024]{1,0:T(8,128)(2,1)S(1)} %get-tuple-element.35), channel_id=1, source_target_pairs={{0,7},{1,4},{2,5},{3,6},{4,3},{5,0},{6,1},{7,2},{8,15},{9,12},{10,... | collective-permute-start | bytes 786440 | tf_op jit(solution)/shard_map/ppermute | solution.py:388
  106.0 21.6 %collective-permute-start.16 = (bf16[128,1024]{1,0:T(8,128)(2,1)S(1)}, bf16[128,1024]{1,0:T(8,128)(2,1)S(1)}, u32[]{:S(2)}, u32[]{:S(2)}) collective-permute-start(bf16[128,1024]{1,0:T(8,128)(2,1)S(1)} %get-tuple-element.36), channel_id=1, source_target_pairs={{0,5},{1,6},{2,7},{3,4},{4,1},{5,2},{6,3},{7,0},{8,13},{9,14},{10,... | collective-permute-start | bytes 786440 | tf_op jit(solution)/shard_map/ppermute | solution.py:388
  109.5 18.2 %collective-permute-start.15 = (bf16[128,1024]{1,0:T(8,128)(2,1)S(1)}, bf16[128,1024]{1,0:T(8,128)(2,1)S(1)}, u32[]{:S(2)}, u32[]{:S(2)}) collective-permute-start(bf16[128,1024]{1,0:T(8,128)(2,1)S(1)} %get-tuple-element.37), channel_id=1, source_target_pairs={{0,6},{1,7},{2,4},{3,5},{4,2},{5,3},{6,0},{7,1},{8,14},{9,15},{10,... | collective-permute-start | bytes 786440 | tf_op jit(solution)/shard_map/ppermute | solution.py:388
  127.7 7.2 %collective-permute-start.21 = (bf16[128,1024]{1,0:T(8,128)(2,1)S(1)}, bf16[128,1024]{1,0:T(8,128)(2,1)S(1)}, u32[]{:S(2)}, u32[]{:S(2)}) collective-permute-start(bf16[128,1024]{1,0:T(8,128)(2,1)S(1)} %get-tuple-element.38), channel_id=1, source_target_pairs={{0,3},{1,0},{2,1},{3,2},{4,7},{5,4},{6,5},{7,6},{8,11},{9,8},{10,9... | collective-permute-start | bytes 786440 | tf_op jit(solution)/shard_map/ppermute | solution.py:388
  131.3 6.4 %collective-permute-start.20 = (bf16[128,1024]{1,0:T(8,128)(2,1)S(1)}, bf16[128,1024]{1,0:T(8,128)(2,1)S(1)}, u32[]{:S(2)}, u32[]{:S(2)}) collective-permute-start(bf16[128,1024]{1,0:T(8,128)(2,1)S(1)} %get-tuple-element.39), channel_id=1, source_target_pairs={{0,1},{1,2},{2,3},{3,0},{4,5},{5,6},{6,7},{7,4},{8,9},{9,10},{10,1... | collective-permute-start | bytes 786440 | tf_op jit(solution)/shard_map/ppermute | solution.py:388
  (21 other events, 310.9 us)

commit v7 on v6

--- a/solution.py
+++ b/solution.py
@@ -321,14 +321,14 @@
 def assemble(lists, parts, late):
     rows, width = parts[0].shape
     count = len(parts) + 1
-    spaces = [pltpu.HBM] * FIRST_STEPS + [pltpu.VMEM] * (count - FIRST_STEPS)
-    parts = [
-        pltpu.with_memory_space_constraint(part, space)
-        for part, space in zip([*parts, late], spaces, strict=True)
+    parts = [*parts[:FIRST_STEPS]] + [
+        pltpu.with_memory_space_constraint(part, pltpu.VMEM) for part in [*parts[FIRST_STEPS:], late]
     ]
     return pl.pallas_call(
         assemble_kernel,
-        in_specs=[pl.BlockSpec(memory_space=pltpu.SMEM)] + [pl.BlockSpec(memory_space=pl.ANY)] * count,
+        in_specs=[pl.BlockSpec(memory_space=pltpu.SMEM)]
+        + [pl.BlockSpec(memory_space=pltpu.VMEM)] * FIRST_STEPS
+        + [pl.BlockSpec(memory_space=pl.ANY)] * (count - FIRST_STEPS),
         out_specs=pl.BlockSpec(memory_space=pl.ANY),
         out_shape=jax.ShapeDtypeStruct((rows, width * count), late.dtype),
         scratch_shapes=[pltpu.SemaphoreType.DMA((count,))],

time: 180 us -> 141 us (0.78)
  the two profiles are of different devices: /device:TPU:1 before, /device:TPU:24 now
where the time goes in v7:
time: 141 us; the launch traced here: 140 us
  Pallas kernels  54.1 us (38%)
  starting transfers between devices  41.8 us (30%)
  waiting for transfers between devices  39.9 us (28%)
  local copies, waits for them, and re-layouts  3.73 us (3%)
    pallas_call x2, Pallas kernels, attend(): pl.pallas_call(functools.partial(attend_kernel, blocks=blocks, steps=step...  42.1 us
    ppermute x15, waiting for transfers between devices, shift(): lax.ppermute(array, axis, [(i, (i + step) % size) for i in range(size)])  29 us
    all_to_all x2, starting transfers between devices, exchange(): lax.all_to_all(cut, head_axes, split_axis=0, concat_axis=0, tiled=True)  15.5 us
    ppermute x7, starting transfers between devices, send(): sent.append(lax.ppermute(part, head_axes, pairs))  15 us
    ppermute x15, starting transfers between devices, shift(): lax.ppermute(array, axis, [(i, (i + step) % size) for i in range(size)])  11.4 us
    ppermute x7, waiting for transfers between devices, send(): sent.append(lax.ppermute(part, head_axes, pairs))  10.9 us
    pallas_call x1, Pallas kernels, plan(): pl.pallas_call(functools.partial(plan_kernel, blocks=blocks, sizes=sizes,...  7.2 us
  transfers between devices with their start and end apart: 24, of which 10 were waited for; matrix products, arithmetic and copies ran while one was open for 2% of the time, Pallas kernels for 16%

profile of v7, /device:TPU:24, one launch (start us, length us, event | category | flops | bytes accessed | tf_op | source)
XLA Modules:
  0.0 139.8 jit_solution(15216929073324985225)
XLA Ops:
  0.0 2.1 %shard_map.55 = bf16[8,128,256]{2,1,0:T(8,128)(2,1)} custom-call(bf16[128,1024]{1,0:T(8,128)(2,1)} %keys.1, bf16[128,1024]{1,0:T(8,128)(2,1)} %values.1), custom_call_target="tpu_custom_call" | custom-call | tf_op jit(solution)/shard_map/pallas_call | solution.py:33
  2.1 8.3 %all-to-all-start = ((bf16[8,128,256]{2,1,0:T(8,128)(2,1)}), bf16[8,128,256]{2,1,0:T(8,128)(2,1)S(1)}, u32[]{:S(2)}, u32[]{:S(2)}) async-start(bf16[8,128,256]{2,1,0:T(8,128)(2,1)} %shard_map.55), calls=%async_computation | async-start | bytes 1048576 | tf_op jit(solution)/shard_map/all_to_all | solution.py:363
  10.4 1.6 %copy.9 = bf16[16,8,8,1024]{3,2,0,1:T(8,128)(2,1)} copy(bf16[16,8,8,1024]{3,2,1,0:T(8,128)(2,1)S(1)} %bitcast.33) | data formatting | bytes 4194304 | tf_op jit(solution)/shard_map/reshape | solution.py:367
  12.6 7.2 %shard_map.56.listed = s32[19,132]{1,0:T(8,128)} custom-call(s32[5]{0:T(128)} %stack.23.place_ref, s32[16,16,16]{2,1,0:T(8,128)} %codes_ref.1, s32[16,16]{1,0:T(8,128)} %counts_ref.1), custom_call_target="tpu_custom_call" | custom-call | bytes 20000000 | tf_op jit(solution)/shard_map/pallas_call | solution.py:94
  22.2 1.9 %collective-permute-start = (bf16[1024,256]{1,0:T(8,128)(2,1)S(1)}, bf16[1024,256]{1,0:T(8,128)(2,1)}, u32[]{:S(2)}, u32[]{:S(2)}) collective-permute-start(bf16[1024,256]{1,0:T(8,128)(2,1)S(1)} %bitcast.36), channel_id=1, source_target_pairs={{0,96},{32,0},{64,32},{96,64},{1,97},{33,1},{65,33},{97,65},{2,98}... | collective-permute-start | bytes 1572872 | tf_op jit(solution)/shard_map/ppermute | solution.py:340
  24.1 7.2 %all-to-all-start.1 = ((bf16[8,128,1024]{2,1,0:T(8,128)(2,1)}), bf16[8,128,1024]{2,1,0:T(8,128)(2,1)S(1)}, u32[]{:S(2)}, u32[]{:S(2)}) async-start(bf16[8,128,1024]{2,1,0:T(8,128)(2,1)} %bitcast.32), calls=%async_computation.1 | async-start | bytes 4194304 | tf_op jit(solution)/shard_map/all_to_all | solution.py:363
  31.3 3.5 %collective-permute-done.3 = bf16[1024,256]{1,0:T(8,128)(2,1)S(1)} collective-permute-done((bf16[1024,256]{1,0:T(8,128)(2,1)S(1)}, bf16[1024,256]{1,0:T(8,128)(2,1)S(1)}, u32[]{:S(2)}, u32[]{:S(2)}) %collective-permute-start.3) | collective-permute-done | bytes 524320 | tf_op jit(solution)/shard_map/ppermute | solution.py:340
  34.8 2.5 %collective-permute-start.4 = (bf16[1024,256]{1,0:T(8,128)(2,1)S(1)}, bf16[1024,256]{1,0:T(8,128)(2,1)S(1)}, u32[]{:S(2)}, u32[]{:S(2)}) collective-permute-start(bf16[1024,256]{1,0:T(8,128)(2,1)S(1)} %collective-permute-done.3), channel_id=1, source_target_pairs={{0,96},{32,0},{64,32},{96,64},{1,97},{33,1},{65,33},{97,65},{2,98}... | collective-permute-start | bytes 1572872 | tf_op jit(solution)/shard_map/ppermute | solution.py:340
  37.9 8.2 %collective-permute-done.4 = bf16[1024,256]{1,0:T(8,128)(2,1)S(1)} collective-permute-done((bf16[1024,256]{1,0:T(8,128)(2,1)S(1)}, bf16[1024,256]{1,0:T(8,128)(2,1)S(1)}, u32[]{:S(2)}, u32[]{:S(2)}) %collective-permute-start.4) | collective-permute-done | bytes 524320 | tf_op jit(solution)/shard_map/ppermute | solution.py:340
  46.1 1.7 %collective-permute-start.2 = (bf16[1024,256]{1,0:T(8,128)(2,1)}, bf16[1024,256]{1,0:T(8,128)(2,1)S(1)}, u32[]{:S(2)}, u32[]{:S(2)}) collective-permute-start(bf16[1024,256]{1,0:T(8,128)(2,1)} %collective-permute-done.1), channel_id=1, source_target_pairs={{0,32},{32,64},{64,96},{96,0},{1,33},{33,65},{65,97},{97,1},{2,34}... | collective-permute-start | bytes 1572872 | tf_op jit(solution)/shard_map/ppermute | solution.py:340
  47.9 1.7 %collective-permute-start.7 = (bf16[1024,256]{1,0:T(8,128)(2,1)S(1)}, bf16[1024,256]{1,0:T(8,128)(2,1)}, u32[]{:S(2)}, u32[]{:S(2)}) collective-permute-start(bf16[1024,256]{1,0:T(8,128)(2,1)S(1)} %collective-permute-done.4), channel_id=1, source_target_pairs={{0,96},{32,0},{64,32},{96,64},{1,97},{33,1},{65,33},{97,65},{2,98}... | collective-permute-start | bytes 1572872 | tf_op jit(solution)/shard_map/ppermute | solution.py:340
  49.6 4.3 %collective-permute-done.8 = bf16[1024,256]{1,0:T(8,128)(2,1)S(1)} collective-permute-done((bf16[1024,256]{1,0:T(8,128)(2,1)S(1)}, bf16[1024,256]{1,0:T(8,128)(2,1)S(1)}, u32[]{:S(2)}, u32[]{:S(2)}) %collective-permute-start.8) | collective-permute-done | bytes 524320 | tf_op jit(solution)/shard_map/ppermute | solution.py:340
  53.9 10.8 %collective-permute-done.2 = bf16[1024,256]{1,0:T(8,128)(2,1)S(1)} collective-permute-done((bf16[1024,256]{1,0:T(8,128)(2,1)}, bf16[1024,256]{1,0:T(8,128)(2,1)S(1)}, u32[]{:S(2)}, u32[]{:S(2)}) %collective-permute-start.2) | collective-permute-done | bytes 524320 | tf_op jit(solution)/shard_map/ppermute | solution.py:340
  68.8 26.6 %shard_map.57 = (bf16[640,1024]{1,0:T(8,128)(2,1)S(1)}, bf16[129,128,256]{2,1,0:T(8,128)(2,1)S(1)}) custom-call(s32[19,132]{1,0:T(8,128)S(1)} %copy-done.2, bf16[1024,1024]{1,0:T(8,128)(2,1)S(1)} %bitcast.30, bf16[8,128,256]{2,1,0:T(8,128)(2,1)} %copy-done.4, bf16[8,128,256]{2,1,0:T(8,128)(2,1)} %bitcast.9.refs_1_, bf16[8,128,256]{2,1,0:T(8,128)(2,1)} %bitcast.44, ...), custom_call_target="tpu_custom_call" | custom-call | flops 22145925120 | bytes 6000000 | tf_op jit(solution)/shard_map/pallas_call | solution.py:285
  95.6 1.8 %collective-permute-start.19 = (bf16[128,1024]{1,0:T(8,128)(2,1)S(1)}, bf16[128,1024]{1,0:T(8,128)(2,1)S(1)}, u32[]{:S(2)}, u32[]{:S(2)}) collective-permute-start(bf16[128,1024]{1,0:T(8,128)(2,1)S(1)} %get-tuple-element.33), channel_id=1, source_target_pairs={{0,4},{1,5},{2,6},{3,7},{4,0},{5,1},{6,2},{7,3},{8,12},{9,13},{10,... | collective-permute-start | bytes 786440 | tf_op jit(solution)/shard_map/ppermute | solution.py:388
  97.3 2.0 %collective-permute-start.18 = (bf16[128,1024]{1,0:T(8,128)(2,1)S(1)}, bf16[128,1024]{1,0:T(8,128)(2,1)S(1)}, u32[]{:S(2)}, u32[]{:S(2)}) collective-permute-start(bf16[128,1024]{1,0:T(8,128)(2,1)S(1)} %get-tuple-element.34), channel_id=1, source_target_pairs={{0,2},{1,3},{2,0},{3,1},{4,6},{5,7},{6,4},{7,5},{8,10},{9,11},{10,... | collective-permute-start | bytes 786440 | tf_op jit(solution)/shard_map/ppermute | solution.py:388
  99.3 5.1 %collective-permute-start.17 = (bf16[128,1024]{1,0:T(8,128)(2,1)S(1)}, bf16[128,1024]{1,0:T(8,128)(2,1)S(1)}, u32[]{:S(2)}, u32[]{:S(2)}) collective-permute-start(bf16[128,1024]{1,0:T(8,128)(2,1)S(1)} %get-tuple-element.35), channel_id=1, source_target_pairs={{0,7},{1,4},{2,5},{3,6},{4,3},{5,0},{6,1},{7,2},{8,15},{9,12},{10,... | collective-permute-start | bytes 786440 | tf_op jit(solution)/shard_map/ppermute | solution.py:388
  104.4 2.2 %collective-permute-start.15 = (bf16[128,1024]{1,0:T(8,128)(2,1)S(1)}, bf16[128,1024]{1,0:T(8,128)(2,1)S(1)}, u32[]{:S(2)}, u32[]{:S(2)}) collective-permute-start(bf16[128,1024]{1,0:T(8,128)(2,1)S(1)} %get-tuple-element.37), channel_id=1, source_target_pairs={{0,6},{1,7},{2,4},{3,5},{4,2},{5,3},{6,0},{7,1},{8,14},{9,15},{10,... | collective-permute-start | bytes 786440 | tf_op jit(solution)/shard_map/ppermute | solution.py:388
  106.6 15.6 %shard_map.58.refs_7_ = bf16[384,1024]{1,0:T(8,128)(2,1)S(1)} custom-call(s32[19,132]{1,0:T(8,128)S(1)} %copy-done.2, bf16[1024,1024]{1,0:T(8,128)(2,1)S(1)} %bitcast.31, bf16[129,128,256]{2,1,0:T(8,128)(2,1)S(1)} %get-tuple-element.25.refs_0_), custom_call_target="tpu_custom_call" | custom-call | flops 13287555072 | bytes 6000000 | tf_op jit(solution)/shard_map/pallas_call | solution.py:285
  122.3 2.0 %collective-permute-done.15.refs_0_ = bf16[128,1024]{1,0:T(8,128)(2,1)S(1)} collective-permute-done((bf16[128,1024]{1,0:T(8,128)(2,1)S(1)}, bf16[128,1024]{1,0:T(8,128)(2,1)S(1)}, u32[]{:S(2)}, u32[]{:S(2)}) %collective-permute-start.15) | collective-permute-done | bytes 262176 | tf_op jit(solution)/shard_map/ppermute | solution.py:388
  124.3 3.9 %collective-permute-start.21 = (bf16[128,1024]{1,0:T(8,128)(2,1)S(1)}, bf16[128,1024]{1,0:T(8,128)(2,1)S(1)}, u32[]{:S(2)}, u32[]{:S(2)}) collective-permute-start(bf16[128,1024]{1,0:T(8,128)(2,1)S(1)} %get-tuple-element.38), channel_id=1, source_target_pairs={{0,3},{1,0},{2,1},{3,2},{4,7},{5,4},{6,5},{7,6},{8,11},{9,8},{10,9... | collective-permute-start | bytes 786440 | tf_op jit(solution)/shard_map/ppermute | solution.py:388
  128.2 5.5 %collective-permute-done.21.refs_6_ = bf16[128,1024]{1,0:T(8,128)(2,1)S(1)} collective-permute-done((bf16[128,1024]{1,0:T(8,128)(2,1)S(1)}, bf16[128,1024]{1,0:T(8,128)(2,1)S(1)}, u32[]{:S(2)}, u32[]{:S(2)}) %collective-permute-start.21) | collective-permute-done | bytes 262176 | tf_op jit(solution)/shard_map/ppermute | solution.py:388
  133.7 3.4 %collective-permute-done.20.refs_5_ = bf16[128,1024]{1,0:T(8,128)(2,1)S(1)} collective-permute-done((bf16[128,1024]{1,0:T(8,128)(2,1)S(1)}, bf16[128,1024]{1,0:T(8,128)(2,1)S(1)}, u32[]{:S(2)}, u32[]{:S(2)}) %collective-permute-start.20) | collective-permute-done | bytes 262176 | tf_op jit(solution)/shard_map/ppermute | solution.py:388
  137.2 2.7 %shard_map.59 = bf16[128,8192]{1,0:T(8,128)(2,1)} custom-call(s32[19,132]{1,0:T(8,128)} %shard_map.56.listed, bf16[128,1024]{1,0:T(8,128)(2,1)} %copy-done.9, bf16[128,1024]{1,0:T(8,128)(2,1)} %copy-done.8, bf16[128,1024]{1,0:T(8,128)(2,1)} %copy-done.7, bf16[128,1024]{1,0:T(8,128)(2,1)} %copy-done.6, bf16[128,1024]{1,0:T(8,128)(2,1)} %copy-done.5, ...), custom_call_target="tpu_custom_call" | custom-call | tf_op jit(solution)/shard_map/pallas_call | solution.py:327
  (75 shorter events, 8.0 us)
Async XLA Ops:
  2.1 17.7 %all-to-all-start = ((bf16[8,128,256]{2,1,0:T(8,128)(2,1)}), bf16[8,128,256]{2,1,0:T(8,128)(2,1)S(1)}, u32[]{:S(2)}, u32[]{:S(2)}) async-start(bf16[8,128,256]{2,1,0:T(8,128)(2,1)} %shard_map.55), calls=%async_computation | async-start | bytes 1048576 | tf_op jit(solution)/shard_map/all_to_all | solution.py:363
  19.9 14.9 %collective-permute-start.3 = (bf16[1024,256]{1,0:T(8,128)(2,1)S(1)}, bf16[1024,256]{1,0:T(8,128)(2,1)S(1)}, u32[]{:S(2)}, u32[]{:S(2)}) collective-permute-start(bf16[1024,256]{1,0:T(8,128)(2,1)S(1)} %bitcast.34), channel_id=1, source_target_pairs={{0,16},{16,0},{1,17},{17,1},{2,18},{18,2},{3,19},{19,3},{4,20},{20... | collective-permute-start | bytes 1572872 | tf_op jit(solution)/shard_map/ppermute | solution.py:340
  20.8 16.5 %collective-permute-start.1 = (bf16[1024,256]{1,0:T(8,128)(2,1)S(1)}, bf16[1024,256]{1,0:T(8,128)(2,1)}, u32[]{:S(2)}, u32[]{:S(2)}) collective-permute-start(bf16[1024,256]{1,0:T(8,128)(2,1)S(1)} %bitcast.35), channel_id=1, source_target_pairs={{0,32},{32,64},{64,96},{96,0},{1,33},{33,65},{65,97},{97,1},{2,34}... | collective-permute-start | bytes 1572872 | tf_op jit(solution)/shard_map/ppermute | solution.py:340
  22.2 15.1 %collective-permute-start = (bf16[1024,256]{1,0:T(8,128)(2,1)S(1)}, bf16[1024,256]{1,0:T(8,128)(2,1)}, u32[]{:S(2)}, u32[]{:S(2)}) collective-permute-start(bf16[1024,256]{1,0:T(8,128)(2,1)S(1)} %bitcast.36), channel_id=1, source_target_pairs={{0,96},{32,0},{64,32},{96,64},{1,97},{33,1},{65,33},{97,65},{2,98}... | collective-permute-start | bytes 1572872 | tf_op jit(solution)/shard_map/ppermute | solution.py:340
  24.1 44.0 %all-to-all-start.1 = ((bf16[8,128,1024]{2,1,0:T(8,128)(2,1)}), bf16[8,128,1024]{2,1,0:T(8,128)(2,1)S(1)}, u32[]{:S(2)}, u32[]{:S(2)}) async-start(bf16[8,128,1024]{2,1,0:T(8,128)(2,1)} %bitcast.32), calls=%async_computation.1 | async-start | bytes 4194304 | tf_op jit(solution)/shard_map/all_to_all | solution.py:363
  34.8 11.3 %collective-permute-start.4 = (bf16[1024,256]{1,0:T(8,128)(2,1)S(1)}, bf16[1024,256]{1,0:T(8,128)(2,1)S(1)}, u32[]{:S(2)}, u32[]{:S(2)}) collective-permute-start(bf16[1024,256]{1,0:T(8,128)(2,1)S(1)} %collective-permute-done.3), channel_id=1, source_target_pairs={{0,96},{32,0},{64,32},{96,64},{1,97},{33,1},{65,33},{97,65},{2,98}... | collective-permute-start | bytes 1572872 | tf_op jit(solution)/shard_map/ppermute | solution.py:340
  37.3 10.5 %collective-permute-start.6 = (bf16[1024,256]{1,0:T(8,128)(2,1)}, bf16[1024,256]{1,0:T(8,128)(2,1)S(1)}, u32[]{:S(2)}, u32[]{:S(2)}) collective-permute-start(bf16[1024,256]{1,0:T(8,128)(2,1)} %collective-permute-done.1), channel_id=1, source_target_pairs={{0,8},{8,0},{1,9},{9,1},{2,10},{10,2},{3,11},{11,3},{4,12},{12,4},... | collective-permute-start | bytes 1572872 | tf_op jit(solution)/shard_map/ppermute | solution.py:340
  37.3 10.5 %collective-permute-start.5 = (bf16[1024,256]{1,0:T(8,128)(2,1)}, bf16[1024,256]{1,0:T(8,128)(2,1)S(1)}, u32[]{:S(2)}, u32[]{:S(2)}) collective-permute-start(bf16[1024,256]{1,0:T(8,128)(2,1)} %collective-permute-done), channel_id=1, source_target_pairs={{0,8},{8,0},{1,9},{9,1},{2,10},{10,2},{3,11},{11,3},{4,12},{12,4},... | collective-permute-start | bytes 1572872 | tf_op jit(solution)/shard_map/ppermute | solution.py:340
  37.8 26.8 %collective-permute-start.9 = (bf16[1024,256]{1,0:T(8,128)(2,1)S(1)}, bf16[1024,256]{1,0:T(8,128)(2,1)S(1)}, u32[]{:S(2)}, u32[]{:S(2)}) collective-permute-start(bf16[1024,256]{1,0:T(8,128)(2,1)S(1)} %bitcast.37), channel_id=1, source_target_pairs={{0,8},{8,0},{1,9},{9,1},{2,10},{10,2},{3,11},{11,3},{4,12},{12,4},... | collective-permute-start | bytes 1572872 | tf_op jit(solution)/shard_map/ppermute | solution.py:340
  37.9 15.9 %collective-permute-start.8 = (bf16[1024,256]{1,0:T(8,128)(2,1)S(1)}, bf16[1024,256]{1,0:T(8,128)(2,1)S(1)}, u32[]{:S(2)}, u32[]{:S(2)}) collective-permute-start(bf16[1024,256]{1,0:T(8,128)(2,1)S(1)} %collective-permute-done.3), channel_id=1, source_target_pairs={{0,32},{32,64},{64,96},{96,0},{1,33},{33,65},{65,97},{97,1},{2,34}... | collective-permute-start | bytes 1572872 | tf_op jit(solution)/shard_map/ppermute | solution.py:340
  46.1 18.5 %collective-permute-start.2 = (bf16[1024,256]{1,0:T(8,128)(2,1)}, bf16[1024,256]{1,0:T(8,128)(2,1)S(1)}, u32[]{:S(2)}, u32[]{:S(2)}) collective-permute-start(bf16[1024,256]{1,0:T(8,128)(2,1)} %collective-permute-done.1), channel_id=1, source_target_pairs={{0,32},{32,64},{64,96},{96,0},{1,33},{33,65},{65,97},{97,1},{2,34}... | collective-permute-start | bytes 1572872 | tf_op jit(solution)/shard_map/ppermute | solution.py:340
  47.9 17.3 %collective-permute-start.7 = (bf16[1024,256]{1,0:T(8,128)(2,1)S(1)}, bf16[1024,256]{1,0:T(8,128)(2,1)}, u32[]{:S(2)}, u32[]{:S(2)}) collective-permute-start(bf16[1024,256]{1,0:T(8,128)(2,1)S(1)} %collective-permute-done.4), channel_id=1, source_target_pairs={{0,96},{32,0},{64,32},{96,64},{1,97},{33,1},{65,33},{97,65},{2,98}... | collective-permute-start | bytes 1572872 | tf_op jit(solution)/shard_map/ppermute | solution.py:340
  49.6 15.7 %collective-permute-start.11 = (bf16[1024,256]{1,0:T(8,128)(2,1)S(1)}, bf16[1024,256]{1,0:T(8,128)(2,1)S(1)}, u32[]{:S(2)}, u32[]{:S(2)}) collective-permute-start(bf16[1024,256]{1,0:T(8,128)(2,1)S(1)} %collective-permute-done.3), channel_id=1, source_target_pairs={{0,8},{8,0},{1,9},{9,1},{2,10},{10,2},{3,11},{11,3},{4,12},{12,4},... | collective-permute-start | bytes 1572872 | tf_op jit(solution)/shard_map/ppermute | solution.py:340
  53.9 11.4 %collective-permute-start.14 = (bf16[1024,256]{1,0:T(8,128)(2,1)S(1)}, bf16[1024,256]{1,0:T(8,128)(2,1)S(1)}, u32[]{:S(2)}, u32[]{:S(2)}) collective-permute-start(bf16[1024,256]{1,0:T(8,128)(2,1)S(1)} %collective-permute-done.8), channel_id=1, source_target_pairs={{0,8},{8,0},{1,9},{9,1},{2,10},{10,2},{3,11},{11,3},{4,12},{12,4},... | collective-permute-start | bytes 1572872 | tf_op jit(solution)/shard_map/ppermute | solution.py:340
  64.6 1.9 %collective-permute-start.10 = (bf16[1024,256]{1,0:T(8,128)(2,1)S(1)}, bf16[1024,256]{1,0:T(8,128)(2,1)S(1)}, u32[]{:S(2)}, u32[]{:S(2)}) collective-permute-start(bf16[1024,256]{1,0:T(8,128)(2,1)S(1)} %collective-permute-done.2), channel_id=1, source_target_pairs={{0,8},{8,0},{1,9},{9,1},{2,10},{10,2},{3,11},{11,3},{4,12},{12,4},... | collective-permute-start | bytes 1572872 | tf_op jit(solution)/shard_map/ppermute | solution.py:340
  64.6 3.4 %collective-permute-start.12 = (bf16[1024,256]{1,0:T(8,128)(2,1)S(1)}, bf16[1024,256]{1,0:T(8,128)(2,1)S(1)}, u32[]{:S(2)}, u32[]{:S(2)}) collective-permute-start(bf16[1024,256]{1,0:T(8,128)(2,1)S(1)} %collective-permute-done.4), channel_id=1, source_target_pairs={{0,8},{8,0},{1,9},{9,1},{2,10},{10,2},{3,11},{11,3},{4,12},{12,4},... | collective-permute-start | bytes 1572872 | tf_op jit(solution)/shard_map/ppermute | solution.py:340
  65.1 3.2 %collective-permute-start.13 = (bf16[1024,256]{1,0:T(8,128)(2,1)}, bf16[1024,256]{1,0:T(8,128)(2,1)}, u32[]{:S(2)}, u32[]{:S(2)}) collective-permute-start(bf16[1024,256]{1,0:T(8,128)(2,1)} %collective-permute-done.7), channel_id=1, source_target_pairs={{0,8},{8,0},{1,9},{9,1},{2,10},{10,2},{3,11},{11,3},{4,12},{12,4},... | collective-permute-start | bytes 1572872 | tf_op jit(solution)/shard_map/ppermute | solution.py:340
  95.6 26.6 %collective-permute-start.19 = (bf16[128,1024]{1,0:T(8,128)(2,1)S(1)}, bf16[128,1024]{1,0:T(8,128)(2,1)S(1)}, u32[]{:S(2)}, u32[]{:S(2)}) collective-permute-start(bf16[128,1024]{1,0:T(8,128)(2,1)S(1)} %get-tuple-element.33), channel_id=1, source_target_pairs={{0,4},{1,5},{2,6},{3,7},{4,0},{5,1},{6,2},{7,3},{8,12},{9,13},{10,... | collective-permute-start | bytes 786440 | tf_op jit(solution)/shard_map/ppermute | solution.py:388
  97.3 24.9 %collective-permute-start.18 = (bf16[128,1024]{1,0:T(8,128)(2,1)S(1)}, bf16[128,1024]{1,0:T(8,128)(2,1)S(1)}, u32[]{:S(2)}, u32[]{:S(2)}) collective-permute-start(bf16[128,1024]{1,0:T(8,128)(2,1)S(1)} %get-tuple-element.34), channel_id=1, source_target_pairs={{0,2},{1,3},{2,0},{3,1},{4,6},{5,7},{6,4},{7,5},{8,10},{9,11},{10,... | collective-permute-start | bytes 786440 | tf_op jit(solution)/shard_map/ppermute | solution.py:388
  99.3 22.9 %collective-permute-start.17 = (bf16[128,1024]{1,0:T(8,128)(2,1)S(1)}, bf16[128,1024]{1,0:T(8,128)(2,1)S(1)}, u32[]{:S(2)}, u32[]{:S(2)}) collective-permute-start(bf16[128,1024]{1,0:T(8,128)(2,1)S(1)} %get-tuple-element.35), channel_id=1, source_target_pairs={{0,7},{1,4},{2,5},{3,6},{4,3},{5,0},{6,1},{7,2},{8,15},{9,12},{10,... | collective-permute-start | bytes 786440 | tf_op jit(solution)/shard_map/ppermute | solution.py:388
  104.4 17.8 %collective-permute-start.16 = (bf16[128,1024]{1,0:T(8,128)(2,1)S(1)}, bf16[128,1024]{1,0:T(8,128)(2,1)S(1)}, u32[]{:S(2)}, u32[]{:S(2)}) collective-permute-start(bf16[128,1024]{1,0:T(8,128)(2,1)S(1)} %get-tuple-element.36), channel_id=1, source_target_pairs={{0,5},{1,6},{2,7},{3,4},{4,1},{5,2},{6,3},{7,0},{8,13},{9,14},{10,... | collective-permute-start | bytes 786440 | tf_op jit(solution)/shard_map/ppermute | solution.py:388
  104.4 19.8 %collective-permute-start.15 = (bf16[128,1024]{1,0:T(8,128)(2,1)S(1)}, bf16[128,1024]{1,0:T(8,128)(2,1)S(1)}, u32[]{:S(2)}, u32[]{:S(2)}) collective-permute-start(bf16[128,1024]{1,0:T(8,128)(2,1)S(1)} %get-tuple-element.37), channel_id=1, source_target_pairs={{0,6},{1,7},{2,4},{3,5},{4,2},{5,3},{6,0},{7,1},{8,14},{9,15},{10,... | collective-permute-start | bytes 786440 | tf_op jit(solution)/shard_map/ppermute | solution.py:388
  124.3 9.5 %collective-permute-start.21 = (bf16[128,1024]{1,0:T(8,128)(2,1)S(1)}, bf16[128,1024]{1,0:T(8,128)(2,1)S(1)}, u32[]{:S(2)}, u32[]{:S(2)}) collective-permute-start(bf16[128,1024]{1,0:T(8,128)(2,1)S(1)} %get-tuple-element.38), channel_id=1, source_target_pairs={{0,3},{1,0},{2,1},{3,2},{4,7},{5,4},{6,5},{7,6},{8,11},{9,8},{10,9... | collective-permute-start | bytes 786440 | tf_op jit(solution)/shard_map/ppermute | solution.py:388
  128.2 8.9 %collective-permute-start.20 = (bf16[128,1024]{1,0:T(8,128)(2,1)S(1)}, bf16[128,1024]{1,0:T(8,128)(2,1)S(1)}, u32[]{:S(2)}, u32[]{:S(2)}) collective-permute-start(bf16[128,1024]{1,0:T(8,128)(2,1)S(1)} %get-tuple-element.39), channel_id=1, source_target_pairs={{0,1},{1,2},{2,3},{3,0},{4,5},{5,6},{6,7},{7,4},{8,9},{9,10},{10,1... | collective-permute-start | bytes 786440 | tf_op jit(solution)/shard_map/ppermute | solution.py:388
  (21 other events, 300.9 us)
